TPU v7x, 128 devices: a whole 4x4x4 slice. The times are simulated.
128 devices in a mesh: row: 16 (over y, x), col: 8 (over z, core).
Axes of the slice: x: 4, y: 4, z: 4, core: 2. Of those that a mesh axis runs over, the one named last changes fastest.
Arguments:
- tokens: bfloat16 [8192, 3072], P('row', 'col'), may hold values from -6 to 6
- weight: bfloat16 [3072, 12288], P('row', 'col'), may hold values from -0.109375 to 0.109375
- cotangent: bfloat16 [8192, 12288], P('row', 'col'), may hold values from -6 to 6
Outputs:
- activated: bfloat16 [8192, 12288], P('row', 'col')
- input_grad: bfloat16 [8192, 3072], P('row', 'col')
- weight_grad: float32 [3072, 12288], P('row', 'col')
All inputs are finite; a program needn't handle non-finite values.
Results may differ from a plain program's by a relative error of at most 0.0049.
Values may be sent and summed in bfloat16 or wider, within the bound.
No kernel may reach another device: no remote copies, remote signals or barrier semaphores. Data moves between devices by JAX's collectives and lax.ppermute only.
A program may use at most 128 MiB of HBM per device.

v0:
```python
import jax
import jax.numpy as jnp
from jax import lax
from jax.sharding import PartitionSpec as P


def gelu_tanh(value):
    return jax.nn.gelu(value, approximate=True)


def shards(tokens, weight, cotangent):
    features = lax.all_gather(tokens, "col", axis=1, tiled=True)
    panel = lax.all_gather(weight, "row", axis=0, tiled=True)
    pre = jnp.dot(features, panel, preferred_element_type=jnp.float32)
    outputs, pullback = jax.vjp(gelu_tanh, pre)
    activated = outputs.astype(jnp.bfloat16)
    grad_pre = pullback(cotangent.astype(jnp.float32))[0].astype(jnp.bfloat16)
    partial_input = lax.dot_general(
        grad_pre, panel, (((1,), (1,)), ((), ())), preferred_element_type=jnp.float32
    )
    input_grad = lax.psum_scatter(partial_input, "col", scatter_dimension=1, tiled=True).astype(
        jnp.bfloat16
    )
    weight_grad = lax.psum_scatter(
        lax.dot_general(
            features, grad_pre, (((0,), (0,)), ((), ())), preferred_element_type=jnp.float32
        ),
        "row",
        scatter_dimension=0,
        tiled=True,
    )
    return (activated, input_grad, weight_grad)


def solution(mesh):
    in_specs = (P("row", "col"), P("row", "col"), P("row", "col"))
    out_specs = (P("row", "col"), P("row", "col"), P("row", "col"))
    return jax.shard_map(shards, mesh=mesh, in_specs=in_specs, out_specs=out_specs, check_vma=False)
```

profile of v0, /device:TPU:6, one launch (start us, length us, event | category | flops | bytes accessed | tf_op | source)
XLA Modules:
  0.0 312.4 jit_solution(2703451830053153495)
XLA Ops:
  7.2 0.0 all-gather.3.cloned.1.call-start
  7.2 0.7 all-gather.3.cloned.1.call-update
  7.9 0.0 all-gather.5.cloned.1.call-start
  7.9 0.7 all-gather.5.cloned.1.call-update
  8.6 0.0 copy-start.2
  8.7 0.0 reduce-scatter.5.cloned.1.call-start
  8.7 31.3 %all-gather.3.cloned.1.call-done = bf16[512,3072]{1,0:T(8,128)(2,1)} async-done(((bf16[512,384]{1,0:T(8,128)(2,1)}), bf16[512,3072]{1,0:T(8,128)(2,1)}) %all-gather.3.cloned.1.call-update) | async-done | bytes 3145744 | tf_op jit(solution)/shard_map/all_gather | solution.py:12
  40.0 77.6 %all-gather.5.cloned.1.call-done = bf16[3072,1536]{1,0:T(8,128)(2,1)} async-done(((bf16[192,1536]{1,0:T(8,128)(2,1)}), bf16[3072,1536]{1,0:T(8,128)(2,1)}) %all-gather.5.cloned.1.call-update) | async-done | bytes 9437200 | tf_op jit(solution)/shard_map/all_gather | solution.py:13
  117.6 0.0 copy-start
  117.6 11.0 %multiply_convert_fusion = (bf16[512,1536]{1,0:T(8,128)(2,1)}, f32[512,1536]{1,0:T(8,128)S(1)}) fusion(bf16[512,3072]{1,0:T(8,128)(2,1)} %all-gather.3.cloned.1.call-done, bf16[3072,1536]{1,0:T(8,128)(2,1)} %all-gather.5.cloned.1.call-done), kind=kOutput, calls=%fused_computation.15 | convolution fusion | flops 4838916096 | bytes 17301504 | tf_op jit(solution)/shard_map/dot_general | solution.py:14
  128.6 0.0 copy-start.3
  128.6 1.6 copy-done.3
  130.3 0.0 copy-done.2
  130.3 0.0 copy-done
  130.3 8.5 %fusion.11 = f32[512,3072]{1,0:T(8,128)} fusion(bf16[3072,1536]{1,0:T(8,128)(2,1)S(1)} %copy-done, bf16[512,1536]{1,0:T(8,128)(2,1)S(1)} %copy-done.2, f32[512,1536]{1,0:T(8,128)S(1)} %get-tuple-element.10), kind=kOutput, calls=%fused_computation.16 | convolution fusion | flops 4848353280 | bytes 20447232 | tf_op jit(solution)/shard_map/dot_general | solution.py:18
  138.8 0.0 copy-start.1
  138.8 0.0 reduce-scatter.5.cloned.1.call-update
  138.8 0.0 reduce-scatter.7.cloned.1.call-start
  138.8 1.8 copy-done.1
  140.7 14.7 %convolution_bitcast_fusion = f32[3072,1536]{0,1:T(8,128)} fusion(bf16[512,3072]{1,0:T(8,128)(2,1)S(1)} %copy-done.1, bf16[512,1536]{1,0:T(8,128)(2,1)} %param.5, f32[512,1536]{1,0:T(8,128)} %copy-done.3), kind=kOutput, calls=%fused_computation | convolution fusion | flops 4848353280 | bytes 26738688 | tf_op jit(solution)/shard_map/dot_general | solution.py:25
  155.4 18.8 %copy.8 = f32[3072,1536]{1,0:T(8,128)} copy(f32[3072,1536]{0,1:T(8,128)} %convolution_bitcast_fusion) | data formatting | bytes 37748736
  174.2 0.0 reduce-scatter.7.cloned.1.call-update
  174.2 7.1 %reduce-scatter.5.cloned.1.call-done = f32[512,384]{1,0:T(8,128)} async-done(((f32[512,3072]{1,0:T(8,128)}), f32[512,384]{1,0:T(8,128)}) %reduce-scatter.5.cloned.1.call-update) | async-done | bytes 786448 | tf_op jit(solution)/shard_map/reduce_scatter | solution.py:21
  181.4 1.9 convert_element_type.15
  183.3 122.5 %reduce-scatter.7.cloned.1.call-done = f32[192,1536]{1,0:T(8,128)} async-done(((f32[3072,1536]{1,0:T(8,128)}), f32[192,1536]{1,0:T(8,128)}) %reduce-scatter.7.cloned.1.call-update) | async-done | bytes 1179664
Async XLA Ops:
  7.2 32.8 %all-gather.3.cloned.1.call-start = ((), (), s32[]{:S(2)}) async-start(), calls=%async_computation.2 | async-start | bytes 3538944 | tf_op jit(solution)/shard_map/all_gather | solution.py:12
  7.9 109.7 %all-gather.5.cloned.1.call-start = ((), (), s32[]{:S(2)}) async-start(), calls=%async_computation.3 | async-start | bytes 10027008 | tf_op jit(solution)/shard_map/all_gather | solution.py:13
  8.6 121.6 %copy-start.2 = (bf16[512,1536]{1,0:T(8,128)(2,1)S(1)}, bf16[512,1536]{1,0:T(8,128)(2,1)}, u32[]{:S(2)}) copy-start(bf16[512,1536]{1,0:T(8,128)(2,1)} %param.5) | copy-start | bytes 4718596
  8.7 172.7 %reduce-scatter.5.cloned.1.call-start = ((), (), s32[]{:S(2)}) async-start(), calls=%async_computation.4 | async-start | bytes 7077888 | tf_op jit(solution)/shard_map/reduce_scatter | solution.py:21
  117.6 12.7 %copy-start = (bf16[3072,1536]{1,0:T(8,128)(2,1)S(1)}, bf16[3072,1536]{1,0:T(8,128)(2,1)}, u32[]{:S(2)}) copy-start(bf16[3072,1536]{1,0:T(8,128)(2,1)} %all-gather.5.cloned.1.call-done) | copy-start | bytes 28311556
  128.6 1.6 copy-start.3
  138.8 1.9 copy-start.1
  138.8 167.0 %reduce-scatter.7.cloned.1.call-start = ((), (), s32[]{:S(2)}) async-start(), calls=%async_computation.5 | async-start | bytes 20054016
Sparse Core Ops, SparseCore 0:
  9.7 30.2 all-gather.2
  42.1 75.4 all-gather.4
  138.9 42.4 reduce-scatter.4
  185.2 120.5 reduce-scatter.6
where the time goes:
time: 314 us; the launch traced here: 312 us
  waiting for transfers between devices  240 us (76%)
  matrix products  34.2 us (11%)
  local copies, waits for them, and re-layouts  22.3 us (7%)
  between operations  13.8 us (4%)
    unnamed x5, waiting for transfers between devices  124 us
    all_gather x1, waiting for transfers between devices, shards(): panel = lax.all_gather(weight, 'row', axis=0, tiled=True)  77.6 us
    all_gather x1, waiting for transfers between devices, shards(): features = lax.all_gather(tokens, 'col', axis=1, tiled=True)  31.3 us
    unnamed x9, local copies, waits for them, and re-layouts  22.3 us
    dot_general x1, matrix products, shards(): lax.dot_general(features, grad_pre, (((0,), (0,)), ((), ())), preferred_e...  14.7 us
    dot_general x1, matrix products, shards(): pre = jnp.dot(features, panel, preferred_element_type=jnp.float32)  11 us
    dot_general x1, matrix products, shards(): lax.dot_general(grad_pre, panel, (((1,), (1,)), ((), ())), preferred_elem...  8.48 us
    reduce_scatter x1, waiting for transfers between devices, shards(): lax.psum_scatter(partial_input, 'col', scatter_dimension=1, tiled=True)  7.12 us
  transfers between devices with their start and end apart: 4, of which 4 were waited for; matrix products, arithmetic and copies ran while one was open for 11% of the time, Pallas kernels for 0%

commit v1 on v0

v1 whole, which is shorter than its diff:
```python
import functools

import jax
import jax.numpy as jnp
from jax import lax
from jax.experimental import pallas as pl
from jax.experimental.pallas import tpu as pltpu
from jax.sharding import PartitionSpec as P

N = 4
BF = jnp.bfloat16
F32 = jnp.float32


def shift(block, step, first):
    pairs = []
    for y in range(N):
        for x in range(N):
            for col in range(2 * N):
                if first == (col % 2 == 0):
                    to = y * N + (x + step) % N
                else:
                    to = (y + step) % N * N + x
                pairs.append(((y * N + x) * 2 * N + col, to * 2 * N + col))
    return lax.ppermute(block, ("row", "col"), pairs)


def small(block, step):
    return shift(block, step, True)


def big(block, step):
    return shift(block, step, False)


def shift_z(block, step):
    pairs = [(2 * z + core, 2 * ((z + step) % N) + core) for z in range(N) for core in range(2)]
    return lax.ppermute(block, "col", pairs)


def swap_core(block):
    pairs = [(col, col ^ 1) for col in range(2 * N)]
    return lax.ppermute(block, "col", pairs)


def tied(*values):
    return lax.optimization_barrier(values)


def dot(a, b, ca, cb):
    return lax.dot_general(a, b, (((ca,), (cb,)), ((), ())), preferred_element_type=F32)


def whole(count):
    return [pl.BlockSpec(memory_space=pltpu.VMEM)] * count


def limits(flops, moved, transcendentals=0):
    return dict(
        compiler_params=pltpu.CompilerParams(vmem_limit_bytes=48 * 2**20),
        cost_estimate=pl.CostEstimate(
            flops=flops, bytes_accessed=moved, transcendentals=transcendentals
        ),
    )


def turn_kernel(source, out):
    out[...] = source[...].T


def turn(block):
    return pl.pallas_call(
        turn_kernel,
        out_shape=jax.ShapeDtypeStruct(block.shape[::-1], block.dtype),
        in_specs=whole(1),
        out_specs=whole(1)[0],
        **limits(0, 4 * block.size),
    )(block)


def chip(place, i, j):
    turned = place[3] == 1
    y = lax.rem(place[0] + jnp.where(turned, j, i), N)
    x = lax.rem(place[1] + jnp.where(turned, i, j), N)
    return y * N + x, y, x


def order_kernel(place, source, out, sem):
    depth = out.shape[2]
    copies = []
    for i in range(N):
        for j in range(N):
            row, _, _ = chip(place, i, j)
            copies.append(
                pltpu.make_async_copy(
                    source.at[pl.ds(pl.multiple_of(row * depth, depth), depth)], out.at[i, j], sem.at[i, j]
                )
            )
            copies[-1].start()
    for copy in copies:
        copy.wait()


def ordered(place, features):
    rows, count = features.shape
    return pl.pallas_call(
        order_kernel,
        out_shape=jax.ShapeDtypeStruct((N, N, rows // (N * N), count), features.dtype),
        in_specs=[pl.BlockSpec(memory_space=pltpu.SMEM), pl.BlockSpec(memory_space=pl.ANY)],
        out_specs=whole(1)[0],
        scratch_shapes=[pltpu.SemaphoreType.DMA((N, N))],
        **limits(0, 4 * features.size),
    )(place, features)


def add_pieces(total, rel, pieces, tokens):
    for (i, h), piece in pieces.items():
        left = rel[i, 2 * h : 2 * h + 2, :, tokens]
        term = dot(left.reshape(-1, left.shape[-1]), piece[...].reshape(-1, piece.shape[-1]), 0, 0)
        total = term if total is None else total + term
    return total


STEP = 128


def sum_kernel(keys, has_first, rel, *refs):
    first = refs[0] if has_first else None
    pieces = dict(zip(keys, refs[has_first : has_first + len(keys)]))
    out = refs[-1]
    for at in range(0, out.shape[0], STEP):
        tokens = slice(at, at + STEP)
        out[tokens] = add_pieces(first[tokens] if has_first else None, rel, pieces, tokens)


def add_sums(rel, first, pieces):
    shape = (rel.shape[-1], next(iter(pieces.values())).shape[-1])
    firsts = () if first is None else (first,)
    return pl.pallas_call(
        functools.partial(sum_kernel, tuple(pieces), len(firsts)),
        out_shape=jax.ShapeDtypeStruct(shape, F32),
        in_specs=whole(1 + len(firsts) + len(pieces)),
        out_specs=whole(1)[0],
        **limits(4 * shape[0] * rel.shape[2] * shape[1] * len(pieces), 12 * 2**20),
    )(rel, *firsts, *pieces.values())


def late_kernel(keys, rel, sums, cot, *refs):
    pieces = dict(zip(keys, refs))
    activated, grad = refs[len(keys) :]
    for at in range(0, sums.shape[0], STEP):
        tokens = slice(at, at + STEP)
        pre = add_pieces(sums[tokens], rel, pieces, tokens)
        square = pre * pre
        bend = jnp.tanh(0.7978845608028654 * (pre + 0.044715 * (square * pre)))
        rise = 0.5 + 0.5 * bend
        activated[tokens] = (pre * rise).astype(BF)
        slope = rise + 0.5 * pre * (1.0 - bend * bend) * (
            0.7978845608028654 * (1.0 + 3 * 0.044715 * square)
        )
        grad[tokens] = (cot[tokens].astype(F32) * slope).astype(BF)


def finish(rel, sums, cot, pieces):
    out = jax.ShapeDtypeStruct(sums.shape, BF)
    return pl.pallas_call(
        functools.partial(late_kernel, tuple(pieces)),
        out_shape=(out, out),
        in_specs=whole(3 + len(pieces)),
        out_specs=whole(2),
        **limits(4 * sums.size * rel.shape[2] * len(pieces), 10 * 2**20, sums.size),
    )(rel, sums, cot, *pieces.values())


def input_kernel(keys, place, g, *refs):
    pieces = dict(zip(keys, refs))
    kept, given, turned = refs[len(keys) :]
    turned[...] = g[...].T
    z, core = place[2], place[3]
    for (i, h), piece in pieces.items():
        depth = piece.shape[1]
        for j in (2 * h, 2 * h + 1):
            total = dot(piece[j % 2], turned[...], 1, 0)
            _, ahead, other = chip(place, i, j)
            to = lax.rem(ahead + N - z, N) * 2 + lax.rem(other, 2)
            rows = pl.ds(pl.multiple_of(to * depth, depth), depth)
            mine = other // 2 == core

            @pl.when(mine)
            def _():
                kept[rows] = total

            @pl.when(jnp.logical_not(mine))
            def _():
                given[rows] = total.astype(given.dtype)


def input_partial(place, g, pieces):
    count, width = g.shape
    rows = N * N * pieces[0, 0].shape[1] // 2
    return pl.pallas_call(
        functools.partial(input_kernel, tuple(pieces)),
        out_shape=(jax.ShapeDtypeStruct((rows, count), F32), jax.ShapeDtypeStruct((rows, count), BF)),
        in_specs=[pl.BlockSpec(memory_space=pltpu.SMEM)] + whole(1 + len(pieces)),
        out_specs=tuple(whole(2)),
        scratch_shapes=[pltpu.VMEM((width, count), BF)],
        **limits(4 * rows * width * count, 8 * 2**20),
    )(place, g, *pieces.values())


def shards(tokens, weight, cotangent):
    row, col = lax.axis_index("row"), lax.axis_index("col")
    place = jnp.stack([row // N, row % N, col // 2, col % 2])
    depth, count = weight.shape[0], tokens.shape[0]
    features = lax.all_gather(turn(tokens), "col", axis=0, tiled=True)

    up, down, across = small(weight, -1), small(weight, 1), small(weight, 2)
    w = {(0, 0): jnp.stack([weight, up]), (0, 1): jnp.stack([across, down])}
    w[1, 0] = big(w[0, 0], -1)
    w[3, 1] = big(w[0, 1], 1)
    w[1, 1] = big(w[0, 1], -1)
    w[3, 0] = big(w[0, 0], 1)
    w[1, 0], w[3, 0], features = tied(w[1, 0], w[3, 0], features)
    rel = ordered(place, features)
    sums = add_sums(rel, None, {k: w[k] for k in ((0, 0), (0, 1), (1, 0), (3, 0))})
    w[2, 0] = big(w[1, 0], -1)
    w[2, 1] = big(w[3, 1], 1)
    sums = add_sums(rel, sums, {k: w[k] for k in ((1, 1), (3, 1))})
    activated, g = finish(rel, sums, cotangent, {k: w[k] for k in ((2, 0), (2, 1))})

    def part(i, h):
        block = rel[i, 2 * h : 2 * h + 2].reshape(2 * depth, count)
        return dot(block, g, 1, 0).reshape(2, depth, -1)

    to_up = big(part(2, 0).astype(BF), 1)
    to_down = big(part(2, 1).astype(BF), -1)
    up_high = big(part(1, 1).astype(BF), 1)
    down_low = big(part(3, 0).astype(BF), -1)
    to_up, to_down, later = tied(to_up, to_down, g)
    up_low = big((part(1, 0) + to_up.astype(F32)).astype(BF), 1)
    down_high = big((part(3, 1) + to_down.astype(F32)).astype(BF), -1)
    kept, given = input_partial(place, later, w)
    high = part(0, 1) + up_high.astype(F32) + down_high.astype(F32)
    low = part(0, 0) + up_low.astype(F32) + down_low.astype(F32)
    across = small(high[0].astype(BF), 2)
    up = small(low[1].astype(BF), 1)
    down = small(high[1].astype(BF), -1)
    weight_grad = low[0] + up.astype(F32) + down.astype(F32) + across.astype(F32)

    sums = (kept + swap_core(given).astype(F32)).reshape(N, -1, count)
    sent = sums.astype(BF)
    z1, z3, z2 = shift_z(sent[1], 1), shift_z(sent[3], -1), shift_z(sent[2], 2)
    input_grad = (sums[0] + z1.astype(F32) + z2.astype(F32) + z3.astype(F32)).T.astype(BF)
    return (activated, input_grad, weight_grad)


def solution(mesh):
    specs = (P("row", "col"), P("row", "col"), P("row", "col"))
    return jax.shard_map(shards, mesh=mesh, in_specs=specs, out_specs=specs, check_vma=False)
```

time: 314 us -> 173 us (0.55)
  waiting for transfers between devices: 240 us -> 65.3 us
  Pallas kernels: 0 us -> 37 us
  starting transfers between devices: 0.16 us -> 32.1 us
  matrix products: 34.2 us -> 9.78 us
  local copies, waits for them, and re-layouts: 22.3 us -> 7.5 us
    unnamed x5 -> x1, waiting for transfers between devices: 124 us -> 0.02 us
    all_gather x2 -> x1, waiting for transfers between devices: 109 us -> 0.01 us  [shards(): features = lax.all_gather(turn(tokens), 'col', axis=0, tiled=True)]
    ppermute x0 -> x22, waiting for transfers between devices: none -> 65.3 us  [the longest x18 57.7 us: shift(): return lax.ppermute(block, ('row', 'col'), pairs)]
    pallas_call x0 -> x6, Pallas kernels: none -> 37 us  [the longest x1 13 us: input_partial(): pl.pallas_call(functools.partial(input_kernel, tuple(pieces)), out_shape=...]
    ppermute x0 -> x22, starting transfers between devices: none -> 32.1 us  [the longest x18 25.5 us: shift(): return lax.ppermute(block, ('row', 'col'), pairs)]
    dot_general x3 -> x8, matrix products: 34.2 us -> 9.78 us  [dot(): lax.dot_general(a, b, (((ca,), (cb,)), ((), ())), preferred_element_type=...]
    unnamed x9 -> x25, local copies, waits for them, and re-layouts: 22.3 us -> 7.28 us
    reduce_scatter x1 -> x0, waiting for transfers between devices: 7.12 us -> none  [shards(): lax.psum_scatter(partial_input, 'col', scatter_dimension=1, tiled=True)]
  transfers between devices with their start and end apart: 4 -> 23, of which waited for: 4 -> 12; matrix products, arithmetic and copies ran while one was open for 11% -> 7% of each run, Pallas kernels for 0% -> 16%
where the time goes in v1:
time: 173 us; the launch traced here: 169 us
  waiting for transfers between devices  65.3 us (38%)
  Pallas kernels  37 us (21%)
  starting transfers between devices  32.1 us (19%)
  between operations  14.2 us (8%)
  matrix products  9.78 us (6%)
  local copies, waits for them, and re-layouts  7.5 us (4%)
  other arithmetic  3.43 us (2%)
    ppermute x18, waiting for transfers between devices, shift(): return lax.ppermute(block, ('row', 'col'), pairs)  57.7 us
    ppermute x18, starting transfers between devices, shift(): return lax.ppermute(block, ('row', 'col'), pairs)  25.5 us
    pallas_call x1, Pallas kernels, input_partial(): pl.pallas_call(functools.partial(input_kernel, tuple(pieces)), out_shape=...  13 us
    pallas_call x2, Pallas kernels, add_sums(): pl.pallas_call(functools.partial(sum_kernel, tuple(pieces), len(firsts)),...  12.1 us
    dot_general x8, matrix products, dot(): lax.dot_general(a, b, (((ca,), (cb,)), ((), ())), preferred_element_type=...  9.78 us
    pallas_call x1, Pallas kernels, finish(): pl.pallas_call(functools.partial(late_kernel, tuple(pieces)), out_shape=(...  8.28 us
    ppermute x3, waiting for transfers between devices, shift_z(): return lax.ppermute(block, 'col', pairs)  7.53 us
    unnamed x25, local copies, waits for them, and re-layouts  7.28 us
  transfers between devices with their start and end apart: 23, of which 12 were waited for; matrix products, arithmetic and copies ran while one was open for 7% of the time, Pallas kernels for 16%

profile of v1, /device:TPU:6, one launch (start us, length us, event | category | flops | bytes accessed | tf_op | source)
XLA Modules:
  0.0 169.4 jit_solution(5903024966869635360)
XLA Ops:
  9.1 1.5 collective-permute-start.3
  10.6 2.1 %collective-permute-start.4 = (bf16[192,1536]{1,0:T(8,128)(2,1)}, bf16[192,1536]{1,0:T(8,128)(2,1)S(1)}, u32[]{:S(2)}, u32[]{:S(2)}) collective-permute-start(bf16[192,1536]{1,0:T(8,128)(2,1)} %param.4), channel_id=1, source_target_pairs={{0,8},{1,33},{2,10},{3,35},{4,12},{5,37},{6,14},{7,39},{8,16},{9,4... | collective-permute-start | bytes 1769480 | tf_op jit(solution)/shard_map/ppermute | solution.py:25
  12.7 8.2 %collective-permute-done.3 = bf16[192,1536]{1,0:T(8,128)(2,1)S(1)} collective-permute-done((bf16[192,1536]{1,0:T(8,128)(2,1)}, bf16[192,1536]{1,0:T(8,128)(2,1)S(1)}, u32[]{:S(2)}, u32[]{:S(2)}) %collective-permute-start.3) | collective-permute-done | bytes 589856 | tf_op jit(solution)/shard_map/ppermute | solution.py:25
  20.9 4.0 %collective-permute-done.4 = bf16[192,1536]{1,0:T(8,128)(2,1)S(1)} collective-permute-done((bf16[192,1536]{1,0:T(8,128)(2,1)}, bf16[192,1536]{1,0:T(8,128)(2,1)S(1)}, u32[]{:S(2)}, u32[]{:S(2)}) %collective-permute-start.4) | collective-permute-done | bytes 589856 | tf_op jit(solution)/shard_map/ppermute | solution.py:25
  25.0 1.7 %collective-permute-start.6 = (bf16[2,192,1536]{2,1,0:T(8,128)(2,1)S(1)}, bf16[2,192,1536]{2,1,0:T(8,128)(2,1)S(1)}, u32[]{:S(2)}, u32[]{:S(2)}) collective-permute-start(bf16[2,192,1536]{2,1,0:T(8,128)(2,1)S(1)} %pad_maximum_fusion.1.refs_1_), channel_id=1, source_target_pairs={{0,32},{1,9},{2,34},{3,11},{4,36},{5,13},{6,38},{7,15},{8,40},{9,1... | collective-permute-start | bytes 3538952 | tf_op jit(solution)/shard_map/ppermute | solution.py:25
  28.3 3.1 %collective-permute-start.1 = (bf16[2,192,1536]{2,1,0:T(8,128)(2,1)S(1)}, bf16[2,192,1536]{2,1,0:T(8,128)(2,1)S(1)}, u32[]{:S(2)}, u32[]{:S(2)}) collective-permute-start(bf16[2,192,1536]{2,1,0:T(8,128)(2,1)S(1)} %pad_maximum_fusion.refs_0_), channel_id=1, source_target_pairs={{0,96},{1,25},{2,98},{3,27},{4,100},{5,29},{6,102},{7,31},{8,104},... | collective-permute-start | bytes 3538952 | tf_op jit(solution)/shard_map/ppermute | solution.py:25
  31.4 3.2 %collective-permute-start.5 = (bf16[2,192,1536]{2,1,0:T(8,128)(2,1)S(1)}, bf16[2,192,1536]{2,1,0:T(8,128)(2,1)}, u32[]{:S(2)}, u32[]{:S(2)}) collective-permute-start(bf16[2,192,1536]{2,1,0:T(8,128)(2,1)S(1)} %pad_maximum_fusion.1.refs_1_), channel_id=1, source_target_pairs={{0,96},{1,25},{2,98},{3,27},{4,100},{5,29},{6,102},{7,31},{8,104},... | collective-permute-start | bytes 3538952 | tf_op jit(solution)/shard_map/ppermute | solution.py:25
  34.6 7.9 %collective-permute-done.6.refs_2_.refs_3_ = bf16[2,192,1536]{2,1,0:T(8,128)(2,1)S(1)} collective-permute-done((bf16[2,192,1536]{2,1,0:T(8,128)(2,1)S(1)}, bf16[2,192,1536]{2,1,0:T(8,128)(2,1)S(1)}, u32[]{:S(2)}, u32[]{:S(2)}) %collective-permute-start.6) | collective-permute-done | bytes 1179680 | tf_op jit(solution)/shard_map/ppermute | solution.py:25
  42.9 2.2 %collective-permute-done.1.refs_2_ = bf16[2,192,1536]{2,1,0:T(8,128)(2,1)S(1)} collective-permute-done((bf16[2,192,1536]{2,1,0:T(8,128)(2,1)S(1)}, bf16[2,192,1536]{2,1,0:T(8,128)(2,1)S(1)}, u32[]{:S(2)}, u32[]{:S(2)}) %collective-permute-start.1) | collective-permute-done | bytes 1179680 | tf_op jit(solution)/shard_map/ppermute | solution.py:25
  46.1 9.0 %collective-permute-done.2.refs_3_.refs_5_ = bf16[2,192,1536]{2,1,0:T(8,128)(2,1)S(1)} collective-permute-done((bf16[2,192,1536]{2,1,0:T(8,128)(2,1)S(1)}, bf16[2,192,1536]{2,1,0:T(8,128)(2,1)S(1)}, u32[]{:S(2)}, u32[]{:S(2)}) %collective-permute-start.2) | collective-permute-done | bytes 1179680 | tf_op jit(solution)/shard_map/ppermute | solution.py:25
  56.2 1.9 %collective-permute-start.7 = (bf16[2,192,1536]{2,1,0:T(8,128)(2,1)}, bf16[2,192,1536]{2,1,0:T(8,128)(2,1)}, u32[]{:S(2)}, u32[]{:S(2)}) collective-permute-start(bf16[2,192,1536]{2,1,0:T(8,128)(2,1)} %copy-done.6), channel_id=1, source_target_pairs={{0,96},{1,25},{2,98},{3,27},{4,100},{5,29},{6,102},{7,31},{8,104},... | collective-permute-start | bytes 3538952 | tf_op jit(solution)/shard_map/ppermute | solution.py:25
  58.1 2.8 %shard_map.59.rel = bf16[4,4,192,512]{3,2,1,0:T(8,128)(2,1)S(1)} custom-call(s32[4]{0:T(128)S(1)} %pad_add_fusion.place, bf16[3072,512]{1,0:T(8,128)(2,1)} %all-gather.2.cloned.1.call-done.source), custom_call_target="tpu_custom_call" | custom-call | bytes 6291456 | tf_op jit(solution)/shard_map/pallas_call | solution.py:106
  60.9 1.6 copy-done
  62.5 7.0 %shard_map.60.refs_0_ = f32[512,1536]{1,0:T(8,128)} custom-call(bf16[4,4,192,512]{3,2,1,0:T(8,128)(2,1)} %copy-done, bf16[2,192,1536]{2,1,0:T(8,128)(2,1)S(1)} %pad_maximum_fusion.refs_0_, bf16[2,192,1536]{2,1,0:T(8,128)(2,1)S(1)} %pad_maximum_fusion.1.refs_1_, bf16[2,192,1536]{2,1,0:T(8,128)(2,1)S(1)} %copy-done.7, bf16[2,192,1536]{2,1,0:T(8,128)(2,1)S(1)} %copy-done.9), custom_call_target="tpu_custom_call" | custom-call | flops 2415919104 | bytes 12582912 | tf_op jit(solution)/shard_map/pallas_call | solution.py:139
  69.6 5.1 %shard_map.61.sums = f32[512,1536]{1,0:T(8,128)S(1)} custom-call(bf16[4,4,192,512]{3,2,1,0:T(8,128)(2,1)} %copy-done, f32[512,1536]{1,0:T(8,128)} %shard_map.60.refs_0_, bf16[2,192,1536]{2,1,0:T(8,128)(2,1)} %collective-permute-done.5.refs_1_.refs_4_, bf16[2,192,1536]{2,1,0:T(8,128)(2,1)S(1)} %collective-permute-done.6.refs_2_.refs_3_), custom_call_target="tpu_custom_call" | custom-call | flops 1207959552 | bytes 12582912 | tf_op jit(solution)/shard_map/pallas_call | solution.py:139
  74.7 1.7 copy-done.2
  76.4 8.3 %shard_map.62 = (bf16[512,1536]{1,0:T(8,128)(2,1)}, bf16[512,1536]{1,0:T(8,128)(2,1)S(1)}) custom-call(bf16[4,4,192,512]{3,2,1,0:T(8,128)(2,1)} %copy-done, f32[512,1536]{1,0:T(8,128)} %copy-done.2, bf16[512,1536]{1,0:T(8,128)(2,1)S(1)} %copy-done.3, bf16[2,192,1536]{2,1,0:T(8,128)(2,1)} %collective-permute-done.7.refs_0_.refs_6_, ...), custom_call_target="tpu_custom_call" | custom-call | flops 1207959552 | bytes 10485760 | tf_op jit(solution)/shard_map/pallas_call | solution.py:166
  88.3 1.9 %convolution_convert_fusion = bf16[2,192,1536]{2,1,0:T(8,128)(2,1)} fusion(bf16[512,1536]{1,0:T(8,128)(2,1)S(1)} %get-tuple-element.18.g, bf16[4,4,192,512]{3,2,1,0:T(8,128)(2,1)S(1)} %copy-done.1), kind=kOutput, calls=%fused_computation.10 | convolution fusion | flops 604569600 | bytes 3145728 | tf_op jit(solution)/shard_map/dot_general | solution.py:51
  90.3 12.2 %collective-permute-done.10 = bf16[2,192,1536]{2,1,0:T(8,128)(2,1)S(1)} collective-permute-done((bf16[2,192,1536]{2,1,0:T(8,128)(2,1)S(1)}, bf16[2,192,1536]{2,1,0:T(8,128)(2,1)S(1)}, u32[]{:S(2)}, u32[]{:S(2)}) %collective-permute-start.10) | collective-permute-done | bytes 1179680 | tf_op jit(solution)/shard_map/ppermute | solution.py:25
  102.5 2.0 %collective-permute-done.9 = bf16[2,192,1536]{2,1,0:T(8,128)(2,1)S(1)} collective-permute-done((bf16[2,192,1536]{2,1,0:T(8,128)(2,1)S(1)}, bf16[2,192,1536]{2,1,0:T(8,128)(2,1)S(1)}, u32[]{:S(2)}, u32[]{:S(2)}) %collective-permute-start.9) | collective-permute-done | bytes 1179680 | tf_op jit(solution)/shard_map/ppermute | solution.py:25
  104.4 1.8 %fusion.4 = bf16[2,192,1536]{2,1,0:T(8,128)(2,1)} fusion(bf16[2,192,1536]{2,1,0:T(8,128)(2,1)S(1)} %collective-permute-done.10, bf16[512,1536]{1,0:T(8,128)(2,1)S(1)} %get-tuple-element.18.g, bf16[4,4,192,512]{3,2,1,0:T(8,128)(2,1)S(1)} %copy-done.1), kind=kOutput, calls=%fused_computation.9 | convolution fusion | flops 605749248 | bytes 4325376 | tf_op jit(solution)/shard_map/dot_general | solution.py:51
  108.9 1.3 collective-permute-start.15
  110.3 13.0 %shard_map.63 = (f32[1536,512]{1,0:T(8,128)}, bf16[1536,512]{1,0:T(8,128)(2,1)}) custom-call(s32[4]{0:T(128)S(1)} %pad_add_fusion.place, bf16[512,1536]{1,0:T(8,128)(2,1)} %copy-done.4, bf16[2,192,1536]{2,1,0:T(8,128)(2,1)S(1)} %pad_maximum_fusion.refs_0_, bf16[2,192,1536]{2,1,0:T(8,128)(2,1)S(1)} %pad_maximum_fusion.1.refs_1_, ...), custom_call_target="tpu_custom_call" | custom-call | flops 4831838208 | bytes 8388608 | tf_op jit(solution)/shard_map/pallas_call | solution.py:201
  123.3 2.1 %fusion.2 = bf16[2,192,1536]{2,1,0:T(8,128)(2,1)S(1)} fusion(bf16[2,192,1536]{2,1,0:T(8,128)(2,1)} %collective-permute-done.19, bf16[2,192,1536]{2,1,0:T(8,128)(2,1)S(1)} %collective-permute-done.18, bf16[512,1536]{1,0:T(8,128)(2,1)S(1)} %copy-done.5, bf16[4,4,192,512]{3,2,1,0:T(8,128)(2,1)S(1)} %copy-done.1), kind=kOutput, calls=%fused_computation.7 | convolution fusion | flops 606928896 | bytes 5505024 | tf_op jit(solution)/shard_map/dot_general | solution.py:51
  125.5 2.2 %collective-permute-start.20 = (bf16[192,1536]{1,0:T(8,128)(2,1)S(1)}, bf16[192,1536]{1,0:T(8,128)(2,1)S(1)}, u32[]{:S(2)}, u32[]{:S(2)}) collective-permute-start(bf16[192,1536]{1,0:T(8,128)(2,1)S(1)} %get-tuple-element.31), channel_id=1, source_target_pairs={{0,24},{1,97},{2,26},{3,99},{4,28},{5,101},{6,30},{7,103},{8,0},{9... | collective-permute-start | bytes 1769480 | tf_op jit(solution)/shard_map/ppermute | solution.py:25
  127.8 1.9 %collective-permute-start.21 = (bf16[192,1536]{1,0:T(8,128)(2,1)S(1)}, bf16[192,1536]{1,0:T(8,128)(2,1)S(1)}, u32[]{:S(2)}, u32[]{:S(2)}) collective-permute-start(bf16[192,1536]{1,0:T(8,128)(2,1)S(1)} %get-tuple-element.32), channel_id=1, source_target_pairs={{0,16},{1,65},{2,18},{3,67},{4,20},{5,69},{6,22},{7,71},{8,24},{9,... | collective-permute-start | bytes 1769480 | tf_op jit(solution)/shard_map/ppermute | solution.py:25
  129.7 11.9 %collective-permute-done.16 = bf16[2,192,1536]{2,1,0:T(8,128)(2,1)S(1)} collective-permute-done((bf16[2,192,1536]{2,1,0:T(8,128)(2,1)S(1)}, bf16[2,192,1536]{2,1,0:T(8,128)(2,1)S(1)}, u32[]{:S(2)}, u32[]{:S(2)}) %collective-permute-start.16) | collective-permute-done | bytes 1179680 | tf_op jit(solution)/shard_map/ppermute | solution.py:25
  142.5 2.7 %collective-permute-start.17 = (bf16[192,1536]{1,0:T(8,128)(2,1)S(1)}, bf16[192,1536]{1,0:T(8,128)(2,1)S(1)}, u32[]{:S(2)}, u32[]{:S(2)}) collective-permute-start(bf16[192,1536]{1,0:T(8,128)(2,1)S(1)} %fusion.19), channel_id=1, source_target_pairs={{0,8},{1,33},{2,10},{3,35},{4,12},{5,37},{6,14},{7,39},{8,16},{9,4... | collective-permute-start | bytes 1769480 | tf_op jit(solution)/shard_map/ppermute | solution.py:25
  145.9 2.0 %collective-permute-start.12 = (bf16[384,512]{1,0:T(8,128)(2,1)S(1)}, bf16[384,512]{1,0:T(8,128)(2,1)S(1)}, u32[]{:S(2)}, u32[]{:S(2)}) collective-permute-start(bf16[384,512]{1,0:T(8,128)(2,1)S(1)} %get-tuple-element.28), channel_id=1, source_target_pairs={{0,2},{1,3},{2,4},{3,5},{4,6},{5,7},{6,0},{7,1},{8,10},{9,11},{10,... | collective-permute-start | bytes 1179656 | tf_op jit(solution)/shard_map/ppermute | solution.py:38
  147.9 3.6 %collective-permute-start.13 = (bf16[384,512]{1,0:T(8,128)(2,1)S(1)}, bf16[384,512]{1,0:T(8,128)(2,1)S(1)}, u32[]{:S(2)}, u32[]{:S(2)}) collective-permute-start(bf16[384,512]{1,0:T(8,128)(2,1)S(1)} %get-tuple-element.30), channel_id=1, source_target_pairs={{0,4},{1,5},{2,6},{3,7},{4,0},{5,1},{6,2},{7,3},{8,12},{9,13},{10,... | collective-permute-start | bytes 1179656 | tf_op jit(solution)/shard_map/ppermute | solution.py:38
  153.9 1.9 %collective-permute-done.12 = bf16[384,512]{1,0:T(8,128)(2,1)S(1)} collective-permute-done((bf16[384,512]{1,0:T(8,128)(2,1)S(1)}, bf16[384,512]{1,0:T(8,128)(2,1)S(1)}, u32[]{:S(2)}, u32[]{:S(2)}) %collective-permute-start.12) | collective-permute-done | bytes 393248 | tf_op jit(solution)/shard_map/ppermute | solution.py:38
  155.7 5.7 %collective-permute-done.13 = bf16[384,512]{1,0:T(8,128)(2,1)S(1)} collective-permute-done((bf16[384,512]{1,0:T(8,128)(2,1)S(1)}, bf16[384,512]{1,0:T(8,128)(2,1)S(1)}, u32[]{:S(2)}, u32[]{:S(2)}) %collective-permute-start.13) | collective-permute-done | bytes 393248 | tf_op jit(solution)/shard_map/ppermute | solution.py:38
  (63 shorter events, 17.9 us)
Async XLA Ops:
  7.2 49.0 %all-gather.2.cloned.1.call-start = ((), (), s32[]{:S(2)}) async-start(), calls=%async_computation | async-start | bytes 3538944 | tf_op jit(solution)/shard_map/all_gather | solution.py:215
  9.1 11.8 %collective-permute-start.3 = (bf16[192,1536]{1,0:T(8,128)(2,1)}, bf16[192,1536]{1,0:T(8,128)(2,1)S(1)}, u32[]{:S(2)}, u32[]{:S(2)}) collective-permute-start(bf16[192,1536]{1,0:T(8,128)(2,1)} %param.4), channel_id=1, source_target_pairs={{0,16},{1,65},{2,18},{3,67},{4,20},{5,69},{6,22},{7,71},{8,24},{9,... | collective-permute-start | bytes 1769480 | tf_op jit(solution)/shard_map/ppermute | solution.py:25
  10.6 14.3 %collective-permute-start.4 = (bf16[192,1536]{1,0:T(8,128)(2,1)}, bf16[192,1536]{1,0:T(8,128)(2,1)S(1)}, u32[]{:S(2)}, u32[]{:S(2)}) collective-permute-start(bf16[192,1536]{1,0:T(8,128)(2,1)} %param.4), channel_id=1, source_target_pairs={{0,8},{1,33},{2,10},{3,35},{4,12},{5,37},{6,14},{7,39},{8,16},{9,4... | collective-permute-start | bytes 1769480 | tf_op jit(solution)/shard_map/ppermute | solution.py:25
  12.7 14.4 %collective-permute-start = (bf16[192,1536]{1,0:T(8,128)(2,1)}, bf16[192,1536]{1,0:T(8,128)(2,1)S(1)}, u32[]{:S(2)}, u32[]{:S(2)}) collective-permute-start(bf16[192,1536]{1,0:T(8,128)(2,1)} %param.4), channel_id=1, source_target_pairs={{0,24},{1,97},{2,26},{3,99},{4,28},{5,101},{6,30},{7,103},{8,0},{9... | collective-permute-start | bytes 1769480 | tf_op jit(solution)/shard_map/ppermute | solution.py:25
  25.0 17.5 %collective-permute-start.6 = (bf16[2,192,1536]{2,1,0:T(8,128)(2,1)S(1)}, bf16[2,192,1536]{2,1,0:T(8,128)(2,1)S(1)}, u32[]{:S(2)}, u32[]{:S(2)}) collective-permute-start(bf16[2,192,1536]{2,1,0:T(8,128)(2,1)S(1)} %pad_maximum_fusion.1.refs_1_), channel_id=1, source_target_pairs={{0,32},{1,9},{2,34},{3,11},{4,36},{5,13},{6,38},{7,15},{8,40},{9,1... | collective-permute-start | bytes 3538952 | tf_op jit(solution)/shard_map/ppermute | solution.py:25
  28.3 16.8 %collective-permute-start.1 = (bf16[2,192,1536]{2,1,0:T(8,128)(2,1)S(1)}, bf16[2,192,1536]{2,1,0:T(8,128)(2,1)S(1)}, u32[]{:S(2)}, u32[]{:S(2)}) collective-permute-start(bf16[2,192,1536]{2,1,0:T(8,128)(2,1)S(1)} %pad_maximum_fusion.refs_0_), channel_id=1, source_target_pairs={{0,96},{1,25},{2,98},{3,27},{4,100},{5,29},{6,102},{7,31},{8,104},... | collective-permute-start | bytes 3538952 | tf_op jit(solution)/shard_map/ppermute | solution.py:25
  31.4 23.7 %collective-permute-start.2 = (bf16[2,192,1536]{2,1,0:T(8,128)(2,1)S(1)}, bf16[2,192,1536]{2,1,0:T(8,128)(2,1)S(1)}, u32[]{:S(2)}, u32[]{:S(2)}) collective-permute-start(bf16[2,192,1536]{2,1,0:T(8,128)(2,1)S(1)} %pad_maximum_fusion.refs_0_), channel_id=1, source_target_pairs={{0,32},{1,9},{2,34},{3,11},{4,36},{5,13},{6,38},{7,15},{8,40},{9,1... | collective-permute-start | bytes 3538952 | tf_op jit(solution)/shard_map/ppermute | solution.py:25
  31.4 38.2 %collective-permute-start.5 = (bf16[2,192,1536]{2,1,0:T(8,128)(2,1)S(1)}, bf16[2,192,1536]{2,1,0:T(8,128)(2,1)}, u32[]{:S(2)}, u32[]{:S(2)}) collective-permute-start(bf16[2,192,1536]{2,1,0:T(8,128)(2,1)S(1)} %pad_maximum_fusion.1.refs_1_), channel_id=1, source_target_pairs={{0,96},{1,25},{2,98},{3,27},{4,100},{5,29},{6,102},{7,31},{8,104},... | collective-permute-start | bytes 3538952 | tf_op jit(solution)/shard_map/ppermute | solution.py:25
  42.5 33.8 %collective-permute-start.8 = (bf16[2,192,1536]{2,1,0:T(8,128)(2,1)S(1)}, bf16[2,192,1536]{2,1,0:T(8,128)(2,1)}, u32[]{:S(2)}, u32[]{:S(2)}) collective-permute-start(bf16[2,192,1536]{2,1,0:T(8,128)(2,1)S(1)} %collective-permute-done.6.refs_2_.refs_3_), channel_id=1, source_target_pairs={{0,32},{1,9},{2,34},{3,11},{4,36},{5,13},{6,38},{7,15},{8,40},{9,1... | collective-permute-start | bytes 3538952 | tf_op jit(solution)/shard_map/ppermute | solution.py:25
  56.2 20.2 %collective-permute-start.7 = (bf16[2,192,1536]{2,1,0:T(8,128)(2,1)}, bf16[2,192,1536]{2,1,0:T(8,128)(2,1)}, u32[]{:S(2)}, u32[]{:S(2)}) collective-permute-start(bf16[2,192,1536]{2,1,0:T(8,128)(2,1)} %copy-done.6), channel_id=1, source_target_pairs={{0,96},{1,25},{2,98},{3,27},{4,100},{5,29},{6,102},{7,31},{8,104},... | collective-permute-start | bytes 3538952 | tf_op jit(solution)/shard_map/ppermute | solution.py:25
  58.1 4.4 %copy-start.7 = (bf16[2,192,1536]{2,1,0:T(8,128)(2,1)S(1)}, bf16[2,192,1536]{2,1,0:T(8,128)(2,1)}, u32[]{:S(2)}) copy-start(bf16[2,192,1536]{2,1,0:T(8,128)(2,1)} %copy-done.6) | copy-start | bytes 3538948
  58.1 4.4 %copy-start.9 = (bf16[2,192,1536]{2,1,0:T(8,128)(2,1)S(1)}, bf16[2,192,1536]{2,1,0:T(8,128)(2,1)}, u32[]{:S(2)}) copy-start(bf16[2,192,1536]{2,1,0:T(8,128)(2,1)} %copy-done.8) | copy-start | bytes 3538948
  60.9 1.6 copy-start
  69.6 6.8 %copy-start.3 = (bf16[512,1536]{1,0:T(8,128)(2,1)S(1)}, bf16[512,1536]{1,0:T(8,128)(2,1)}, u32[]{:S(2)}) copy-start(bf16[512,1536]{1,0:T(8,128)(2,1)} %cot.1) | copy-start | bytes 4718596
  74.6 1.7 copy-start.2
  76.3 8.3 %copy-start.1 = (bf16[4,4,192,512]{3,2,1,0:T(8,128)(2,1)S(1)}, bf16[4,4,192,512]{3,2,1,0:T(8,128)(2,1)}, u32[]{:S(2)}) copy-start(bf16[4,4,192,512]{3,2,1,0:T(8,128)(2,1)} %copy-done) | copy-start | bytes 9437188
  84.6 23.5 %copy-start.4 = (bf16[512,1536]{1,0:T(8,128)(2,1)}, bf16[512,1536]{1,0:T(8,128)(2,1)S(1)}, u32[]{:S(2)}) copy-start(bf16[512,1536]{1,0:T(8,128)(2,1)S(1)} %get-tuple-element.18.g) | copy-start | bytes 4718596
  86.2 16.3 %collective-permute-start.10 = (bf16[2,192,1536]{2,1,0:T(8,128)(2,1)S(1)}, bf16[2,192,1536]{2,1,0:T(8,128)(2,1)S(1)}, u32[]{:S(2)}, u32[]{:S(2)}) collective-permute-start(bf16[2,192,1536]{2,1,0:T(8,128)(2,1)S(1)} %convolution_convert_fusion.2), channel_id=1, source_target_pairs={{0,96},{1,25},{2,98},{3,27},{4,100},{5,29},{6,102},{7,31},{8,104},... | collective-permute-start | bytes 3538952 | tf_op jit(solution)/shard_map/ppermute | solution.py:25
  87.0 17.4 %collective-permute-start.9 = (bf16[2,192,1536]{2,1,0:T(8,128)(2,1)S(1)}, bf16[2,192,1536]{2,1,0:T(8,128)(2,1)S(1)}, u32[]{:S(2)}, u32[]{:S(2)}) collective-permute-start(bf16[2,192,1536]{2,1,0:T(8,128)(2,1)S(1)} %convolution_convert_fusion.3), channel_id=1, source_target_pairs={{0,32},{1,9},{2,34},{3,11},{4,36},{5,13},{6,38},{7,15},{8,40},{9,1... | collective-permute-start | bytes 3538952 | tf_op jit(solution)/shard_map/ppermute | solution.py:25
  90.2 33.1 %collective-permute-start.18 = (bf16[2,192,1536]{2,1,0:T(8,128)(2,1)}, bf16[2,192,1536]{2,1,0:T(8,128)(2,1)S(1)}, u32[]{:S(2)}, u32[]{:S(2)}) collective-permute-start(bf16[2,192,1536]{2,1,0:T(8,128)(2,1)} %convolution_convert_fusion), channel_id=1, source_target_pairs={{0,32},{1,9},{2,34},{3,11},{4,36},{5,13},{6,38},{7,15},{8,40},{9,1... | collective-permute-start | bytes 3538952 | tf_op jit(solution)/shard_map/ppermute | solution.py:25
  106.2 17.0 %collective-permute-start.19 = (bf16[2,192,1536]{2,1,0:T(8,128)(2,1)}, bf16[2,192,1536]{2,1,0:T(8,128)(2,1)}, u32[]{:S(2)}, u32[]{:S(2)}) collective-permute-start(bf16[2,192,1536]{2,1,0:T(8,128)(2,1)} %fusion.4), channel_id=1, source_target_pairs={{0,96},{1,25},{2,98},{3,27},{4,100},{5,29},{6,102},{7,31},{8,104},... | collective-permute-start | bytes 3538952 | tf_op jit(solution)/shard_map/ppermute | solution.py:25
  107.0 34.5 %collective-permute-start.16 = (bf16[2,192,1536]{2,1,0:T(8,128)(2,1)S(1)}, bf16[2,192,1536]{2,1,0:T(8,128)(2,1)S(1)}, u32[]{:S(2)}, u32[]{:S(2)}) collective-permute-start(bf16[2,192,1536]{2,1,0:T(8,128)(2,1)S(1)} %convolution_convert_fusion.1), channel_id=1, source_target_pairs={{0,96},{1,25},{2,98},{3,27},{4,100},{5,29},{6,102},{7,31},{8,104},... | collective-permute-start | bytes 3538952 | tf_op jit(solution)/shard_map/ppermute | solution.py:25
  108.9 14.3 %copy-start.5 = (bf16[512,1536]{1,0:T(8,128)(2,1)S(1)}, bf16[512,1536]{1,0:T(8,128)(2,1)}, u32[]{:S(2)}) copy-start(bf16[512,1536]{1,0:T(8,128)(2,1)} %copy-done.4) | copy-start | bytes 4718596
  108.9 32.6 %collective-permute-start.15 = (bf16[2,192,1536]{2,1,0:T(8,128)(2,1)S(1)}, bf16[2,192,1536]{2,1,0:T(8,128)(2,1)S(1)}, u32[]{:S(2)}, u32[]{:S(2)}) collective-permute-start(bf16[2,192,1536]{2,1,0:T(8,128)(2,1)S(1)} %fusion.3), channel_id=1, source_target_pairs={{0,32},{1,9},{2,34},{3,11},{4,36},{5,13},{6,38},{7,15},{8,40},{9,1... | collective-permute-start | bytes 3538952 | tf_op jit(solution)/shard_map/ppermute | solution.py:25
  123.3 21.9 %collective-permute-start.11 = (bf16[1536,512]{1,0:T(8,128)(2,1)}, bf16[1536,512]{1,0:T(8,128)(2,1)S(1)}, u32[]{:S(2)}, u32[]{:S(2)}) collective-permute-start(bf16[1536,512]{1,0:T(8,128)(2,1)} %get-tuple-element.20), channel_id=1, source_target_pairs={{0,1},{1,0},{2,3},{3,2},{4,5},{5,4},{6,7},{7,6},{8,9},{9,8},{10,11... | collective-permute-start | bytes 4718600 | tf_op jit(solution)/shard_map/ppermute | solution.py:43
  125.5 25.9 %collective-permute-start.20 = (bf16[192,1536]{1,0:T(8,128)(2,1)S(1)}, bf16[192,1536]{1,0:T(8,128)(2,1)S(1)}, u32[]{:S(2)}, u32[]{:S(2)}) collective-permute-start(bf16[192,1536]{1,0:T(8,128)(2,1)S(1)} %get-tuple-element.31), channel_id=1, source_target_pairs={{0,24},{1,97},{2,26},{3,99},{4,28},{5,101},{6,30},{7,103},{8,0},{9... | collective-permute-start | bytes 1769480 | tf_op jit(solution)/shard_map/ppermute | solution.py:25
  127.8 24.7 %collective-permute-start.21 = (bf16[192,1536]{1,0:T(8,128)(2,1)S(1)}, bf16[192,1536]{1,0:T(8,128)(2,1)S(1)}, u32[]{:S(2)}, u32[]{:S(2)}) collective-permute-start(bf16[192,1536]{1,0:T(8,128)(2,1)S(1)} %get-tuple-element.32), channel_id=1, source_target_pairs={{0,16},{1,65},{2,18},{3,67},{4,20},{5,69},{6,22},{7,71},{8,24},{9,... | collective-permute-start | bytes 1769480 | tf_op jit(solution)/shard_map/ppermute | solution.py:25
  141.6 3.6 %copy-start.11 = (f32[1536,512]{1,0:T(8,128)S(1)}, f32[1536,512]{1,0:T(8,128)}, u32[]{:S(2)}) copy-start(f32[1536,512]{1,0:T(8,128)} %get-tuple-element.19) | copy-start | bytes 9437188
  142.5 10.1 %collective-permute-start.17 = (bf16[192,1536]{1,0:T(8,128)(2,1)S(1)}, bf16[192,1536]{1,0:T(8,128)(2,1)S(1)}, u32[]{:S(2)}, u32[]{:S(2)}) collective-permute-start(bf16[192,1536]{1,0:T(8,128)(2,1)S(1)} %fusion.19), channel_id=1, source_target_pairs={{0,8},{1,33},{2,10},{3,35},{4,12},{5,37},{6,14},{7,39},{8,16},{9,4... | collective-permute-start | bytes 1769480 | tf_op jit(solution)/shard_map/ppermute | solution.py:25
  145.9 9.9 %collective-permute-start.12 = (bf16[384,512]{1,0:T(8,128)(2,1)S(1)}, bf16[384,512]{1,0:T(8,128)(2,1)S(1)}, u32[]{:S(2)}, u32[]{:S(2)}) collective-permute-start(bf16[384,512]{1,0:T(8,128)(2,1)S(1)} %get-tuple-element.28), channel_id=1, source_target_pairs={{0,2},{1,3},{2,4},{3,5},{4,6},{5,7},{6,0},{7,1},{8,10},{9,11},{10,... | collective-permute-start | bytes 1179656 | tf_op jit(solution)/shard_map/ppermute | solution.py:38
  147.9 13.5 %collective-permute-start.13 = (bf16[384,512]{1,0:T(8,128)(2,1)S(1)}, bf16[384,512]{1,0:T(8,128)(2,1)S(1)}, u32[]{:S(2)}, u32[]{:S(2)}) collective-permute-start(bf16[384,512]{1,0:T(8,128)(2,1)S(1)} %get-tuple-element.30), channel_id=1, source_target_pairs={{0,4},{1,5},{2,6},{3,7},{4,0},{5,1},{6,2},{7,3},{8,12},{9,13},{10,... | collective-permute-start | bytes 1179656 | tf_op jit(solution)/shard_map/ppermute | solution.py:38
  151.4 10.0 %collective-permute-start.14 = (bf16[384,512]{1,0:T(8,128)(2,1)S(1)}, bf16[384,512]{1,0:T(8,128)(2,1)S(1)}, u32[]{:S(2)}, u32[]{:S(2)}) collective-permute-start(bf16[384,512]{1,0:T(8,128)(2,1)S(1)} %get-tuple-element.29), channel_id=1, source_target_pairs={{0,6},{1,7},{2,0},{3,1},{4,2},{5,3},{6,4},{7,5},{8,14},{9,15},{10,... | collective-permute-start | bytes 1179656 | tf_op jit(solution)/shard_map/ppermute | solution.py:38
  (3 other events, 3.0 us)
Sparse Core Ops, SparseCore 0:
  10.3 30.2 all-gather.1

commit v2 on v1

v2 whole, which is shorter than its diff:
```python
import functools

import jax
import jax.numpy as jnp
from jax import lax
from jax.experimental import pallas as pl
from jax.experimental.pallas import tpu as pltpu
from jax.sharding import PartitionSpec as P

N = 4
BF = jnp.bfloat16
F32 = jnp.float32


def shift(block, step, first):
    pairs = []
    for y in range(N):
        for x in range(N):
            for col in range(2 * N):
                if first == (col % 2 == 0):
                    to = y * N + (x + step) % N
                else:
                    to = (y + step) % N * N + x
                pairs.append(((y * N + x) * 2 * N + col, to * 2 * N + col))
    return lax.ppermute(block, ("row", "col"), pairs)


def small(block, step):
    return shift(block, step, True)


def big(block, step):
    return shift(block, step, False)


def shift_z(block, step):
    pairs = [(2 * z + core, 2 * ((z + step) % N) + core) for z in range(N) for core in range(2)]
    return lax.ppermute(block, "col", pairs)


def spread_z(block):
    pairs = [(2 * z + core, 2 * ((z + 1 - 2 * core) % N) + core) for z in range(N) for core in range(2)]
    return lax.ppermute(block, "col", pairs)


def swap_core(block):
    pairs = [(col, col ^ 1) for col in range(2 * N)]
    return lax.ppermute(block, "col", pairs)


def tied(*values):
    return lax.optimization_barrier(values)


def dot(a, b, ca, cb):
    return lax.dot_general(a, b, (((ca,), (cb,)), ((), ())), preferred_element_type=F32)


def whole(count):
    return [pl.BlockSpec(memory_space=pltpu.VMEM)] * count


def limits(flops):
    return dict(
        compiler_params=pltpu.CompilerParams(vmem_limit_bytes=24 * 2**20),
        cost_estimate=pl.CostEstimate(flops=flops, bytes_accessed=0, transcendentals=0),
    )


def turn_kernel(source, out):
    out[...] = source[...].T


def turn(block):
    return pl.pallas_call(
        turn_kernel,
        out_shape=jax.ShapeDtypeStruct(block.shape[::-1], block.dtype),
        in_specs=whole(1),
        out_specs=whole(1)[0],
        **limits(0),
    )(block)


def chip(place, i, j):
    turned = place[3] == 1
    y = lax.rem(place[0] + jnp.where(turned, j, i), N)
    x = lax.rem(place[1] + jnp.where(turned, i, j), N)
    return y * N + x, y, x


def arrange_kernel(place, here, got, other, out, sems):
    z, core = place[2], place[3]
    depth = out.shape[2]
    copies = []
    for i in range(N):
        for j in range(N):
            _, y, x = chip(place, i, j)
            ahead = lax.rem(y + N - z, N)
            rows = pl.ds(pl.multiple_of(lax.rem(x, 2) * depth, depth), depth)
            swapped = jnp.where(x // 2 == core, 0, 1)
            near = ahead == jnp.where(core == 0, 3, 1)
            two = ahead == 2
            choices = (
                (here, ahead == 0, swapped),
                (got, jnp.logical_or(near, jnp.logical_and(two, swapped == 0)), jnp.where(two, 2, swapped)),
                (
                    other,
                    jnp.logical_or(
                        ahead == jnp.where(core == 0, 1, 3), jnp.logical_and(two, swapped == 1)
                    ),
                    jnp.where(two, 2, 1 - swapped),
                ),
            )
            for source, chosen, at in choices:
                copy = pltpu.make_async_copy(source.at[at, rows], out.at[i, j], sems.at[i, j])
                pl.when(chosen)(copy.start)
            copies.append(pltpu.make_async_copy(here.at[0, rows], out.at[i, j], sems.at[i, j]))
    for copy in copies:
        copy.wait()


def arrange(place, here, got, other):
    _, rows, count = here.shape
    anywhere = pl.BlockSpec(memory_space=pl.ANY)
    return pl.pallas_call(
        arrange_kernel,
        out_shape=jax.ShapeDtypeStruct((N, N, rows // 2, count), BF),
        in_specs=[pl.BlockSpec(memory_space=pltpu.SMEM), anywhere, anywhere, anywhere],
        out_specs=whole(1)[0],
        scratch_shapes=[pltpu.SemaphoreType.DMA((N, N))],
        **limits(0),
    )(place, here, got, other)


def add_pieces(total, rel, pieces, tokens, columns):
    for (i, h), piece in pieces.items():
        left = rel[i, 2 * h : 2 * h + 2, :, tokens]
        right = piece[:, :, columns]
        term = dot(left.reshape(-1, left.shape[-1]), right.reshape(-1, right.shape[-1]), 0, 0)
        total = term if total is None else total + term
    return total


STEP, WIDE = 128, 768


def sum_kernel(keys, has_first, rel, *refs):
    first = refs[0] if has_first else None
    pieces = dict(zip(keys, refs[has_first : has_first + len(keys)]))
    out = refs[-1]
    for at in range(0, out.shape[0], STEP):
        for left in range(0, out.shape[1], WIDE):
            tokens, columns = slice(at, at + STEP), slice(left, left + WIDE)
            before = first[tokens, columns] if has_first else None
            out[tokens, columns] = add_pieces(before, rel, pieces, tokens, columns)


def add_sums(rel, first, pieces):
    shape = (rel.shape[-1], next(iter(pieces.values())).shape[-1])
    firsts = () if first is None else (first,)
    return pl.pallas_call(
        functools.partial(sum_kernel, tuple(pieces), len(firsts)),
        out_shape=jax.ShapeDtypeStruct(shape, F32),
        in_specs=whole(1 + len(firsts) + len(pieces)),
        out_specs=whole(1)[0],
        **limits(0),
    )(rel, *firsts, *pieces.values())


SCALE = 0.7978845608028654


def late_kernel(keys, rel, sums, cot, *refs):
    pieces = dict(zip(keys, refs))
    activated, grad = refs[len(keys) :]
    for at in range(0, sums.shape[0], STEP):
        for left in range(0, sums.shape[1], WIDE):
            tokens, columns = slice(at, at + STEP), slice(left, left + WIDE)
            pre = add_pieces(sums[tokens, columns], rel, pieces, tokens, columns)
            square = pre * pre
            rise = 0.5 + 0.5 * jnp.tanh(pre * (SCALE + (SCALE * 0.044715) * square))
            activated[tokens, columns] = (pre * rise).astype(BF)
            bend = pre * (2 * SCALE + (6 * SCALE * 0.044715) * square)
            slope = rise + rise * ((1.0 - rise) * bend)
            grad[tokens, columns] = (cot[tokens, columns].astype(F32) * slope).astype(BF)


def finish(rel, sums, cot, pieces):
    out = jax.ShapeDtypeStruct(sums.shape, BF)
    return pl.pallas_call(
        functools.partial(late_kernel, tuple(pieces)),
        out_shape=(out, out),
        in_specs=whole(3 + len(pieces)),
        out_specs=whole(2),
        **limits(0),
    )(rel, sums, cot, *pieces.values())


def near_kernel(i, h, rel, g, got, out):
    for j in range(N):
        total = dot(rel[i, j], g[...], 1, 0)
        if j // 2 == h:
            total += got[j % 2].astype(F32)
        out[j] = total.astype(BF)


def near(i, h, rel, g, got):
    depth, width = rel.shape[2], g.shape[1]
    return pl.pallas_call(
        functools.partial(near_kernel, i, h),
        out_shape=jax.ShapeDtypeStruct((N, depth, width), BF),
        in_specs=whole(3),
        out_specs=whole(1)[0],
        **limits(0),
    )(rel, g, got)


def own_kernel(rel, g, from_up, from_down, kept, *sent):
    for j in (2, 1, 3, 0):
        total = dot(rel[0, j], g[...], 1, 0)
        total += from_up[j].astype(F32) + from_down[j].astype(F32)
        if j == 0:
            kept[...] = total
        else:
            sent[j - 1][...] = total.astype(BF)


def own(rel, g, from_up, from_down):
    depth, width = rel.shape[2], g.shape[1]
    block = jax.ShapeDtypeStruct((depth, width), BF)
    return pl.pallas_call(
        own_kernel,
        out_shape=(jax.ShapeDtypeStruct((depth, width), F32), block, block, block),
        in_specs=whole(4),
        out_specs=tuple(whole(4)),
        **limits(0),
    )(rel, g, from_up, from_down)


def total_kernel(kept, a, b, c, out):
    out[...] = kept[...] + (a[...].astype(F32) + b[...].astype(F32) + c[...].astype(F32))


def add_all(kept, *arrived):
    return pl.pallas_call(
        total_kernel,
        out_shape=jax.ShapeDtypeStruct(kept.shape, F32),
        in_specs=whole(4),
        out_specs=whole(1)[0],
        **limits(0),
    )(kept, *arrived)


def input_kernel(keys, place, g, *refs):
    pieces = dict(zip(keys, refs))
    kept, given, turned = refs[len(keys) :]
    turned[...] = g[...].T
    z, core = place[2], place[3]
    for (i, h), piece in pieces.items():
        depth = piece.shape[1]
        for j in (2 * h, 2 * h + 1):
            total = dot(piece[j % 2], turned[...], 1, 0)
            _, ahead, other = chip(place, i, j)
            to = lax.rem(ahead + N - z, N) * 2 + lax.rem(other, 2)
            rows = pl.ds(pl.multiple_of(to * depth, depth), depth)
            mine = other // 2 == core

            @pl.when(mine)
            def _():
                kept[rows] = total

            @pl.when(jnp.logical_not(mine))
            def _():
                given[rows] = total.astype(given.dtype)


def input_partial(place, g, pieces):
    count, width = g.shape
    rows = N * N * pieces[0, 0].shape[1] // 2
    return pl.pallas_call(
        functools.partial(input_kernel, tuple(pieces)),
        out_shape=(jax.ShapeDtypeStruct((rows, count), F32), jax.ShapeDtypeStruct((rows, count), BF)),
        in_specs=[pl.BlockSpec(memory_space=pltpu.SMEM)] + whole(1 + len(pieces)),
        out_specs=tuple(whole(2)),
        scratch_shapes=[pltpu.VMEM((width, count), BF)],
        **limits(10 * rows * width * count),
    )(place, g, *pieces.values())


def shards(tokens, weight, cotangent):
    row, col = lax.axis_index("row"), lax.axis_index("col")
    place = jnp.stack([row // N, row % N, col // 2, col % 2])
    depth = weight.shape[0]

    up, down, across = small(weight, -1), small(weight, 1), small(weight, 2)
    mine = turn(tokens)
    here = jnp.stack([mine, swap_core(mine)])
    got = spread_z(here)
    up, down, across = tied(up, down, across)
    w = {(0, 0): jnp.stack([weight, up]), (0, 1): jnp.stack([across, down])}
    w[1, 0] = big(w[0, 0], -1)
    w[3, 1] = big(w[0, 1], 1)
    w[1, 1] = big(w[0, 1], -1)
    w[3, 0] = big(w[0, 0], 1)
    got = jnp.concatenate([got, spread_z(got[:1])], axis=0)
    rel = arrange(place, here, got, swap_core(got))
    sums = add_sums(rel, None, {k: w[k] for k in ((0, 0), (0, 1), (1, 0), (3, 1))})
    w[2, 0] = big(w[1, 0], -1)
    w[2, 1] = big(w[3, 1], 1)
    sums = add_sums(rel, sums, {k: w[k] for k in ((1, 1), (3, 0))})
    activated, g = finish(rel, sums, cotangent, {k: w[k] for k in ((2, 0), (2, 1))})

    def far(h):
        block = rel[2, 2 * h : 2 * h + 2].reshape(2 * depth, -1)
        return dot(block, g, 1, 0).astype(BF).reshape(2, depth, -1)

    to_up, to_down = big(far(0), 1), big(far(1), -1)
    kept, given = input_partial(place, g, w)
    to_up, to_down, kept, given = tied(to_up, to_down, kept, given)
    up, down = big(near(1, 0, rel, g, to_up), 1), big(near(3, 1, rel, g, to_down), -1)
    total, sent_1, sent_2, sent_3 = own(rel, g, up, down)
    weight_grad = add_all(total, small(sent_2, 2), small(sent_1, 1), small(sent_3, -1))

    sums = (kept + swap_core(given).astype(F32)).reshape(N, 2 * depth, -1)
    sent = sums.astype(BF)
    z1, z3, z2 = shift_z(sent[1], 1), shift_z(sent[3], -1), shift_z(sent[2], 2)
    input_grad = (sums[0] + z1.astype(F32) + z2.astype(F32) + z3.astype(F32)).T.astype(BF)
    return (activated, input_grad, weight_grad)


def solution(mesh):
    specs = (P("row", "col"), P("row", "col"), P("row", "col"))
    return jax.shard_map(shards, mesh=mesh, in_specs=specs, out_specs=specs, check_vma=False)
```

time: 173 us -> 146 us (0.84)
  between operations: 14.2 us -> 0.83 us
  matrix products: 9.78 us -> 1.54 us
  local copies, waits for them, and re-layouts: 7.5 us -> 4.3 us
  waiting for transfers between devices: 65.3 us -> 67.8 us
  Pallas kernels: 37 us -> 34.7 us
    dot_general x8 -> x2, matrix products: 9.78 us -> 1.54 us  [dot(): lax.dot_general(a, b, (((ca,), (cb,)), ((), ())), preferred_element_type=...]
    ppermute x0 -> x2, waiting for transfers between devices: none -> 7.82 us  [spread_z(): return lax.ppermute(block, 'col', pairs)]
    ppermute x3, waiting for transfers between devices: 7.53 us -> 0.01 us  [shift_z(): return lax.ppermute(block, 'col', pairs)]
    pallas_call x1 -> x5, Pallas kernels: 2.76 us -> 9.56 us  [the longest x1 3.88 us: arrange(): pl.pallas_call(arrange_kernel, out_shape=jax.ShapeDtypeStruct((N, N, rows...]
    ppermute x18 -> x16, starting transfers between devices: 25.5 us -> 20.9 us  [shift(): return lax.ppermute(block, ('row', 'col'), pairs)]
    ppermute x0 -> x2, starting transfers between devices: none -> 3.97 us  [spread_z(): return lax.ppermute(block, 'col', pairs)]
    pallas_call x2, Pallas kernels: 12.1 us -> 8.51 us  [add_sums(): pl.pallas_call(functools.partial(sum_kernel, tuple(pieces), len(firsts)),...]
    unnamed x25 -> x12, local copies, waits for them, and re-layouts: 7.28 us -> 4.11 us
  transfers between devices with their start and end apart: 23 -> 24, of which waited for: 12 -> 13; matrix products, arithmetic and copies ran while one was open for 7% -> 3% of each run, Pallas kernels for 16% -> 20%
where the time goes in v2:
time: 146 us; the launch traced here: 144 us
  waiting for transfers between devices  67.8 us (46%)
  Pallas kernels  34.7 us (24%)
  starting transfers between devices  32.4 us (22%)
  local copies, waits for them, and re-layouts  4.3 us (3%)
  other arithmetic  1.94 us (1%)
  matrix products  1.54 us (1%)
    ppermute x16, waiting for transfers between devices, shift(): return lax.ppermute(block, ('row', 'col'), pairs)  58.7 us
    ppermute x16, starting transfers between devices, shift(): return lax.ppermute(block, ('row', 'col'), pairs)  20.9 us
    pallas_call x1, Pallas kernels, input_partial(): pl.pallas_call(functools.partial(input_kernel, tuple(pieces)), out_shape=...  11.2 us
    pallas_call x2, Pallas kernels, add_sums(): pl.pallas_call(functools.partial(sum_kernel, tuple(pieces), len(firsts)),...  8.51 us
    ppermute x2, waiting for transfers between devices, spread_z(): return lax.ppermute(block, 'col', pairs)  7.82 us
    ppermute x3, starting transfers between devices, shift_z(): return lax.ppermute(block, 'col', pairs)  6.58 us
    pallas_call x1, Pallas kernels, finish(): pl.pallas_call(functools.partial(late_kernel, tuple(pieces)), out_shape=(...  5.24 us
    unnamed x12, local copies, waits for them, and re-layouts  4.11 us
  transfers between devices with their start and end apart: 24, of which 13 were waited for; matrix products, arithmetic and copies ran while one was open for 3% of the time, Pallas kernels for 20%

profile of v2, /device:TPU:6, one launch (start us, length us, event | category | flops | bytes accessed | tf_op | source)
XLA Modules:
  0.0 143.5 jit_solution(14912449669610662182)
XLA Ops:
  1.5 2.4 %collective-permute-start.5 = (bf16[192,1536]{1,0:T(8,128)(2,1)}, bf16[192,1536]{1,0:T(8,128)(2,1)S(1)}, u32[]{:S(2)}, u32[]{:S(2)}) collective-permute-start(bf16[192,1536]{1,0:T(8,128)(2,1)} %param.4), channel_id=1, source_target_pairs={{0,8},{1,33},{2,10},{3,35},{4,12},{5,37},{6,14},{7,39},{8,16},{9,4... | collective-permute-start | bytes 1769480 | tf_op jit(solution)/shard_map/ppermute | solution.py:25
  7.6 2.0 %collective-permute-start.1 = (bf16[2,384,512]{2,1,0:T(8,128)(2,1)S(1)}, bf16[2,384,512]{2,1,0:T(8,128)(2,1)S(1)}, u32[]{:S(2)}, u32[]{:S(2)}) collective-permute-start(bf16[2,384,512]{2,1,0:T(8,128)(2,1)S(1)} %pad_maximum_fusion.2.here), channel_id=1, source_target_pairs={{0,2},{1,7},{2,4},{3,1},{4,6},{5,3},{6,0},{7,5},{8,10},{9,15},{10,... | collective-permute-start | bytes 2359304 | tf_op jit(solution)/shard_map/ppermute | solution.py:43
  9.6 8.7 %collective-permute-done.4 = bf16[192,1536]{1,0:T(8,128)(2,1)S(1)} collective-permute-done((bf16[192,1536]{1,0:T(8,128)(2,1)}, bf16[192,1536]{1,0:T(8,128)(2,1)S(1)}, u32[]{:S(2)}, u32[]{:S(2)}) %collective-permute-start.4) | collective-permute-done | bytes 589856 | tf_op jit(solution)/shard_map/ppermute | solution.py:25
  18.4 1.6 %collective-permute-start.8 = (bf16[2,192,1536]{2,1,0:T(8,128)(2,1)S(1)}, bf16[2,192,1536]{2,1,0:T(8,128)(2,1)}, u32[]{:S(2)}, u32[]{:S(2)}) collective-permute-start(bf16[2,192,1536]{2,1,0:T(8,128)(2,1)S(1)} %pad_maximum_fusion.1.refs_1_), channel_id=1, source_target_pairs={{0,32},{1,9},{2,34},{3,11},{4,36},{5,13},{6,38},{7,15},{8,40},{9,1... | collective-permute-start | bytes 3538952 | tf_op jit(solution)/shard_map/ppermute | solution.py:25
  20.2 1.7 %collective-permute-start.7 = (bf16[2,192,1536]{2,1,0:T(8,128)(2,1)S(1)}, bf16[2,192,1536]{2,1,0:T(8,128)(2,1)}, u32[]{:S(2)}, u32[]{:S(2)}) collective-permute-start(bf16[2,192,1536]{2,1,0:T(8,128)(2,1)S(1)} %pad_maximum_fusion.refs_0_), channel_id=1, source_target_pairs={{0,96},{1,25},{2,98},{3,27},{4,100},{5,29},{6,102},{7,31},{8,104},... | collective-permute-start | bytes 3538952 | tf_op jit(solution)/shard_map/ppermute | solution.py:25
  22.0 2.0 %collective-permute-start.2 = (bf16[1,384,512]{2,1,0:T(8,128)(2,1)S(1)}, bf16[1,384,512]{2,1,0:T(8,128)(2,1)S(1)}, u32[]{:S(2)}, u32[]{:S(2)}) collective-permute-start(bf16[1,384,512]{2,1,0:T(8,128)(2,1)S(1)} %slice.32), channel_id=1, source_target_pairs={{0,2},{1,7},{2,4},{3,1},{4,6},{5,3},{6,0},{7,5},{8,10},{9,15},{10,... | collective-permute-start | bytes 1179656 | tf_op jit(solution)/shard_map/ppermute | solution.py:43
  24.0 7.8 %collective-permute-done.2 = bf16[1,384,512]{2,1,0:T(8,128)(2,1)S(1)} collective-permute-done((bf16[1,384,512]{2,1,0:T(8,128)(2,1)S(1)}, bf16[1,384,512]{2,1,0:T(8,128)(2,1)S(1)}, u32[]{:S(2)}, u32[]{:S(2)}) %collective-permute-start.2) | collective-permute-done | bytes 393248 | tf_op jit(solution)/shard_map/ppermute | solution.py:43
  32.0 1.9 %collective-permute-start.9 = (bf16[2,192,1536]{2,1,0:T(8,128)(2,1)S(1)}, bf16[2,192,1536]{2,1,0:T(8,128)(2,1)}, u32[]{:S(2)}, u32[]{:S(2)}) collective-permute-start(bf16[2,192,1536]{2,1,0:T(8,128)(2,1)S(1)} %pad_maximum_fusion.1.refs_1_), channel_id=1, source_target_pairs={{0,96},{1,25},{2,98},{3,27},{4,100},{5,29},{6,102},{7,31},{8,104},... | collective-permute-start | bytes 3538952 | tf_op jit(solution)/shard_map/ppermute | solution.py:25
  34.1 2.0 %collective-permute-done.8.refs_3_ = bf16[2,192,1536]{2,1,0:T(8,128)(2,1)} collective-permute-done((bf16[2,192,1536]{2,1,0:T(8,128)(2,1)S(1)}, bf16[2,192,1536]{2,1,0:T(8,128)(2,1)}, u32[]{:S(2)}, u32[]{:S(2)}) %collective-permute-start.8) | collective-permute-done | bytes 1179680 | tf_op jit(solution)/shard_map/ppermute | solution.py:25
  36.6 2.9 %collective-permute-start.11 = (bf16[2,192,1536]{2,1,0:T(8,128)(2,1)}, bf16[2,192,1536]{2,1,0:T(8,128)(2,1)}, u32[]{:S(2)}, u32[]{:S(2)}) collective-permute-start(bf16[2,192,1536]{2,1,0:T(8,128)(2,1)} %collective-permute-done.7.refs_2_), channel_id=1, source_target_pairs={{0,96},{1,25},{2,98},{3,27},{4,100},{5,29},{6,102},{7,31},{8,104},... | collective-permute-start | bytes 3538952 | tf_op jit(solution)/shard_map/ppermute | solution.py:25
  40.7 3.9 %shard_map.59.rel = bf16[4,4,192,512]{3,2,1,0:T(8,128)(2,1)S(1)} custom-call(s32[4]{0:T(128)S(1)} %pad_add_fusion.place, bf16[2,384,512]{2,1,0:T(8,128)(2,1)S(1)} %copy-done.1, bf16[3,384,512]{2,1,0:T(8,128)(2,1)S(1)} %constant_dynamic-update-slice_fusion.got, bf16[3,384,512]{2,1,0:T(8,128)(2,1)} %collective-permute-done.3.other), custom_call_target="tpu_custom_call" | custom-call | tf_op jit(solution)/shard_map/pallas_call | solution.py:125
  44.6 5.1 %shard_map.60.refs_0_ = f32[512,1536]{1,0:T(8,128)S(1)} custom-call(bf16[4,4,192,512]{3,2,1,0:T(8,128)(2,1)S(1)} %shard_map.59.rel, bf16[2,192,1536]{2,1,0:T(8,128)(2,1)S(1)} %pad_maximum_fusion.refs_0_, bf16[2,192,1536]{2,1,0:T(8,128)(2,1)S(1)} %pad_maximum_fusion.1.refs_1_, bf16[2,192,1536]{2,1,0:T(8,128)(2,1)} %collective-permute-done.7.refs_2_, ...), custom_call_target="tpu_custom_call" | custom-call | tf_op jit(solution)/shard_map/pallas_call | solution.py:161
  49.7 1.7 %collective-permute-done.10.refs_2_.refs_5_ = bf16[2,192,1536]{2,1,0:T(8,128)(2,1)} collective-permute-done((bf16[2,192,1536]{2,1,0:T(8,128)(2,1)S(1)}, bf16[2,192,1536]{2,1,0:T(8,128)(2,1)}, u32[]{:S(2)}, u32[]{:S(2)}) %collective-permute-start.10) | collective-permute-done | bytes 1179680 | tf_op jit(solution)/shard_map/ppermute | solution.py:25
  51.4 3.4 %shard_map.61.sums = f32[512,1536]{1,0:T(8,128)S(1)} custom-call(bf16[4,4,192,512]{3,2,1,0:T(8,128)(2,1)S(1)} %shard_map.59.rel, f32[512,1536]{1,0:T(8,128)S(1)} %shard_map.60.refs_0_, bf16[2,192,1536]{2,1,0:T(8,128)(2,1)} %collective-permute-done.9.refs_1_.refs_4_, bf16[2,192,1536]{2,1,0:T(8,128)(2,1)} %collective-permute-done.10.refs_2_.refs_5_), custom_call_target="tpu_custom_call" | custom-call | tf_op jit(solution)/shard_map/pallas_call | solution.py:161
  54.9 9.1 %collective-permute-done.12.refs_1_.refs_7_ = bf16[2,192,1536]{2,1,0:T(8,128)(2,1)} collective-permute-done((bf16[2,192,1536]{2,1,0:T(8,128)(2,1)}, bf16[2,192,1536]{2,1,0:T(8,128)(2,1)}, u32[]{:S(2)}, u32[]{:S(2)}) %collective-permute-start.12) | collective-permute-done | bytes 1179680 | tf_op jit(solution)/shard_map/ppermute | solution.py:25
  64.0 5.2 %shard_map.62 = (bf16[512,1536]{1,0:T(8,128)(2,1)}, bf16[512,1536]{1,0:T(8,128)(2,1)S(1)}) custom-call(bf16[4,4,192,512]{3,2,1,0:T(8,128)(2,1)S(1)} %shard_map.59.rel, f32[512,1536]{1,0:T(8,128)S(1)} %shard_map.61.sums, bf16[512,1536]{1,0:T(8,128)(2,1)S(1)} %copy-done.2, bf16[2,192,1536]{2,1,0:T(8,128)(2,1)} %collective-permute-done.11.refs_0_.refs_6_, ...), custom_call_target="tpu_custom_call" | custom-call | tf_op jit(solution)/shard_map/pallas_call | solution.py:190
  71.6 1.4 collective-permute-start.13
  73.0 11.2 %shard_map.63 = (f32[1536,512]{1,0:T(8,128)S(1)}, bf16[1536,512]{1,0:T(8,128)(2,1)S(1)}) custom-call(s32[4]{0:T(128)S(1)} %pad_add_fusion.place, bf16[512,1536]{1,0:T(8,128)(2,1)S(1)} %get-tuple-element.22.g, bf16[2,192,1536]{2,1,0:T(8,128)(2,1)S(1)} %pad_maximum_fusion.refs_0_, bf16[2,192,1536]{2,1,0:T(8,128)(2,1)S(1)} %pad_maximum_fusion.1.refs_1_, ...), custom_call_target="tpu_custom_call" | custom-call | flops 12079595520 | tf_op jit(solution)/shard_map/pallas_call | solution.py:280
  84.2 2.1 %collective-permute-done.14.got = bf16[2,192,1536]{2,1,0:T(8,128)(2,1)S(1)} collective-permute-done((bf16[2,192,1536]{2,1,0:T(8,128)(2,1)S(1)}, bf16[2,192,1536]{2,1,0:T(8,128)(2,1)S(1)}, u32[]{:S(2)}, u32[]{:S(2)}) %collective-permute-start.14) | collective-permute-done | bytes 1179680 | tf_op jit(solution)/shard_map/ppermute | solution.py:25
  86.3 2.8 %collective-permute-done.13.got = bf16[2,192,1536]{2,1,0:T(8,128)(2,1)S(1)} collective-permute-done((bf16[2,192,1536]{2,1,0:T(8,128)(2,1)S(1)}, bf16[2,192,1536]{2,1,0:T(8,128)(2,1)S(1)}, u32[]{:S(2)}, u32[]{:S(2)}) %collective-permute-start.13) | collective-permute-done | bytes 1179680 | tf_op jit(solution)/shard_map/ppermute | solution.py:25
  89.1 1.4 shard_map.65
  90.6 1.4 shard_map.64
  92.0 2.1 %collective-permute-start.19 = (bf16[4,192,1536]{2,1,0:T(8,128)(2,1)S(1)}, bf16[4,192,1536]{2,1,0:T(8,128)(2,1)S(1)}, u32[]{:S(2)}, u32[]{:S(2)}) collective-permute-start(bf16[4,192,1536]{2,1,0:T(8,128)(2,1)S(1)} %shard_map.64), channel_id=1, source_target_pairs={{0,32},{1,9},{2,34},{3,11},{4,36},{5,13},{6,38},{7,15},{8,40},{9,1... | collective-permute-start | bytes 7077896 | tf_op jit(solution)/shard_map/ppermute | solution.py:25
  94.8 2.0 %collective-permute-start.16 = (bf16[384,512]{1,0:T(8,128)(2,1)S(1)}, bf16[384,512]{1,0:T(8,128)(2,1)S(1)}, u32[]{:S(2)}, u32[]{:S(2)}) collective-permute-start(bf16[384,512]{1,0:T(8,128)(2,1)S(1)} %get-tuple-element.40), channel_id=1, source_target_pairs={{0,2},{1,3},{2,4},{3,5},{4,6},{5,7},{6,0},{7,1},{8,10},{9,11},{10,... | collective-permute-start | bytes 1179656 | tf_op jit(solution)/shard_map/ppermute | solution.py:38
  96.8 3.6 %collective-permute-start.17 = (bf16[384,512]{1,0:T(8,128)(2,1)S(1)}, bf16[384,512]{1,0:T(8,128)(2,1)S(1)}, u32[]{:S(2)}, u32[]{:S(2)}) collective-permute-start(bf16[384,512]{1,0:T(8,128)(2,1)S(1)} %get-tuple-element.42), channel_id=1, source_target_pairs={{0,4},{1,5},{2,6},{3,7},{4,0},{5,1},{6,2},{7,3},{8,12},{9,13},{10,... | collective-permute-start | bytes 1179656 | tf_op jit(solution)/shard_map/ppermute | solution.py:38
  101.4 18.1 %collective-permute-done.20.from_down = bf16[4,192,1536]{2,1,0:T(8,128)(2,1)S(1)} collective-permute-done((bf16[4,192,1536]{2,1,0:T(8,128)(2,1)S(1)}, bf16[4,192,1536]{2,1,0:T(8,128)(2,1)S(1)}, u32[]{:S(2)}, u32[]{:S(2)}) %collective-permute-start.20) | collective-permute-done | bytes 2359328 | tf_op jit(solution)/shard_map/ppermute | solution.py:25
  119.4 2.7 %collective-permute-done.19.from_up = bf16[4,192,1536]{2,1,0:T(8,128)(2,1)S(1)} collective-permute-done((bf16[4,192,1536]{2,1,0:T(8,128)(2,1)S(1)}, bf16[4,192,1536]{2,1,0:T(8,128)(2,1)S(1)}, u32[]{:S(2)}, u32[]{:S(2)}) %collective-permute-start.19) | collective-permute-done | bytes 2359328 | tf_op jit(solution)/shard_map/ppermute | solution.py:25
  122.1 1.6 %shard_map.66 = (f32[192,1536]{1,0:T(8,128)S(1)}, bf16[192,1536]{1,0:T(8,128)(2,1)}, bf16[192,1536]{1,0:T(8,128)(2,1)}, bf16[192,1536]{1,0:T(8,128)(2,1)S(1)}) custom-call(bf16[4,4,192,512]{3,2,1,0:T(8,128)(2,1)S(1)} %shard_map.59.rel, bf16[512,1536]{1,0:T(8,128)(2,1)S(1)} %get-tuple-element.22.g, bf16[4,192,1536]{2,1,0:T(8,128)(2,1)S(1)} %collective-permute-done.19.from_up, ...), custom_call_target="tpu_custom_call" | custom-call | tf_op jit(solution)/shard_map/pallas_call | solution.py:231
  123.7 2.3 %collective-permute-start.21 = (bf16[192,1536]{1,0:T(8,128)(2,1)}, bf16[192,1536]{1,0:T(8,128)(2,1)S(1)}, u32[]{:S(2)}, u32[]{:S(2)}) collective-permute-start(bf16[192,1536]{1,0:T(8,128)(2,1)} %get-tuple-element.30), channel_id=1, source_target_pairs={{0,16},{1,65},{2,18},{3,67},{4,20},{5,69},{6,22},{7,71},{8,24},{9,... | collective-permute-start | bytes 1769480 | tf_op jit(solution)/shard_map/ppermute | solution.py:25
  129.1 1.9 %copy.6 = bf16[512,384]{1,0:T(8,128)(2,1)} copy(bf16[512,384]{0,1:T(8,128)(2,1)} %fusion.3) | data formatting | bytes 786432
  131.0 4.5 %collective-permute-done.21.a = bf16[192,1536]{1,0:T(8,128)(2,1)S(1)} collective-permute-done((bf16[192,1536]{1,0:T(8,128)(2,1)}, bf16[192,1536]{1,0:T(8,128)(2,1)S(1)}, u32[]{:S(2)}, u32[]{:S(2)}) %collective-permute-start.21) | collective-permute-done | bytes 589856 | tf_op jit(solution)/shard_map/ppermute | solution.py:25
  135.4 6.8 %collective-permute-done.22.b = bf16[192,1536]{1,0:T(8,128)(2,1)S(1)} collective-permute-done((bf16[192,1536]{1,0:T(8,128)(2,1)}, bf16[192,1536]{1,0:T(8,128)(2,1)S(1)}, u32[]{:S(2)}, u32[]{:S(2)}) %collective-permute-start.22) | collective-permute-done | bytes 589856 | tf_op jit(solution)/shard_map/ppermute | solution.py:25
  (50 shorter events, 15.4 us)
Async XLA Ops:
  0.6 17.7 %collective-permute-start.4 = (bf16[192,1536]{1,0:T(8,128)(2,1)}, bf16[192,1536]{1,0:T(8,128)(2,1)S(1)}, u32[]{:S(2)}, u32[]{:S(2)}) collective-permute-start(bf16[192,1536]{1,0:T(8,128)(2,1)} %param.4), channel_id=1, source_target_pairs={{0,24},{1,97},{2,26},{3,99},{4,28},{5,101},{6,30},{7,103},{8,0},{9... | collective-permute-start | bytes 1769480 | tf_op jit(solution)/shard_map/ppermute | solution.py:25
  1.5 16.8 %collective-permute-start.5 = (bf16[192,1536]{1,0:T(8,128)(2,1)}, bf16[192,1536]{1,0:T(8,128)(2,1)S(1)}, u32[]{:S(2)}, u32[]{:S(2)}) collective-permute-start(bf16[192,1536]{1,0:T(8,128)(2,1)} %param.4), channel_id=1, source_target_pairs={{0,8},{1,33},{2,10},{3,35},{4,12},{5,37},{6,14},{7,39},{8,16},{9,4... | collective-permute-start | bytes 1769480 | tf_op jit(solution)/shard_map/ppermute | solution.py:25
  3.9 14.4 %collective-permute-start.6 = (bf16[192,1536]{1,0:T(8,128)(2,1)}, bf16[192,1536]{1,0:T(8,128)(2,1)S(1)}, u32[]{:S(2)}, u32[]{:S(2)}) collective-permute-start(bf16[192,1536]{1,0:T(8,128)(2,1)} %param.4), channel_id=1, source_target_pairs={{0,16},{1,65},{2,18},{3,67},{4,20},{5,69},{6,22},{7,71},{8,24},{9,... | collective-permute-start | bytes 1769480 | tf_op jit(solution)/shard_map/ppermute | solution.py:25
  4.1 1.0 copy-start.3
  5.3 2.2 %collective-permute-start = (bf16[384,512]{1,0:T(8,128)(2,1)S(1)}, bf16[384,512]{1,0:T(8,128)(2,1)S(1)}, u32[]{:S(2)}, u32[]{:S(2)}) collective-permute-start(bf16[384,512]{1,0:T(8,128)(2,1)S(1)} %shard_map.58), channel_id=1, source_target_pairs={{0,1},{1,0},{2,3},{3,2},{4,5},{5,4},{6,7},{7,6},{8,9},{9,8},{10,11... | collective-permute-start | bytes 1179656 | tf_op jit(solution)/shard_map/ppermute | solution.py:48
  7.6 12.6 %copy-start = (bf16[2,384,512]{2,1,0:T(8,128)(2,1)}, bf16[2,384,512]{2,1,0:T(8,128)(2,1)S(1)}, u32[]{:S(2)}) copy-start(bf16[2,384,512]{2,1,0:T(8,128)(2,1)S(1)} %pad_maximum_fusion.2.here) | copy-start | bytes 2359300
  7.6 12.5 %copy-start.4 = (bf16[192,1536]{1,0:T(8,128)(2,1)S(1)}, bf16[192,1536]{1,0:T(8,128)(2,1)}, u32[]{:S(2)}) copy-start(bf16[192,1536]{1,0:T(8,128)(2,1)} %param.4) | copy-start | bytes 1769476
  7.6 14.3 %collective-permute-start.1 = (bf16[2,384,512]{2,1,0:T(8,128)(2,1)S(1)}, bf16[2,384,512]{2,1,0:T(8,128)(2,1)S(1)}, u32[]{:S(2)}, u32[]{:S(2)}) collective-permute-start(bf16[2,384,512]{2,1,0:T(8,128)(2,1)S(1)} %pad_maximum_fusion.2.here), channel_id=1, source_target_pairs={{0,2},{1,7},{2,4},{3,1},{4,6},{5,3},{6,0},{7,5},{8,10},{9,15},{10,... | collective-permute-start | bytes 2359304 | tf_op jit(solution)/shard_map/ppermute | solution.py:43
  18.4 17.6 %collective-permute-start.8 = (bf16[2,192,1536]{2,1,0:T(8,128)(2,1)S(1)}, bf16[2,192,1536]{2,1,0:T(8,128)(2,1)}, u32[]{:S(2)}, u32[]{:S(2)}) collective-permute-start(bf16[2,192,1536]{2,1,0:T(8,128)(2,1)S(1)} %pad_maximum_fusion.1.refs_1_), channel_id=1, source_target_pairs={{0,32},{1,9},{2,34},{3,11},{4,36},{5,13},{6,38},{7,15},{8,40},{9,1... | collective-permute-start | bytes 3538952 | tf_op jit(solution)/shard_map/ppermute | solution.py:25
  20.2 16.4 %collective-permute-start.7 = (bf16[2,192,1536]{2,1,0:T(8,128)(2,1)S(1)}, bf16[2,192,1536]{2,1,0:T(8,128)(2,1)}, u32[]{:S(2)}, u32[]{:S(2)}) collective-permute-start(bf16[2,192,1536]{2,1,0:T(8,128)(2,1)S(1)} %pad_maximum_fusion.refs_0_), channel_id=1, source_target_pairs={{0,96},{1,25},{2,98},{3,27},{4,100},{5,29},{6,102},{7,31},{8,104},... | collective-permute-start | bytes 3538952 | tf_op jit(solution)/shard_map/ppermute | solution.py:25
  22.0 9.9 %collective-permute-start.2 = (bf16[1,384,512]{2,1,0:T(8,128)(2,1)S(1)}, bf16[1,384,512]{2,1,0:T(8,128)(2,1)S(1)}, u32[]{:S(2)}, u32[]{:S(2)}) collective-permute-start(bf16[1,384,512]{2,1,0:T(8,128)(2,1)S(1)} %slice.32), channel_id=1, source_target_pairs={{0,2},{1,7},{2,4},{3,1},{4,6},{5,3},{6,0},{7,5},{8,10},{9,15},{10,... | collective-permute-start | bytes 1179656 | tf_op jit(solution)/shard_map/ppermute | solution.py:43
  31.9 7.7 %collective-permute-start.3 = (bf16[3,384,512]{2,1,0:T(8,128)(2,1)S(1)}, bf16[3,384,512]{2,1,0:T(8,128)(2,1)}, u32[]{:S(2)}, u32[]{:S(2)}) collective-permute-start(bf16[3,384,512]{2,1,0:T(8,128)(2,1)S(1)} %constant_dynamic-update-slice_fusion.got), channel_id=1, source_target_pairs={{0,1},{1,0},{2,3},{3,2},{4,5},{5,4},{6,7},{7,6},{8,9},{9,8},{10,11... | collective-permute-start | bytes 3538952 | tf_op jit(solution)/shard_map/ppermute | solution.py:48
  32.0 17.7 %collective-permute-start.9 = (bf16[2,192,1536]{2,1,0:T(8,128)(2,1)S(1)}, bf16[2,192,1536]{2,1,0:T(8,128)(2,1)}, u32[]{:S(2)}, u32[]{:S(2)}) collective-permute-start(bf16[2,192,1536]{2,1,0:T(8,128)(2,1)S(1)} %pad_maximum_fusion.1.refs_1_), channel_id=1, source_target_pairs={{0,96},{1,25},{2,98},{3,27},{4,100},{5,29},{6,102},{7,31},{8,104},... | collective-permute-start | bytes 3538952 | tf_op jit(solution)/shard_map/ppermute | solution.py:25
  33.8 17.5 %collective-permute-start.10 = (bf16[2,192,1536]{2,1,0:T(8,128)(2,1)S(1)}, bf16[2,192,1536]{2,1,0:T(8,128)(2,1)}, u32[]{:S(2)}, u32[]{:S(2)}) collective-permute-start(bf16[2,192,1536]{2,1,0:T(8,128)(2,1)S(1)} %pad_maximum_fusion.refs_0_), channel_id=1, source_target_pairs={{0,32},{1,9},{2,34},{3,11},{4,36},{5,13},{6,38},{7,15},{8,40},{9,1... | collective-permute-start | bytes 3538952 | tf_op jit(solution)/shard_map/ppermute | solution.py:25
  36.0 28.0 %collective-permute-start.12 = (bf16[2,192,1536]{2,1,0:T(8,128)(2,1)}, bf16[2,192,1536]{2,1,0:T(8,128)(2,1)}, u32[]{:S(2)}, u32[]{:S(2)}) collective-permute-start(bf16[2,192,1536]{2,1,0:T(8,128)(2,1)} %collective-permute-done.8.refs_3_), channel_id=1, source_target_pairs={{0,32},{1,9},{2,34},{3,11},{4,36},{5,13},{6,38},{7,15},{8,40},{9,1... | collective-permute-start | bytes 3538952 | tf_op jit(solution)/shard_map/ppermute | solution.py:25
  36.6 27.4 %collective-permute-start.11 = (bf16[2,192,1536]{2,1,0:T(8,128)(2,1)}, bf16[2,192,1536]{2,1,0:T(8,128)(2,1)}, u32[]{:S(2)}, u32[]{:S(2)}) collective-permute-start(bf16[2,192,1536]{2,1,0:T(8,128)(2,1)} %collective-permute-done.7.refs_2_), channel_id=1, source_target_pairs={{0,96},{1,25},{2,98},{3,27},{4,100},{5,29},{6,102},{7,31},{8,104},... | collective-permute-start | bytes 3538952 | tf_op jit(solution)/shard_map/ppermute | solution.py:25
  39.5 1.1 copy-start.1
  54.8 9.2 %copy-start.2 = (bf16[512,1536]{1,0:T(8,128)(2,1)S(1)}, bf16[512,1536]{1,0:T(8,128)(2,1)}, u32[]{:S(2)}) copy-start(bf16[512,1536]{1,0:T(8,128)(2,1)} %cot.1) | copy-start | bytes 4718596
  70.0 16.3 %collective-permute-start.14 = (bf16[2,192,1536]{2,1,0:T(8,128)(2,1)S(1)}, bf16[2,192,1536]{2,1,0:T(8,128)(2,1)S(1)}, u32[]{:S(2)}, u32[]{:S(2)}) collective-permute-start(bf16[2,192,1536]{2,1,0:T(8,128)(2,1)S(1)} %bitcast.28), channel_id=1, source_target_pairs={{0,96},{1,25},{2,98},{3,27},{4,100},{5,29},{6,102},{7,31},{8,104},... | collective-permute-start | bytes 3538952 | tf_op jit(solution)/shard_map/ppermute | solution.py:25
  71.6 17.5 %collective-permute-start.13 = (bf16[2,192,1536]{2,1,0:T(8,128)(2,1)S(1)}, bf16[2,192,1536]{2,1,0:T(8,128)(2,1)S(1)}, u32[]{:S(2)}, u32[]{:S(2)}) collective-permute-start(bf16[2,192,1536]{2,1,0:T(8,128)(2,1)S(1)} %bitcast.29), channel_id=1, source_target_pairs={{0,32},{1,9},{2,34},{3,11},{4,36},{5,13},{6,38},{7,15},{8,40},{9,1... | collective-permute-start | bytes 3538952 | tf_op jit(solution)/shard_map/ppermute | solution.py:25
  89.1 5.0 %collective-permute-start.15 = (bf16[1536,512]{1,0:T(8,128)(2,1)S(1)}, bf16[1536,512]{1,0:T(8,128)(2,1)S(1)}, u32[]{:S(2)}, u32[]{:S(2)}) collective-permute-start(bf16[1536,512]{1,0:T(8,128)(2,1)S(1)} %get-tuple-element.26), channel_id=1, source_target_pairs={{0,1},{1,0},{2,3},{3,2},{4,5},{5,4},{6,7},{7,6},{8,9},{9,8},{10,11... | collective-permute-start | bytes 4718600 | tf_op jit(solution)/shard_map/ppermute | solution.py:48
  90.5 28.9 %collective-permute-start.20 = (bf16[4,192,1536]{2,1,0:T(8,128)(2,1)S(1)}, bf16[4,192,1536]{2,1,0:T(8,128)(2,1)S(1)}, u32[]{:S(2)}, u32[]{:S(2)}) collective-permute-start(bf16[4,192,1536]{2,1,0:T(8,128)(2,1)S(1)} %shard_map.65), channel_id=1, source_target_pairs={{0,96},{1,25},{2,98},{3,27},{4,100},{5,29},{6,102},{7,31},{8,104},... | collective-permute-start | bytes 7077896 | tf_op jit(solution)/shard_map/ppermute | solution.py:25
  92.0 30.1 %collective-permute-start.19 = (bf16[4,192,1536]{2,1,0:T(8,128)(2,1)S(1)}, bf16[4,192,1536]{2,1,0:T(8,128)(2,1)S(1)}, u32[]{:S(2)}, u32[]{:S(2)}) collective-permute-start(bf16[4,192,1536]{2,1,0:T(8,128)(2,1)S(1)} %shard_map.64), channel_id=1, source_target_pairs={{0,32},{1,9},{2,34},{3,11},{4,36},{5,13},{6,38},{7,15},{8,40},{9,1... | collective-permute-start | bytes 7077896 | tf_op jit(solution)/shard_map/ppermute | solution.py:25
  94.8 32.5 %collective-permute-start.16 = (bf16[384,512]{1,0:T(8,128)(2,1)S(1)}, bf16[384,512]{1,0:T(8,128)(2,1)S(1)}, u32[]{:S(2)}, u32[]{:S(2)}) collective-permute-start(bf16[384,512]{1,0:T(8,128)(2,1)S(1)} %get-tuple-element.40), channel_id=1, source_target_pairs={{0,2},{1,3},{2,4},{3,5},{4,6},{5,7},{6,0},{7,1},{8,10},{9,11},{10,... | collective-permute-start | bytes 1179656 | tf_op jit(solution)/shard_map/ppermute | solution.py:38
  96.8 31.3 %collective-permute-start.17 = (bf16[384,512]{1,0:T(8,128)(2,1)S(1)}, bf16[384,512]{1,0:T(8,128)(2,1)S(1)}, u32[]{:S(2)}, u32[]{:S(2)}) collective-permute-start(bf16[384,512]{1,0:T(8,128)(2,1)S(1)} %get-tuple-element.42), channel_id=1, source_target_pairs={{0,4},{1,5},{2,6},{3,7},{4,0},{5,1},{6,2},{7,3},{8,12},{9,13},{10,... | collective-permute-start | bytes 1179656 | tf_op jit(solution)/shard_map/ppermute | solution.py:38
  100.3 27.8 %collective-permute-start.18 = (bf16[384,512]{1,0:T(8,128)(2,1)S(1)}, bf16[384,512]{1,0:T(8,128)(2,1)S(1)}, u32[]{:S(2)}, u32[]{:S(2)}) collective-permute-start(bf16[384,512]{1,0:T(8,128)(2,1)S(1)} %get-tuple-element.41), channel_id=1, source_target_pairs={{0,6},{1,7},{2,0},{3,1},{4,2},{5,3},{6,4},{7,5},{8,14},{9,15},{10,... | collective-permute-start | bytes 1179656 | tf_op jit(solution)/shard_map/ppermute | solution.py:38
  123.7 11.7 %collective-permute-start.21 = (bf16[192,1536]{1,0:T(8,128)(2,1)}, bf16[192,1536]{1,0:T(8,128)(2,1)S(1)}, u32[]{:S(2)}, u32[]{:S(2)}) collective-permute-start(bf16[192,1536]{1,0:T(8,128)(2,1)} %get-tuple-element.30), channel_id=1, source_target_pairs={{0,16},{1,65},{2,18},{3,67},{4,20},{5,69},{6,22},{7,71},{8,24},{9,... | collective-permute-start | bytes 1769480 | tf_op jit(solution)/shard_map/ppermute | solution.py:25
  126.1 16.2 %collective-permute-start.22 = (bf16[192,1536]{1,0:T(8,128)(2,1)}, bf16[192,1536]{1,0:T(8,128)(2,1)S(1)}, u32[]{:S(2)}, u32[]{:S(2)}) collective-permute-start(bf16[192,1536]{1,0:T(8,128)(2,1)} %get-tuple-element.31), channel_id=1, source_target_pairs={{0,8},{1,33},{2,10},{3,35},{4,12},{5,37},{6,14},{7,39},{8,16},{9,4... | collective-permute-start | bytes 1769480 | tf_op jit(solution)/shard_map/ppermute | solution.py:25
  127.3 15.0 %collective-permute-start.23 = (bf16[192,1536]{1,0:T(8,128)(2,1)S(1)}, bf16[192,1536]{1,0:T(8,128)(2,1)S(1)}, u32[]{:S(2)}, u32[]{:S(2)}) collective-permute-start(bf16[192,1536]{1,0:T(8,128)(2,1)S(1)} %get-tuple-element.32), channel_id=1, source_target_pairs={{0,24},{1,97},{2,26},{3,99},{4,28},{5,101},{6,30},{7,103},{8,0},{9... | collective-permute-start | bytes 1769480 | tf_op jit(solution)/shard_map/ppermute | solution.py:25

commit v3 on v2

--- a/solution.py
+++ b/solution.py
@@ -172,69 +172,50 @@
 
 def late_kernel(keys, rel, sums, cot, *refs):
     pieces = dict(zip(keys, refs))
-    activated, grad = refs[len(keys) :]
+    held, grad = refs[len(keys) :]
     for at in range(0, sums.shape[0], STEP):
         for left in range(0, sums.shape[1], WIDE):
             tokens, columns = slice(at, at + STEP), slice(left, left + WIDE)
             pre = add_pieces(sums[tokens, columns], rel, pieces, tokens, columns)
             square = pre * pre
             rise = 0.5 + 0.5 * jnp.tanh(pre * (SCALE + (SCALE * 0.044715) * square))
-            activated[tokens, columns] = (pre * rise).astype(BF)
+            held[tokens, columns] = pre * rise
             bend = pre * (2 * SCALE + (6 * SCALE * 0.044715) * square)
             slope = rise + rise * ((1.0 - rise) * bend)
             grad[tokens, columns] = (cot[tokens, columns].astype(F32) * slope).astype(BF)
 
 
 def finish(rel, sums, cot, pieces):
-    out = jax.ShapeDtypeStruct(sums.shape, BF)
     return pl.pallas_call(
         functools.partial(late_kernel, tuple(pieces)),
-        out_shape=(out, out),
+        out_shape=(jax.ShapeDtypeStruct(sums.shape, F32), jax.ShapeDtypeStruct(sums.shape, BF)),
         in_specs=whole(3 + len(pieces)),
-        out_specs=whole(2),
+        out_specs=tuple(whole(2)),
         **limits(0),
     )(rel, sums, cot, *pieces.values())
 
 
-def near_kernel(i, h, rel, g, got, out):
-    for j in range(N):
-        total = dot(rel[i, j], g[...], 1, 0)
-        if j // 2 == h:
-            total += got[j % 2].astype(F32)
-        out[j] = total.astype(BF)
-
-
-def near(i, h, rel, g, got):
-    depth, width = rel.shape[2], g.shape[1]
-    return pl.pallas_call(
-        functools.partial(near_kernel, i, h),
-        out_shape=jax.ShapeDtypeStruct((N, depth, width), BF),
-        in_specs=whole(3),
-        out_specs=whole(1)[0],
-        **limits(0),
-    )(rel, g, got)
-
-
-def own_kernel(rel, g, from_up, from_down, kept, *sent):
+def own_kernel(rel, g, up_low, up_high, down_low, down_high, kept, *sent):
     for j in (2, 1, 3, 0):
         total = dot(rel[0, j], g[...], 1, 0)
-        total += from_up[j].astype(F32) + from_down[j].astype(F32)
+        for low, high in ((up_low, up_high), (down_low, down_high)):
+            total += (low if j < 2 else high)[j % 2].astype(F32)
         if j == 0:
             kept[...] = total
         else:
             sent[j - 1][...] = total.astype(BF)
 
 
-def own(rel, g, from_up, from_down):
+def own(rel, g, *arrived):
     depth, width = rel.shape[2], g.shape[1]
     block = jax.ShapeDtypeStruct((depth, width), BF)
     return pl.pallas_call(
         own_kernel,
         out_shape=(jax.ShapeDtypeStruct((depth, width), F32), block, block, block),
-        in_specs=whole(4),
+        in_specs=whole(6),
         out_specs=tuple(whole(4)),
         **limits(0),
-    )(rel, g, from_up, from_down)
+    )(rel, g, *arrived)
 
 
 def total_kernel(kept, a, b, c, out):
@@ -245,6 +226,21 @@
     return pl.pallas_call(
         total_kernel,
         out_shape=jax.ShapeDtypeStruct(kept.shape, F32),
+        in_specs=whole(4),
+        out_specs=whole(1)[0],
+        **limits(0),
+    )(kept, *arrived)
+
+
+def join_kernel(kept, a, b, c, out):
+    total = kept[...] + (a[...].astype(F32) + b[...].astype(F32) + c[...].astype(F32))
+    out[...] = total.astype(BF).T
+
+
+def join(kept, *arrived):
+    return pl.pallas_call(
+        join_kernel,
+        out_shape=jax.ShapeDtypeStruct(kept.shape[::-1], BF),
         in_specs=whole(4),
         out_specs=whole(1)[0],
         **limits(0),
@@ -283,7 +279,7 @@
         in_specs=[pl.BlockSpec(memory_space=pltpu.SMEM)] + whole(1 + len(pieces)),
         out_specs=tuple(whole(2)),
         scratch_shapes=[pltpu.VMEM((width, count), BF)],
-        **limits(10 * rows * width * count),
+        **limits(0),
     )(place, g, *pieces.values())
 
 
@@ -308,23 +304,28 @@
     w[2, 0] = big(w[1, 0], -1)
     w[2, 1] = big(w[3, 1], 1)
     sums = add_sums(rel, sums, {k: w[k] for k in ((1, 1), (3, 0))})
-    activated, g = finish(rel, sums, cotangent, {k: w[k] for k in ((2, 0), (2, 1))})
-
-    def far(h):
-        block = rel[2, 2 * h : 2 * h + 2].reshape(2 * depth, -1)
-        return dot(block, g, 1, 0).astype(BF).reshape(2, depth, -1)
-
-    to_up, to_down = big(far(0), 1), big(far(1), -1)
+    held, g = finish(rel, sums, cotangent, {k: w[k] for k in ((2, 0), (2, 1))})
+
+    def part(i, h):
+        block = rel[i, 2 * h : 2 * h + 2].reshape(2 * depth, -1)
+        return dot(block, g, 1, 0).reshape(2, depth, -1)
+
+    to_up, to_down = big(part(2, 0).astype(BF), 1), big(part(2, 1).astype(BF), -1)
+    up_high, down_low = big(part(1, 1).astype(BF), 1), big(part(3, 0).astype(BF), -1)
     kept, given = input_partial(place, g, w)
-    to_up, to_down, kept, given = tied(to_up, to_down, kept, given)
-    up, down = big(near(1, 0, rel, g, to_up), 1), big(near(3, 1, rel, g, to_down), -1)
-    total, sent_1, sent_2, sent_3 = own(rel, g, up, down)
-    weight_grad = add_all(total, small(sent_2, 2), small(sent_1, 1), small(sent_3, -1))
+    to_up, to_down, kept, given, held = tied(to_up, to_down, kept, given, held)
+    activated = held.astype(BF)
+    up_low = (part(1, 0) + to_up.astype(F32)).astype(BF)
+    down_high = (part(3, 1) + to_down.astype(F32)).astype(BF)
+    up_low, down_high = big(up_low, 1), big(down_high, -1)
 
     sums = (kept + swap_core(given).astype(F32)).reshape(N, 2 * depth, -1)
     sent = sums.astype(BF)
     z1, z3, z2 = shift_z(sent[1], 1), shift_z(sent[3], -1), shift_z(sent[2], 2)
-    input_grad = (sums[0] + z1.astype(F32) + z2.astype(F32) + z3.astype(F32)).T.astype(BF)
+
+    total, sent_1, sent_2, sent_3 = own(rel, g, up_low, up_high, down_low, down_high)
+    weight_grad = add_all(total, small(sent_2, 2), small(sent_1, 1), small(sent_3, -1))
+    input_grad = join(sums[0], z1, z2, z3)
     return (activated, input_grad, weight_grad)
 
 

time: 146 us -> 144 us (0.986); the launches traced: 144 us -> 143 us
  Pallas kernels: 34.7 us -> 30.6 us
  starting transfers between devices: 32.4 us -> 35.8 us
  matrix products: 1.54 us -> 4.65 us
  waiting for transfers between devices: 67.8 us -> 65.1 us
    ppermute x16 -> x18, waiting for transfers between devices: 58.7 us -> 48.4 us  [shift(): return lax.ppermute(block, ('row', 'col'), pairs)]
    ppermute x3, waiting for transfers between devices: 0.01 us -> 8.04 us  [shift_z(): return lax.ppermute(block, 'col', pairs)]
    ppermute x16 -> x18, starting transfers between devices: 20.9 us -> 25.7 us  [shift(): return lax.ppermute(block, ('row', 'col'), pairs)]
    dot_general x2 -> x6, matrix products: 1.54 us -> 4.65 us  [dot(): lax.dot_general(a, b, (((ca,), (cb,)), ((), ())), preferred_element_type=...]
    pallas_call x2 -> x1, Pallas kernels: 2.81 us -> 0.97 us  [join(): pl.pallas_call(join_kernel, out_shape=jax.ShapeDtypeStruct(kept.shape[::-...]
    unnamed x12 -> x11, local copies, waits for them, and re-layouts: 4.11 us -> 3.08 us
  transfers between devices with their start and end apart: 24 -> 26, of which waited for: 13 -> 16; matrix products, arithmetic and copies ran while one was open for 3% -> 5% of each run, Pallas kernels for 20% -> 18%
where the time goes in v3:
time: 144 us; the launch traced here: 143 us
  waiting for transfers between devices  65.1 us (45%)
  starting transfers between devices  35.8 us (25%)
  Pallas kernels  30.6 us (21%)
  matrix products  4.65 us (3%)
  local copies, waits for them, and re-layouts  4.01 us (3%)
  other arithmetic  2.29 us (2%)
    ppermute x18, waiting for transfers between devices, shift(): return lax.ppermute(block, ('row', 'col'), pairs)  48.4 us
    ppermute x18, starting transfers between devices, shift(): return lax.ppermute(block, ('row', 'col'), pairs)  25.7 us
    pallas_call x1, Pallas kernels, input_partial(): pl.pallas_call(functools.partial(input_kernel, tuple(pieces)), out_shape=...  10.9 us
    pallas_call x2, Pallas kernels, add_sums(): pl.pallas_call(functools.partial(sum_kernel, tuple(pieces), len(firsts)),...  8.21 us
    ppermute x3, waiting for transfers between devices, shift_z(): return lax.ppermute(block, 'col', pairs)  8.04 us
    ppermute x2, waiting for transfers between devices, spread_z(): return lax.ppermute(block, 'col', pairs)  6.95 us
    ppermute x3, starting transfers between devices, shift_z(): return lax.ppermute(block, 'col', pairs)  6.02 us
    dot_general x6, matrix products, dot(): lax.dot_general(a, b, (((ca,), (cb,)), ((), ())), preferred_element_type=...  4.65 us
  transfers between devices with their start and end apart: 26, of which 16 were waited for; matrix products, arithmetic and copies ran while one was open for 5% of the time, Pallas kernels for 18%

profile of v3, /device:TPU:6, one launch (start us, length us, event | category | flops | bytes accessed | tf_op | source)
XLA Modules:
  0.0 143.3 jit_solution(13907008418399152078)
XLA Ops:
  2.6 2.2 %collective-permute-start.5 = (bf16[192,1536]{1,0:T(8,128)(2,1)}, bf16[192,1536]{1,0:T(8,128)(2,1)S(1)}, u32[]{:S(2)}, u32[]{:S(2)}) collective-permute-start(bf16[192,1536]{1,0:T(8,128)(2,1)} %param.4), channel_id=1, source_target_pairs={{0,8},{1,33},{2,10},{3,35},{4,12},{5,37},{6,14},{7,39},{8,16},{9,4... | collective-permute-start | bytes 1769480 | tf_op jit(solution)/shard_map/ppermute | solution.py:25
  6.0 1.7 %collective-permute-done = bf16[384,512]{1,0:T(8,128)(2,1)S(1)} collective-permute-done((bf16[384,512]{1,0:T(8,128)(2,1)S(1)}, bf16[384,512]{1,0:T(8,128)(2,1)S(1)}, u32[]{:S(2)}, u32[]{:S(2)}) %collective-permute-start) | collective-permute-done | bytes 393248 | tf_op jit(solution)/shard_map/ppermute | solution.py:48
  7.8 2.0 %collective-permute-start.1 = (bf16[2,384,512]{2,1,0:T(8,128)(2,1)S(1)}, bf16[2,384,512]{2,1,0:T(8,128)(2,1)S(1)}, u32[]{:S(2)}, u32[]{:S(2)}) collective-permute-start(bf16[2,384,512]{2,1,0:T(8,128)(2,1)S(1)} %pad_maximum_fusion.2.here), channel_id=1, source_target_pairs={{0,2},{1,7},{2,4},{3,1},{4,6},{5,3},{6,0},{7,5},{8,10},{9,15},{10,... | collective-permute-start | bytes 2359304 | tf_op jit(solution)/shard_map/ppermute | solution.py:43
  9.8 8.6 %collective-permute-done.4 = bf16[192,1536]{1,0:T(8,128)(2,1)S(1)} collective-permute-done((bf16[192,1536]{1,0:T(8,128)(2,1)}, bf16[192,1536]{1,0:T(8,128)(2,1)S(1)}, u32[]{:S(2)}, u32[]{:S(2)}) %collective-permute-start.4) | collective-permute-done | bytes 589856 | tf_op jit(solution)/shard_map/ppermute | solution.py:25
  19.3 3.1 %collective-permute-start.7 = (bf16[2,192,1536]{2,1,0:T(8,128)(2,1)S(1)}, bf16[2,192,1536]{2,1,0:T(8,128)(2,1)}, u32[]{:S(2)}, u32[]{:S(2)}) collective-permute-start(bf16[2,192,1536]{2,1,0:T(8,128)(2,1)S(1)} %pad_maximum_fusion.refs_0_), channel_id=1, source_target_pairs={{0,96},{1,25},{2,98},{3,27},{4,100},{5,29},{6,102},{7,31},{8,104},... | collective-permute-start | bytes 3538952 | tf_op jit(solution)/shard_map/ppermute | solution.py:25
  22.7 2.0 %collective-permute-start.2 = (bf16[1,384,512]{2,1,0:T(8,128)(2,1)S(1)}, bf16[1,384,512]{2,1,0:T(8,128)(2,1)S(1)}, u32[]{:S(2)}, u32[]{:S(2)}) collective-permute-start(bf16[1,384,512]{2,1,0:T(8,128)(2,1)S(1)} %slice.48), channel_id=1, source_target_pairs={{0,2},{1,7},{2,4},{3,1},{4,6},{5,3},{6,0},{7,5},{8,10},{9,15},{10,... | collective-permute-start | bytes 1179656 | tf_op jit(solution)/shard_map/ppermute | solution.py:43
  25.6 6.9 %collective-permute-done.2 = bf16[1,384,512]{2,1,0:T(8,128)(2,1)S(1)} collective-permute-done((bf16[1,384,512]{2,1,0:T(8,128)(2,1)S(1)}, bf16[1,384,512]{2,1,0:T(8,128)(2,1)S(1)}, u32[]{:S(2)}, u32[]{:S(2)}) %collective-permute-start.2) | collective-permute-done | bytes 393248 | tf_op jit(solution)/shard_map/ppermute | solution.py:43
  33.9 2.7 %collective-permute-start.9 = (bf16[2,192,1536]{2,1,0:T(8,128)(2,1)S(1)}, bf16[2,192,1536]{2,1,0:T(8,128)(2,1)}, u32[]{:S(2)}, u32[]{:S(2)}) collective-permute-start(bf16[2,192,1536]{2,1,0:T(8,128)(2,1)S(1)} %pad_maximum_fusion.1.refs_1_), channel_id=1, source_target_pairs={{0,96},{1,25},{2,98},{3,27},{4,100},{5,29},{6,102},{7,31},{8,104},... | collective-permute-start | bytes 3538952 | tf_op jit(solution)/shard_map/ppermute | solution.py:25
  36.6 3.4 %collective-permute-start.11 = (bf16[2,192,1536]{2,1,0:T(8,128)(2,1)}, bf16[2,192,1536]{2,1,0:T(8,128)(2,1)}, u32[]{:S(2)}, u32[]{:S(2)}) collective-permute-start(bf16[2,192,1536]{2,1,0:T(8,128)(2,1)} %collective-permute-done.7.refs_2_), channel_id=1, source_target_pairs={{0,96},{1,25},{2,98},{3,27},{4,100},{5,29},{6,102},{7,31},{8,104},... | collective-permute-start | bytes 3538952 | tf_op jit(solution)/shard_map/ppermute | solution.py:25
  41.4 3.6 %shard_map.59.rel = bf16[4,4,192,512]{3,2,1,0:T(8,128)(2,1)S(1)} custom-call(s32[4]{0:T(128)S(1)} %pad_add_fusion.place, bf16[2,384,512]{2,1,0:T(8,128)(2,1)S(1)} %copy-done.1, bf16[3,384,512]{2,1,0:T(8,128)(2,1)} %constant_dynamic-update-slice_fusion.got, bf16[3,384,512]{2,1,0:T(8,128)(2,1)} %collective-permute-done.3.other), custom_call_target="tpu_custom_call" | custom-call | tf_op jit(solution)/shard_map/pallas_call | solution.py:125
  45.0 5.1 %shard_map.60.refs_0_ = f32[512,1536]{1,0:T(8,128)S(1)} custom-call(bf16[4,4,192,512]{3,2,1,0:T(8,128)(2,1)S(1)} %shard_map.59.rel, bf16[2,192,1536]{2,1,0:T(8,128)(2,1)S(1)} %pad_maximum_fusion.refs_0_, bf16[2,192,1536]{2,1,0:T(8,128)(2,1)S(1)} %pad_maximum_fusion.1.refs_1_, bf16[2,192,1536]{2,1,0:T(8,128)(2,1)} %collective-permute-done.7.refs_2_, ...), custom_call_target="tpu_custom_call" | custom-call | tf_op jit(solution)/shard_map/pallas_call | solution.py:161
  50.1 2.6 %collective-permute-done.10.refs_2_.refs_5_ = bf16[2,192,1536]{2,1,0:T(8,128)(2,1)S(1)} collective-permute-done((bf16[2,192,1536]{2,1,0:T(8,128)(2,1)S(1)}, bf16[2,192,1536]{2,1,0:T(8,128)(2,1)S(1)}, u32[]{:S(2)}, u32[]{:S(2)}) %collective-permute-start.10) | collective-permute-done | bytes 1179680 | tf_op jit(solution)/shard_map/ppermute | solution.py:25
  52.7 3.1 %shard_map.61.sums = f32[512,1536]{1,0:T(8,128)S(1)} custom-call(bf16[4,4,192,512]{3,2,1,0:T(8,128)(2,1)S(1)} %shard_map.59.rel, f32[512,1536]{1,0:T(8,128)S(1)} %shard_map.60.refs_0_, bf16[2,192,1536]{2,1,0:T(8,128)(2,1)} %collective-permute-done.9.refs_1_.refs_4_, bf16[2,192,1536]{2,1,0:T(8,128)(2,1)S(1)} %collective-permute-done.10.refs_2_.refs_5_), custom_call_target="tpu_custom_call" | custom-call | tf_op jit(solution)/shard_map/pallas_call | solution.py:161
  55.8 7.2 %collective-permute-done.11.refs_0_.refs_6_ = bf16[2,192,1536]{2,1,0:T(8,128)(2,1)} collective-permute-done((bf16[2,192,1536]{2,1,0:T(8,128)(2,1)}, bf16[2,192,1536]{2,1,0:T(8,128)(2,1)}, u32[]{:S(2)}, u32[]{:S(2)}) %collective-permute-start.11) | collective-permute-done | bytes 1179680 | tf_op jit(solution)/shard_map/ppermute | solution.py:25
  63.0 2.4 %collective-permute-done.12.refs_1_.refs_7_ = bf16[2,192,1536]{2,1,0:T(8,128)(2,1)} collective-permute-done((bf16[2,192,1536]{2,1,0:T(8,128)(2,1)}, bf16[2,192,1536]{2,1,0:T(8,128)(2,1)}, u32[]{:S(2)}, u32[]{:S(2)}) %collective-permute-start.12) | collective-permute-done | bytes 1179680 | tf_op jit(solution)/shard_map/ppermute | solution.py:25
  65.4 4.0 %shard_map.62 = (f32[512,1536]{1,0:T(8,128)S(1)}, bf16[512,1536]{1,0:T(8,128)(2,1)S(1)}) custom-call(bf16[4,4,192,512]{3,2,1,0:T(8,128)(2,1)S(1)} %shard_map.59.rel, f32[512,1536]{1,0:T(8,128)S(1)} %shard_map.61.sums, bf16[512,1536]{1,0:T(8,128)(2,1)S(1)} %copy-done.2, bf16[2,192,1536]{2,1,0:T(8,128)(2,1)} %collective-permute-done.11.refs_0_.refs_6_, ...), custom_call_target="tpu_custom_call" | custom-call | tf_op jit(solution)/shard_map/pallas_call | solution.py:189
  71.1 3.2 %collective-permute-start.14 = (bf16[2,192,1536]{2,1,0:T(8,128)(2,1)S(1)}, bf16[2,192,1536]{2,1,0:T(8,128)(2,1)S(1)}, u32[]{:S(2)}, u32[]{:S(2)}) collective-permute-start(bf16[2,192,1536]{2,1,0:T(8,128)(2,1)S(1)} %convolution_convert_fusion.2), channel_id=1, source_target_pairs={{0,96},{1,25},{2,98},{3,27},{4,100},{5,29},{6,102},{7,31},{8,104},... | collective-permute-start | bytes 3538952 | tf_op jit(solution)/shard_map/ppermute | solution.py:25
  76.0 2.0 %collective-permute-start.20 = (bf16[2,192,1536]{2,1,0:T(8,128)(2,1)S(1)}, bf16[2,192,1536]{2,1,0:T(8,128)(2,1)S(1)}, u32[]{:S(2)}, u32[]{:S(2)}) collective-permute-start(bf16[2,192,1536]{2,1,0:T(8,128)(2,1)S(1)} %convolution_convert_fusion.1), channel_id=1, source_target_pairs={{0,32},{1,9},{2,34},{3,11},{4,36},{5,13},{6,38},{7,15},{8,40},{9,1... | collective-permute-start | bytes 3538952 | tf_op jit(solution)/shard_map/ppermute | solution.py:25
  78.0 10.9 %shard_map.63 = (f32[1536,512]{1,0:T(8,128)S(1)}, bf16[1536,512]{1,0:T(8,128)(2,1)S(1)}) custom-call(s32[4]{0:T(128)S(1)} %pad_add_fusion.place, bf16[512,1536]{1,0:T(8,128)(2,1)S(1)} %get-tuple-element.22.g, bf16[2,192,1536]{2,1,0:T(8,128)(2,1)S(1)} %pad_maximum_fusion.refs_0_, bf16[2,192,1536]{2,1,0:T(8,128)(2,1)S(1)} %pad_maximum_fusion.1.refs_1_, ...), custom_call_target="tpu_custom_call" | custom-call | tf_op jit(solution)/shard_map/pallas_call | solution.py:276
  90.6 2.8 %collective-permute-start.22 = (bf16[2,192,1536]{2,1,0:T(8,128)(2,1)S(1)}, bf16[2,192,1536]{2,1,0:T(8,128)(2,1)S(1)}, u32[]{:S(2)}, u32[]{:S(2)}) collective-permute-start(bf16[2,192,1536]{2,1,0:T(8,128)(2,1)S(1)} %fusion.1), channel_id=1, source_target_pairs={{0,96},{1,25},{2,98},{3,27},{4,100},{5,29},{6,102},{7,31},{8,104},... | collective-permute-start | bytes 3538952 | tf_op jit(solution)/shard_map/ppermute | solution.py:25
  93.4 7.3 %collective-permute-done.21.down_low = bf16[2,192,1536]{2,1,0:T(8,128)(2,1)S(1)} collective-permute-done((bf16[2,192,1536]{2,1,0:T(8,128)(2,1)S(1)}, bf16[2,192,1536]{2,1,0:T(8,128)(2,1)S(1)}, u32[]{:S(2)}, u32[]{:S(2)}) %collective-permute-start.21) | collective-permute-done | bytes 1179680 | tf_op jit(solution)/shard_map/ppermute | solution.py:25
  101.1 12.2 %collective-permute-done.22.down_high = bf16[2,192,1536]{2,1,0:T(8,128)(2,1)S(1)} collective-permute-done((bf16[2,192,1536]{2,1,0:T(8,128)(2,1)S(1)}, bf16[2,192,1536]{2,1,0:T(8,128)(2,1)S(1)}, u32[]{:S(2)}, u32[]{:S(2)}) %collective-permute-start.22) | collective-permute-done | bytes 1179680 | tf_op jit(solution)/shard_map/ppermute | solution.py:25
  113.7 1.5 %shard_map.65 = (f32[192,1536]{1,0:T(8,128)S(1)}, bf16[192,1536]{1,0:T(8,128)(2,1)S(1)}, bf16[192,1536]{1,0:T(8,128)(2,1)S(1)}, bf16[192,1536]{1,0:T(8,128)(2,1)S(1)}) custom-call(bf16[4,4,192,512]{3,2,1,0:T(8,128)(2,1)S(1)} %shard_map.59.rel, bf16[512,1536]{1,0:T(8,128)(2,1)S(1)} %get-tuple-element.22.g, ...), custom_call_target="tpu_custom_call" | custom-call | tf_op jit(solution)/shard_map/pallas_call | solution.py:212
  115.3 1.5 %collective-permute-start.23 = (bf16[192,1536]{1,0:T(8,128)(2,1)S(1)}, bf16[192,1536]{1,0:T(8,128)(2,1)S(1)}, u32[]{:S(2)}, u32[]{:S(2)}) collective-permute-start(bf16[192,1536]{1,0:T(8,128)(2,1)S(1)} %get-tuple-element.32), channel_id=1, source_target_pairs={{0,16},{1,65},{2,18},{3,67},{4,20},{5,69},{6,22},{7,71},{8,24},{9,... | collective-permute-start | bytes 1769480 | tf_op jit(solution)/shard_map/ppermute | solution.py:25
  116.8 2.0 %collective-permute-start.24 = (bf16[192,1536]{1,0:T(8,128)(2,1)S(1)}, bf16[192,1536]{1,0:T(8,128)(2,1)S(1)}, u32[]{:S(2)}, u32[]{:S(2)}) collective-permute-start(bf16[192,1536]{1,0:T(8,128)(2,1)S(1)} %get-tuple-element.33), channel_id=1, source_target_pairs={{0,8},{1,33},{2,10},{3,35},{4,12},{5,37},{6,14},{7,39},{8,16},{9,4... | collective-permute-start | bytes 1769480 | tf_op jit(solution)/shard_map/ppermute | solution.py:25
  119.5 4.1 %collective-permute-start.18 = (bf16[384,512]{1,0:T(8,128)(2,1)S(1)}, bf16[384,512]{1,0:T(8,128)(2,1)S(1)}, u32[]{:S(2)}, u32[]{:S(2)}) collective-permute-start(bf16[384,512]{1,0:T(8,128)(2,1)S(1)} %get-tuple-element.37), channel_id=1, source_target_pairs={{0,6},{1,7},{2,0},{3,1},{4,2},{5,3},{6,4},{7,5},{8,14},{9,15},{10,... | collective-permute-start | bytes 1179656 | tf_op jit(solution)/shard_map/ppermute | solution.py:38
  123.7 3.2 %collective-permute-done.23.a = bf16[192,1536]{1,0:T(8,128)(2,1)S(1)} collective-permute-done((bf16[192,1536]{1,0:T(8,128)(2,1)S(1)}, bf16[192,1536]{1,0:T(8,128)(2,1)S(1)}, u32[]{:S(2)}, u32[]{:S(2)}) %collective-permute-start.23) | collective-permute-done | bytes 589856 | tf_op jit(solution)/shard_map/ppermute | solution.py:25
  126.9 1.9 %collective-permute-start.16 = (bf16[384,512]{1,0:T(8,128)(2,1)S(1)}, bf16[384,512]{1,0:T(8,128)(2,1)S(1)}, u32[]{:S(2)}, u32[]{:S(2)}) collective-permute-start(bf16[384,512]{1,0:T(8,128)(2,1)S(1)} %get-tuple-element.39), channel_id=1, source_target_pairs={{0,2},{1,3},{2,4},{3,5},{4,6},{5,7},{6,0},{7,1},{8,10},{9,11},{10,... | collective-permute-start | bytes 1179656 | tf_op jit(solution)/shard_map/ppermute | solution.py:38
  128.8 1.3 convert_element_type.36
  130.1 2.9 %collective-permute-done.24.b = bf16[192,1536]{1,0:T(8,128)(2,1)S(1)} collective-permute-done((bf16[192,1536]{1,0:T(8,128)(2,1)S(1)}, bf16[192,1536]{1,0:T(8,128)(2,1)S(1)}, u32[]{:S(2)}, u32[]{:S(2)}) %collective-permute-start.24) | collective-permute-done | bytes 589856 | tf_op jit(solution)/shard_map/ppermute | solution.py:25
  134.3 4.4 %collective-permute-done.18.c = bf16[384,512]{1,0:T(8,128)(2,1)S(1)} collective-permute-done((bf16[384,512]{1,0:T(8,128)(2,1)S(1)}, bf16[384,512]{1,0:T(8,128)(2,1)S(1)}, u32[]{:S(2)}, u32[]{:S(2)}) %collective-permute-start.18) | collective-permute-done | bytes 393248 | tf_op jit(solution)/shard_map/ppermute | solution.py:38
  138.7 3.7 %collective-permute-done.16.a = bf16[384,512]{1,0:T(8,128)(2,1)S(1)} collective-permute-done((bf16[384,512]{1,0:T(8,128)(2,1)S(1)}, bf16[384,512]{1,0:T(8,128)(2,1)S(1)}, u32[]{:S(2)}, u32[]{:S(2)}) %collective-permute-start.16) | collective-permute-done | bytes 393248 | tf_op jit(solution)/shard_map/ppermute | solution.py:38
  (56 shorter events, 17.0 us)
Async XLA Ops:
  0.6 17.7 %collective-permute-start.4 = (bf16[192,1536]{1,0:T(8,128)(2,1)}, bf16[192,1536]{1,0:T(8,128)(2,1)S(1)}, u32[]{:S(2)}, u32[]{:S(2)}) collective-permute-start(bf16[192,1536]{1,0:T(8,128)(2,1)} %param.4), channel_id=1, source_target_pairs={{0,24},{1,97},{2,26},{3,99},{4,28},{5,101},{6,30},{7,103},{8,0},{9... | collective-permute-start | bytes 1769480 | tf_op jit(solution)/shard_map/ppermute | solution.py:25
  1.5 16.8 %collective-permute-start.6 = (bf16[192,1536]{1,0:T(8,128)(2,1)}, bf16[192,1536]{1,0:T(8,128)(2,1)S(1)}, u32[]{:S(2)}, u32[]{:S(2)}) collective-permute-start(bf16[192,1536]{1,0:T(8,128)(2,1)} %param.4), channel_id=1, source_target_pairs={{0,16},{1,65},{2,18},{3,67},{4,20},{5,69},{6,22},{7,71},{8,24},{9,... | collective-permute-start | bytes 1769480 | tf_op jit(solution)/shard_map/ppermute | solution.py:25
  2.6 16.7 %collective-permute-start.5 = (bf16[192,1536]{1,0:T(8,128)(2,1)}, bf16[192,1536]{1,0:T(8,128)(2,1)S(1)}, u32[]{:S(2)}, u32[]{:S(2)}) collective-permute-start(bf16[192,1536]{1,0:T(8,128)(2,1)} %param.4), channel_id=1, source_target_pairs={{0,8},{1,33},{2,10},{3,35},{4,12},{5,37},{6,14},{7,39},{8,16},{9,4... | collective-permute-start | bytes 1769480 | tf_op jit(solution)/shard_map/ppermute | solution.py:25
  4.7 1.0 copy-start.3
  5.7 13.5 %copy-start.4 = (bf16[192,1536]{1,0:T(8,128)(2,1)S(1)}, bf16[192,1536]{1,0:T(8,128)(2,1)}, u32[]{:S(2)}) copy-start(bf16[192,1536]{1,0:T(8,128)(2,1)} %param.4) | copy-start | bytes 1769476
  5.9 1.8 %collective-permute-start = (bf16[384,512]{1,0:T(8,128)(2,1)S(1)}, bf16[384,512]{1,0:T(8,128)(2,1)S(1)}, u32[]{:S(2)}, u32[]{:S(2)}) collective-permute-start(bf16[384,512]{1,0:T(8,128)(2,1)S(1)} %shard_map.58), channel_id=1, source_target_pairs={{0,1},{1,0},{2,3},{3,2},{4,5},{5,4},{6,7},{7,6},{8,9},{9,8},{10,11... | collective-permute-start | bytes 1179656 | tf_op jit(solution)/shard_map/ppermute | solution.py:48
  7.8 14.8 %copy-start = (bf16[2,384,512]{2,1,0:T(8,128)(2,1)}, bf16[2,384,512]{2,1,0:T(8,128)(2,1)S(1)}, u32[]{:S(2)}) copy-start(bf16[2,384,512]{2,1,0:T(8,128)(2,1)S(1)} %pad_maximum_fusion.2.here) | copy-start | bytes 2359300
  7.8 14.8 %collective-permute-start.1 = (bf16[2,384,512]{2,1,0:T(8,128)(2,1)S(1)}, bf16[2,384,512]{2,1,0:T(8,128)(2,1)S(1)}, u32[]{:S(2)}, u32[]{:S(2)}) collective-permute-start(bf16[2,384,512]{2,1,0:T(8,128)(2,1)S(1)} %pad_maximum_fusion.2.here), channel_id=1, source_target_pairs={{0,2},{1,7},{2,4},{3,1},{4,6},{5,3},{6,0},{7,5},{8,10},{9,15},{10,... | collective-permute-start | bytes 2359304 | tf_op jit(solution)/shard_map/ppermute | solution.py:43
  19.3 17.2 %collective-permute-start.7 = (bf16[2,192,1536]{2,1,0:T(8,128)(2,1)S(1)}, bf16[2,192,1536]{2,1,0:T(8,128)(2,1)}, u32[]{:S(2)}, u32[]{:S(2)}) collective-permute-start(bf16[2,192,1536]{2,1,0:T(8,128)(2,1)S(1)} %pad_maximum_fusion.refs_0_), channel_id=1, source_target_pairs={{0,96},{1,25},{2,98},{3,27},{4,100},{5,29},{6,102},{7,31},{8,104},... | collective-permute-start | bytes 3538952 | tf_op jit(solution)/shard_map/ppermute | solution.py:25
  22.5 17.6 %collective-permute-start.8 = (bf16[2,192,1536]{2,1,0:T(8,128)(2,1)S(1)}, bf16[2,192,1536]{2,1,0:T(8,128)(2,1)}, u32[]{:S(2)}, u32[]{:S(2)}) collective-permute-start(bf16[2,192,1536]{2,1,0:T(8,128)(2,1)S(1)} %pad_maximum_fusion.1.refs_1_), channel_id=1, source_target_pairs={{0,32},{1,9},{2,34},{3,11},{4,36},{5,13},{6,38},{7,15},{8,40},{9,1... | collective-permute-start | bytes 3538952 | tf_op jit(solution)/shard_map/ppermute | solution.py:25
  22.7 9.9 %collective-permute-start.2 = (bf16[1,384,512]{2,1,0:T(8,128)(2,1)S(1)}, bf16[1,384,512]{2,1,0:T(8,128)(2,1)S(1)}, u32[]{:S(2)}, u32[]{:S(2)}) collective-permute-start(bf16[1,384,512]{2,1,0:T(8,128)(2,1)S(1)} %slice.48), channel_id=1, source_target_pairs={{0,2},{1,7},{2,4},{3,1},{4,6},{5,3},{6,0},{7,5},{8,10},{9,15},{10,... | collective-permute-start | bytes 1179656 | tf_op jit(solution)/shard_map/ppermute | solution.py:43
  33.3 6.9 %collective-permute-start.3 = (bf16[3,384,512]{2,1,0:T(8,128)(2,1)}, bf16[3,384,512]{2,1,0:T(8,128)(2,1)}, u32[]{:S(2)}, u32[]{:S(2)}) collective-permute-start(bf16[3,384,512]{2,1,0:T(8,128)(2,1)} %constant_dynamic-update-slice_fusion.got), channel_id=1, source_target_pairs={{0,1},{1,0},{2,3},{3,2},{4,5},{5,4},{6,7},{7,6},{8,9},{9,8},{10,11... | collective-permute-start | bytes 3538952 | tf_op jit(solution)/shard_map/ppermute | solution.py:48
  33.3 19.4 %collective-permute-start.10 = (bf16[2,192,1536]{2,1,0:T(8,128)(2,1)S(1)}, bf16[2,192,1536]{2,1,0:T(8,128)(2,1)S(1)}, u32[]{:S(2)}, u32[]{:S(2)}) collective-permute-start(bf16[2,192,1536]{2,1,0:T(8,128)(2,1)S(1)} %pad_maximum_fusion.refs_0_), channel_id=1, source_target_pairs={{0,32},{1,9},{2,34},{3,11},{4,36},{5,13},{6,38},{7,15},{8,40},{9,1... | collective-permute-start | bytes 3538952 | tf_op jit(solution)/shard_map/ppermute | solution.py:25
  33.9 18.8 %collective-permute-start.9 = (bf16[2,192,1536]{2,1,0:T(8,128)(2,1)S(1)}, bf16[2,192,1536]{2,1,0:T(8,128)(2,1)}, u32[]{:S(2)}, u32[]{:S(2)}) collective-permute-start(bf16[2,192,1536]{2,1,0:T(8,128)(2,1)S(1)} %pad_maximum_fusion.1.refs_1_), channel_id=1, source_target_pairs={{0,96},{1,25},{2,98},{3,27},{4,100},{5,29},{6,102},{7,31},{8,104},... | collective-permute-start | bytes 3538952 | tf_op jit(solution)/shard_map/ppermute | solution.py:25
  36.6 26.5 %collective-permute-start.11 = (bf16[2,192,1536]{2,1,0:T(8,128)(2,1)}, bf16[2,192,1536]{2,1,0:T(8,128)(2,1)}, u32[]{:S(2)}, u32[]{:S(2)}) collective-permute-start(bf16[2,192,1536]{2,1,0:T(8,128)(2,1)} %collective-permute-done.7.refs_2_), channel_id=1, source_target_pairs={{0,96},{1,25},{2,98},{3,27},{4,100},{5,29},{6,102},{7,31},{8,104},... | collective-permute-start | bytes 3538952 | tf_op jit(solution)/shard_map/ppermute | solution.py:25
  40.1 25.3 %collective-permute-start.12 = (bf16[2,192,1536]{2,1,0:T(8,128)(2,1)}, bf16[2,192,1536]{2,1,0:T(8,128)(2,1)}, u32[]{:S(2)}, u32[]{:S(2)}) collective-permute-start(bf16[2,192,1536]{2,1,0:T(8,128)(2,1)} %collective-permute-done.8.refs_3_), channel_id=1, source_target_pairs={{0,32},{1,9},{2,34},{3,11},{4,36},{5,13},{6,38},{7,15},{8,40},{9,1... | collective-permute-start | bytes 3538952 | tf_op jit(solution)/shard_map/ppermute | solution.py:25
  40.2 1.1 copy-start.1
  50.1 15.4 %copy-start.2 = (bf16[512,1536]{1,0:T(8,128)(2,1)S(1)}, bf16[512,1536]{1,0:T(8,128)(2,1)}, u32[]{:S(2)}) copy-start(bf16[512,1536]{1,0:T(8,128)(2,1)} %cot.1) | copy-start | bytes 4718596
  71.0 17.9 %collective-permute-start.13 = (bf16[2,192,1536]{2,1,0:T(8,128)(2,1)S(1)}, bf16[2,192,1536]{2,1,0:T(8,128)(2,1)S(1)}, u32[]{:S(2)}, u32[]{:S(2)}) collective-permute-start(bf16[2,192,1536]{2,1,0:T(8,128)(2,1)S(1)} %convolution_convert_fusion.3), channel_id=1, source_target_pairs={{0,32},{1,9},{2,34},{3,11},{4,36},{5,13},{6,38},{7,15},{8,40},{9,1... | collective-permute-start | bytes 3538952 | tf_op jit(solution)/shard_map/ppermute | solution.py:25
  71.1 17.8 %collective-permute-start.14 = (bf16[2,192,1536]{2,1,0:T(8,128)(2,1)S(1)}, bf16[2,192,1536]{2,1,0:T(8,128)(2,1)S(1)}, u32[]{:S(2)}, u32[]{:S(2)}) collective-permute-start(bf16[2,192,1536]{2,1,0:T(8,128)(2,1)S(1)} %convolution_convert_fusion.2), channel_id=1, source_target_pairs={{0,96},{1,25},{2,98},{3,27},{4,100},{5,29},{6,102},{7,31},{8,104},... | collective-permute-start | bytes 3538952 | tf_op jit(solution)/shard_map/ppermute | solution.py:25
  75.1 25.6 %collective-permute-start.21 = (bf16[2,192,1536]{2,1,0:T(8,128)(2,1)S(1)}, bf16[2,192,1536]{2,1,0:T(8,128)(2,1)S(1)}, u32[]{:S(2)}, u32[]{:S(2)}) collective-permute-start(bf16[2,192,1536]{2,1,0:T(8,128)(2,1)S(1)} %convolution_convert_fusion), channel_id=1, source_target_pairs={{0,96},{1,25},{2,98},{3,27},{4,100},{5,29},{6,102},{7,31},{8,104},... | collective-permute-start | bytes 3538952 | tf_op jit(solution)/shard_map/ppermute | solution.py:25
  76.0 25.1 %collective-permute-start.20 = (bf16[2,192,1536]{2,1,0:T(8,128)(2,1)S(1)}, bf16[2,192,1536]{2,1,0:T(8,128)(2,1)S(1)}, u32[]{:S(2)}, u32[]{:S(2)}) collective-permute-start(bf16[2,192,1536]{2,1,0:T(8,128)(2,1)S(1)} %convolution_convert_fusion.1), channel_id=1, source_target_pairs={{0,32},{1,9},{2,34},{3,11},{4,36},{5,13},{6,38},{7,15},{8,40},{9,1... | collective-permute-start | bytes 3538952 | tf_op jit(solution)/shard_map/ppermute | solution.py:25
  88.9 29.9 %collective-permute-start.15 = (bf16[1536,512]{1,0:T(8,128)(2,1)S(1)}, bf16[1536,512]{1,0:T(8,128)(2,1)S(1)}, u32[]{:S(2)}, u32[]{:S(2)}) collective-permute-start(bf16[1536,512]{1,0:T(8,128)(2,1)S(1)} %get-tuple-element.28), channel_id=1, source_target_pairs={{0,1},{1,0},{2,3},{3,2},{4,5},{5,4},{6,7},{7,6},{8,9},{9,8},{10,11... | collective-permute-start | bytes 4718600 | tf_op jit(solution)/shard_map/ppermute | solution.py:48
  90.6 22.7 %collective-permute-start.22 = (bf16[2,192,1536]{2,1,0:T(8,128)(2,1)S(1)}, bf16[2,192,1536]{2,1,0:T(8,128)(2,1)S(1)}, u32[]{:S(2)}, u32[]{:S(2)}) collective-permute-start(bf16[2,192,1536]{2,1,0:T(8,128)(2,1)S(1)} %fusion.1), channel_id=1, source_target_pairs={{0,96},{1,25},{2,98},{3,27},{4,100},{5,29},{6,102},{7,31},{8,104},... | collective-permute-start | bytes 3538952 | tf_op jit(solution)/shard_map/ppermute | solution.py:25
  93.4 20.4 %collective-permute-start.19 = (bf16[2,192,1536]{2,1,0:T(8,128)(2,1)S(1)}, bf16[2,192,1536]{2,1,0:T(8,128)(2,1)S(1)}, u32[]{:S(2)}, u32[]{:S(2)}) collective-permute-start(bf16[2,192,1536]{2,1,0:T(8,128)(2,1)S(1)} %fusion), channel_id=1, source_target_pairs={{0,32},{1,9},{2,34},{3,11},{4,36},{5,13},{6,38},{7,15},{8,40},{9,1... | collective-permute-start | bytes 3538952 | tf_op jit(solution)/shard_map/ppermute | solution.py:25
  115.3 11.6 %collective-permute-start.23 = (bf16[192,1536]{1,0:T(8,128)(2,1)S(1)}, bf16[192,1536]{1,0:T(8,128)(2,1)S(1)}, u32[]{:S(2)}, u32[]{:S(2)}) collective-permute-start(bf16[192,1536]{1,0:T(8,128)(2,1)S(1)} %get-tuple-element.32), channel_id=1, source_target_pairs={{0,16},{1,65},{2,18},{3,67},{4,20},{5,69},{6,22},{7,71},{8,24},{9,... | collective-permute-start | bytes 1769480 | tf_op jit(solution)/shard_map/ppermute | solution.py:25
  116.8 16.3 %collective-permute-start.24 = (bf16[192,1536]{1,0:T(8,128)(2,1)S(1)}, bf16[192,1536]{1,0:T(8,128)(2,1)S(1)}, u32[]{:S(2)}, u32[]{:S(2)}) collective-permute-start(bf16[192,1536]{1,0:T(8,128)(2,1)S(1)} %get-tuple-element.33), channel_id=1, source_target_pairs={{0,8},{1,33},{2,10},{3,35},{4,12},{5,37},{6,14},{7,39},{8,16},{9,4... | collective-permute-start | bytes 1769480 | tf_op jit(solution)/shard_map/ppermute | solution.py:25
  118.8 14.3 %collective-permute-start.25 = (bf16[192,1536]{1,0:T(8,128)(2,1)S(1)}, bf16[192,1536]{1,0:T(8,128)(2,1)S(1)}, u32[]{:S(2)}, u32[]{:S(2)}) collective-permute-start(bf16[192,1536]{1,0:T(8,128)(2,1)S(1)} %get-tuple-element.34), channel_id=1, source_target_pairs={{0,24},{1,97},{2,26},{3,99},{4,28},{5,101},{6,30},{7,103},{8,0},{9... | collective-permute-start | bytes 1769480 | tf_op jit(solution)/shard_map/ppermute | solution.py:25
  119.5 19.1 %collective-permute-start.18 = (bf16[384,512]{1,0:T(8,128)(2,1)S(1)}, bf16[384,512]{1,0:T(8,128)(2,1)S(1)}, u32[]{:S(2)}, u32[]{:S(2)}) collective-permute-start(bf16[384,512]{1,0:T(8,128)(2,1)S(1)} %get-tuple-element.37), channel_id=1, source_target_pairs={{0,6},{1,7},{2,0},{3,1},{4,2},{5,3},{6,4},{7,5},{8,14},{9,15},{10,... | collective-permute-start | bytes 1179656 | tf_op jit(solution)/shard_map/ppermute | solution.py:38
  123.7 15.0 %collective-permute-start.17 = (bf16[384,512]{1,0:T(8,128)(2,1)S(1)}, bf16[384,512]{1,0:T(8,128)(2,1)S(1)}, u32[]{:S(2)}, u32[]{:S(2)}) collective-permute-start(bf16[384,512]{1,0:T(8,128)(2,1)S(1)} %get-tuple-element.38), channel_id=1, source_target_pairs={{0,4},{1,5},{2,6},{3,7},{4,0},{5,1},{6,2},{7,3},{8,12},{9,13},{10,... | collective-permute-start | bytes 1179656 | tf_op jit(solution)/shard_map/ppermute | solution.py:38
  126.9 15.5 %collective-permute-start.16 = (bf16[384,512]{1,0:T(8,128)(2,1)S(1)}, bf16[384,512]{1,0:T(8,128)(2,1)S(1)}, u32[]{:S(2)}, u32[]{:S(2)}) collective-permute-start(bf16[384,512]{1,0:T(8,128)(2,1)S(1)} %get-tuple-element.39), channel_id=1, source_target_pairs={{0,2},{1,3},{2,4},{3,5},{4,6},{5,7},{6,0},{7,1},{8,10},{9,11},{10,... | collective-permute-start | bytes 1179656 | tf_op jit(solution)/shard_map/ppermute | solution.py:38

commit v4 on v3

--- a/solution.py
+++ b/solution.py
@@ -288,11 +288,11 @@
     place = jnp.stack([row // N, row % N, col // 2, col % 2])
     depth = weight.shape[0]
 
-    up, down, across = small(weight, -1), small(weight, 1), small(weight, 2)
+    across, up, down = small(weight, 2), small(weight, -1), small(weight, 1)
     mine = turn(tokens)
     here = jnp.stack([mine, swap_core(mine)])
     got = spread_z(here)
-    up, down, across = tied(up, down, across)
+    across, up, down = tied(across, up, down)
     w = {(0, 0): jnp.stack([weight, up]), (0, 1): jnp.stack([across, down])}
     w[1, 0] = big(w[0, 0], -1)
     w[3, 1] = big(w[0, 1], 1)

time: 144 us -> 143 us (level)
  waiting for transfers between devices: 65.1 us -> 63.6 us
    ppermute x3, starting transfers between devices: 0.17 us -> 2.09 us  [swap_core(): return lax.ppermute(block, 'col', pairs)]
    ppermute x18, waiting for transfers between devices: 48.4 us -> 46.7 us  [shift(): return lax.ppermute(block, ('row', 'col'), pairs)]
  transfers between devices with their start and end apart: 26 -> 26, of which waited for: 16 -> 19; matrix products, arithmetic and copies ran while one was open for 5% -> 5% of each run, Pallas kernels for 18% -> 18%
where the time goes in v4:
time: 143 us; the launch traced here: 142 us
  waiting for transfers between devices  63.6 us (44%)
  starting transfers between devices  36.4 us (25%)
  Pallas kernels  30.6 us (21%)
  matrix products  4.65 us (3%)
  local copies, waits for them, and re-layouts  4.01 us (3%)
  other arithmetic  2.29 us (2%)
    ppermute x18, waiting for transfers between devices, shift(): return lax.ppermute(block, ('row', 'col'), pairs)  46.7 us
    ppermute x18, starting transfers between devices, shift(): return lax.ppermute(block, ('row', 'col'), pairs)  25.2 us
    pallas_call x1, Pallas kernels, input_partial(): pl.pallas_call(functools.partial(input_kernel, tuple(pieces)), out_shape=...  10.9 us
    pallas_call x2, Pallas kernels, add_sums(): pl.pallas_call(functools.partial(sum_kernel, tuple(pieces), len(firsts)),...  8.21 us
    ppermute x2, waiting for transfers between devices, spread_z(): return lax.ppermute(block, 'col', pairs)  7.83 us
    ppermute x3, waiting for transfers between devices, shift_z(): return lax.ppermute(block, 'col', pairs)  7.73 us
    ppermute x3, starting transfers between devices, shift_z(): return lax.ppermute(block, 'col', pairs)  6.01 us
    dot_general x6, matrix products, dot(): lax.dot_general(a, b, (((ca,), (cb,)), ((), ())), preferred_element_type=...  4.65 us
  transfers between devices with their start and end apart: 26, of which 19 were waited for; matrix products, arithmetic and copies ran while one was open for 5% of the time, Pallas kernels for 18%

profile of v4, /device:TPU:6, one launch (start us, length us, event | category | flops | bytes accessed | tf_op | source)
XLA Modules:
  0.0 142.4 jit_solution(7230701412613900696)
XLA Ops:
  0.6 1.5 %collective-permute-start.4 = (bf16[192,1536]{1,0:T(8,128)(2,1)}, bf16[192,1536]{1,0:T(8,128)(2,1)S(1)}, u32[]{:S(2)}, u32[]{:S(2)}) collective-permute-start(bf16[192,1536]{1,0:T(8,128)(2,1)} %param.4), channel_id=1, source_target_pairs={{0,16},{1,65},{2,18},{3,67},{4,20},{5,69},{6,22},{7,71},{8,24},{9,... | collective-permute-start | bytes 1769480 | tf_op jit(solution)/shard_map/ppermute | solution.py:25
  2.1 2.1 %collective-permute-start.6 = (bf16[192,1536]{1,0:T(8,128)(2,1)}, bf16[192,1536]{1,0:T(8,128)(2,1)S(1)}, u32[]{:S(2)}, u32[]{:S(2)}) collective-permute-start(bf16[192,1536]{1,0:T(8,128)(2,1)} %param.4), channel_id=1, source_target_pairs={{0,8},{1,33},{2,10},{3,35},{4,12},{5,37},{6,14},{7,39},{8,16},{9,4... | collective-permute-start | bytes 1769480 | tf_op jit(solution)/shard_map/ppermute | solution.py:25
  5.4 2.0 %collective-permute-start = (bf16[384,512]{1,0:T(8,128)(2,1)S(1)}, bf16[384,512]{1,0:T(8,128)(2,1)S(1)}, u32[]{:S(2)}, u32[]{:S(2)}) collective-permute-start(bf16[384,512]{1,0:T(8,128)(2,1)S(1)} %shard_map.58), channel_id=1, source_target_pairs={{0,1},{1,0},{2,3},{3,2},{4,5},{5,4},{6,7},{7,6},{8,9},{9,8},{10,11... | collective-permute-start | bytes 1179656 | tf_op jit(solution)/shard_map/ppermute | solution.py:48
  8.8 2.0 %collective-permute-start.1 = (bf16[2,384,512]{2,1,0:T(8,128)(2,1)S(1)}, bf16[2,384,512]{2,1,0:T(8,128)(2,1)S(1)}, u32[]{:S(2)}, u32[]{:S(2)}) collective-permute-start(bf16[2,384,512]{2,1,0:T(8,128)(2,1)S(1)} %pad_maximum_fusion.2.here), channel_id=1, source_target_pairs={{0,2},{1,7},{2,4},{3,1},{4,6},{5,3},{6,0},{7,5},{8,10},{9,15},{10,... | collective-permute-start | bytes 2359304 | tf_op jit(solution)/shard_map/ppermute | solution.py:43
  10.8 1.6 %collective-permute-done.4 = bf16[192,1536]{1,0:T(8,128)(2,1)S(1)} collective-permute-done((bf16[192,1536]{1,0:T(8,128)(2,1)}, bf16[192,1536]{1,0:T(8,128)(2,1)S(1)}, u32[]{:S(2)}, u32[]{:S(2)}) %collective-permute-start.4) | collective-permute-done | bytes 589856 | tf_op jit(solution)/shard_map/ppermute | solution.py:25
  12.4 4.0 %collective-permute-done.6 = bf16[192,1536]{1,0:T(8,128)(2,1)S(1)} collective-permute-done((bf16[192,1536]{1,0:T(8,128)(2,1)}, bf16[192,1536]{1,0:T(8,128)(2,1)S(1)}, u32[]{:S(2)}, u32[]{:S(2)}) %collective-permute-start.6) | collective-permute-done | bytes 589856 | tf_op jit(solution)/shard_map/ppermute | solution.py:25
  16.4 2.2 %collective-permute-done.5 = bf16[192,1536]{1,0:T(8,128)(2,1)S(1)} collective-permute-done((bf16[192,1536]{1,0:T(8,128)(2,1)}, bf16[192,1536]{1,0:T(8,128)(2,1)S(1)}, u32[]{:S(2)}, u32[]{:S(2)}) %collective-permute-start.5) | collective-permute-done | bytes 589856 | tf_op jit(solution)/shard_map/ppermute | solution.py:25
  18.7 3.1 %collective-permute-start.7 = (bf16[2,192,1536]{2,1,0:T(8,128)(2,1)S(1)}, bf16[2,192,1536]{2,1,0:T(8,128)(2,1)}, u32[]{:S(2)}, u32[]{:S(2)}) collective-permute-start(bf16[2,192,1536]{2,1,0:T(8,128)(2,1)S(1)} %pad_maximum_fusion.refs_0_), channel_id=1, source_target_pairs={{0,96},{1,25},{2,98},{3,27},{4,100},{5,29},{6,102},{7,31},{8,104},... | collective-permute-start | bytes 3538952 | tf_op jit(solution)/shard_map/ppermute | solution.py:25
  25.0 7.0 %collective-permute-done.2 = bf16[1,384,512]{2,1,0:T(8,128)(2,1)S(1)} collective-permute-done((bf16[1,384,512]{2,1,0:T(8,128)(2,1)S(1)}, bf16[1,384,512]{2,1,0:T(8,128)(2,1)S(1)}, u32[]{:S(2)}, u32[]{:S(2)}) %collective-permute-start.2) | collective-permute-done | bytes 393248 | tf_op jit(solution)/shard_map/ppermute | solution.py:43
  33.3 2.7 %collective-permute-start.9 = (bf16[2,192,1536]{2,1,0:T(8,128)(2,1)S(1)}, bf16[2,192,1536]{2,1,0:T(8,128)(2,1)}, u32[]{:S(2)}, u32[]{:S(2)}) collective-permute-start(bf16[2,192,1536]{2,1,0:T(8,128)(2,1)S(1)} %pad_maximum_fusion.1.refs_1_), channel_id=1, source_target_pairs={{0,96},{1,25},{2,98},{3,27},{4,100},{5,29},{6,102},{7,31},{8,104},... | collective-permute-start | bytes 3538952 | tf_op jit(solution)/shard_map/ppermute | solution.py:25
  36.0 3.4 %collective-permute-start.11 = (bf16[2,192,1536]{2,1,0:T(8,128)(2,1)}, bf16[2,192,1536]{2,1,0:T(8,128)(2,1)}, u32[]{:S(2)}, u32[]{:S(2)}) collective-permute-start(bf16[2,192,1536]{2,1,0:T(8,128)(2,1)} %collective-permute-done.7.refs_2_), channel_id=1, source_target_pairs={{0,96},{1,25},{2,98},{3,27},{4,100},{5,29},{6,102},{7,31},{8,104},... | collective-permute-start | bytes 3538952 | tf_op jit(solution)/shard_map/ppermute | solution.py:25
  40.8 3.6 %shard_map.59.rel = bf16[4,4,192,512]{3,2,1,0:T(8,128)(2,1)S(1)} custom-call(s32[4]{0:T(128)S(1)} %pad_add_fusion.place, bf16[2,384,512]{2,1,0:T(8,128)(2,1)S(1)} %copy-done.1, bf16[3,384,512]{2,1,0:T(8,128)(2,1)} %constant_dynamic-update-slice_fusion.got, bf16[3,384,512]{2,1,0:T(8,128)(2,1)} %collective-permute-done.3.other), custom_call_target="tpu_custom_call" | custom-call | tf_op jit(solution)/shard_map/pallas_call | solution.py:125
  44.4 5.1 %shard_map.60.refs_0_ = f32[512,1536]{1,0:T(8,128)S(1)} custom-call(bf16[4,4,192,512]{3,2,1,0:T(8,128)(2,1)S(1)} %shard_map.59.rel, bf16[2,192,1536]{2,1,0:T(8,128)(2,1)S(1)} %pad_maximum_fusion.refs_0_, bf16[2,192,1536]{2,1,0:T(8,128)(2,1)S(1)} %pad_maximum_fusion.1.refs_1_, bf16[2,192,1536]{2,1,0:T(8,128)(2,1)} %collective-permute-done.7.refs_2_, ...), custom_call_target="tpu_custom_call" | custom-call | tf_op jit(solution)/shard_map/pallas_call | solution.py:161
  49.5 2.6 %collective-permute-done.10.refs_2_.refs_5_ = bf16[2,192,1536]{2,1,0:T(8,128)(2,1)S(1)} collective-permute-done((bf16[2,192,1536]{2,1,0:T(8,128)(2,1)S(1)}, bf16[2,192,1536]{2,1,0:T(8,128)(2,1)S(1)}, u32[]{:S(2)}, u32[]{:S(2)}) %collective-permute-start.10) | collective-permute-done | bytes 1179680 | tf_op jit(solution)/shard_map/ppermute | solution.py:25
  52.1 3.1 %shard_map.61.sums = f32[512,1536]{1,0:T(8,128)S(1)} custom-call(bf16[4,4,192,512]{3,2,1,0:T(8,128)(2,1)S(1)} %shard_map.59.rel, f32[512,1536]{1,0:T(8,128)S(1)} %shard_map.60.refs_0_, bf16[2,192,1536]{2,1,0:T(8,128)(2,1)} %collective-permute-done.9.refs_1_.refs_4_, bf16[2,192,1536]{2,1,0:T(8,128)(2,1)S(1)} %collective-permute-done.10.refs_2_.refs_5_), custom_call_target="tpu_custom_call" | custom-call | tf_op jit(solution)/shard_map/pallas_call | solution.py:161
  55.2 7.2 %collective-permute-done.11.refs_0_.refs_6_ = bf16[2,192,1536]{2,1,0:T(8,128)(2,1)} collective-permute-done((bf16[2,192,1536]{2,1,0:T(8,128)(2,1)}, bf16[2,192,1536]{2,1,0:T(8,128)(2,1)}, u32[]{:S(2)}, u32[]{:S(2)}) %collective-permute-start.11) | collective-permute-done | bytes 1179680 | tf_op jit(solution)/shard_map/ppermute | solution.py:25
  62.5 2.4 %collective-permute-done.12.refs_1_.refs_7_ = bf16[2,192,1536]{2,1,0:T(8,128)(2,1)} collective-permute-done((bf16[2,192,1536]{2,1,0:T(8,128)(2,1)}, bf16[2,192,1536]{2,1,0:T(8,128)(2,1)}, u32[]{:S(2)}, u32[]{:S(2)}) %collective-permute-start.12) | collective-permute-done | bytes 1179680 | tf_op jit(solution)/shard_map/ppermute | solution.py:25
  64.8 4.0 %shard_map.62 = (f32[512,1536]{1,0:T(8,128)S(1)}, bf16[512,1536]{1,0:T(8,128)(2,1)S(1)}) custom-call(bf16[4,4,192,512]{3,2,1,0:T(8,128)(2,1)S(1)} %shard_map.59.rel, f32[512,1536]{1,0:T(8,128)S(1)} %shard_map.61.sums, bf16[512,1536]{1,0:T(8,128)(2,1)S(1)} %copy-done.2, bf16[2,192,1536]{2,1,0:T(8,128)(2,1)} %collective-permute-done.11.refs_0_.refs_6_, ...), custom_call_target="tpu_custom_call" | custom-call | tf_op jit(solution)/shard_map/pallas_call | solution.py:189
  70.5 3.2 %collective-permute-start.14 = (bf16[2,192,1536]{2,1,0:T(8,128)(2,1)S(1)}, bf16[2,192,1536]{2,1,0:T(8,128)(2,1)S(1)}, u32[]{:S(2)}, u32[]{:S(2)}) collective-permute-start(bf16[2,192,1536]{2,1,0:T(8,128)(2,1)S(1)} %convolution_convert_fusion.2), channel_id=1, source_target_pairs={{0,96},{1,25},{2,98},{3,27},{4,100},{5,29},{6,102},{7,31},{8,104},... | collective-permute-start | bytes 3538952 | tf_op jit(solution)/shard_map/ppermute | solution.py:25
  75.4 2.0 %collective-permute-start.20 = (bf16[2,192,1536]{2,1,0:T(8,128)(2,1)S(1)}, bf16[2,192,1536]{2,1,0:T(8,128)(2,1)S(1)}, u32[]{:S(2)}, u32[]{:S(2)}) collective-permute-start(bf16[2,192,1536]{2,1,0:T(8,128)(2,1)S(1)} %convolution_convert_fusion.1), channel_id=1, source_target_pairs={{0,32},{1,9},{2,34},{3,11},{4,36},{5,13},{6,38},{7,15},{8,40},{9,1... | collective-permute-start | bytes 3538952 | tf_op jit(solution)/shard_map/ppermute | solution.py:25
  77.4 10.9 %shard_map.63 = (f32[1536,512]{1,0:T(8,128)S(1)}, bf16[1536,512]{1,0:T(8,128)(2,1)S(1)}) custom-call(s32[4]{0:T(128)S(1)} %pad_add_fusion.place, bf16[512,1536]{1,0:T(8,128)(2,1)S(1)} %get-tuple-element.22.g, bf16[2,192,1536]{2,1,0:T(8,128)(2,1)S(1)} %pad_maximum_fusion.refs_0_, bf16[2,192,1536]{2,1,0:T(8,128)(2,1)S(1)} %pad_maximum_fusion.1.refs_1_, ...), custom_call_target="tpu_custom_call" | custom-call | tf_op jit(solution)/shard_map/pallas_call | solution.py:276
  90.0 2.8 %collective-permute-start.22 = (bf16[2,192,1536]{2,1,0:T(8,128)(2,1)S(1)}, bf16[2,192,1536]{2,1,0:T(8,128)(2,1)S(1)}, u32[]{:S(2)}, u32[]{:S(2)}) collective-permute-start(bf16[2,192,1536]{2,1,0:T(8,128)(2,1)S(1)} %fusion.1), channel_id=1, source_target_pairs={{0,96},{1,25},{2,98},{3,27},{4,100},{5,29},{6,102},{7,31},{8,104},... | collective-permute-start | bytes 3538952 | tf_op jit(solution)/shard_map/ppermute | solution.py:25
  92.7 7.3 %collective-permute-done.21.down_low = bf16[2,192,1536]{2,1,0:T(8,128)(2,1)S(1)} collective-permute-done((bf16[2,192,1536]{2,1,0:T(8,128)(2,1)S(1)}, bf16[2,192,1536]{2,1,0:T(8,128)(2,1)S(1)}, u32[]{:S(2)}, u32[]{:S(2)}) %collective-permute-start.21) | collective-permute-done | bytes 1179680 | tf_op jit(solution)/shard_map/ppermute | solution.py:25
  100.5 12.2 %collective-permute-done.22.down_high = bf16[2,192,1536]{2,1,0:T(8,128)(2,1)S(1)} collective-permute-done((bf16[2,192,1536]{2,1,0:T(8,128)(2,1)S(1)}, bf16[2,192,1536]{2,1,0:T(8,128)(2,1)S(1)}, u32[]{:S(2)}, u32[]{:S(2)}) %collective-permute-start.22) | collective-permute-done | bytes 1179680 | tf_op jit(solution)/shard_map/ppermute | solution.py:25
  113.1 1.5 %shard_map.65 = (f32[192,1536]{1,0:T(8,128)S(1)}, bf16[192,1536]{1,0:T(8,128)(2,1)S(1)}, bf16[192,1536]{1,0:T(8,128)(2,1)S(1)}, bf16[192,1536]{1,0:T(8,128)(2,1)S(1)}) custom-call(bf16[4,4,192,512]{3,2,1,0:T(8,128)(2,1)S(1)} %shard_map.59.rel, bf16[512,1536]{1,0:T(8,128)(2,1)S(1)} %get-tuple-element.22.g, ...), custom_call_target="tpu_custom_call" | custom-call | tf_op jit(solution)/shard_map/pallas_call | solution.py:212
  114.7 1.6 %collective-permute-start.23 = (bf16[192,1536]{1,0:T(8,128)(2,1)S(1)}, bf16[192,1536]{1,0:T(8,128)(2,1)S(1)}, u32[]{:S(2)}, u32[]{:S(2)}) collective-permute-start(bf16[192,1536]{1,0:T(8,128)(2,1)S(1)} %get-tuple-element.32), channel_id=1, source_target_pairs={{0,16},{1,65},{2,18},{3,67},{4,20},{5,69},{6,22},{7,71},{8,24},{9,... | collective-permute-start | bytes 1769480 | tf_op jit(solution)/shard_map/ppermute | solution.py:25
  119.0 4.1 %collective-permute-start.18 = (bf16[384,512]{1,0:T(8,128)(2,1)S(1)}, bf16[384,512]{1,0:T(8,128)(2,1)S(1)}, u32[]{:S(2)}, u32[]{:S(2)}) collective-permute-start(bf16[384,512]{1,0:T(8,128)(2,1)S(1)} %get-tuple-element.37), channel_id=1, source_target_pairs={{0,6},{1,7},{2,0},{3,1},{4,2},{5,3},{6,4},{7,5},{8,14},{9,15},{10,... | collective-permute-start | bytes 1179656 | tf_op jit(solution)/shard_map/ppermute | solution.py:38
  123.1 3.2 %collective-permute-done.23.a = bf16[192,1536]{1,0:T(8,128)(2,1)S(1)} collective-permute-done((bf16[192,1536]{1,0:T(8,128)(2,1)S(1)}, bf16[192,1536]{1,0:T(8,128)(2,1)S(1)}, u32[]{:S(2)}, u32[]{:S(2)}) %collective-permute-start.23) | collective-permute-done | bytes 589856 | tf_op jit(solution)/shard_map/ppermute | solution.py:25
  126.3 1.9 %collective-permute-start.16 = (bf16[384,512]{1,0:T(8,128)(2,1)S(1)}, bf16[384,512]{1,0:T(8,128)(2,1)S(1)}, u32[]{:S(2)}, u32[]{:S(2)}) collective-permute-start(bf16[384,512]{1,0:T(8,128)(2,1)S(1)} %get-tuple-element.39), channel_id=1, source_target_pairs={{0,2},{1,3},{2,4},{3,5},{4,6},{5,7},{6,0},{7,1},{8,10},{9,11},{10,... | collective-permute-start | bytes 1179656 | tf_op jit(solution)/shard_map/ppermute | solution.py:38
  130.4 2.0 %collective-permute-done.25.c = bf16[192,1536]{1,0:T(8,128)(2,1)S(1)} collective-permute-done((bf16[192,1536]{1,0:T(8,128)(2,1)S(1)}, bf16[192,1536]{1,0:T(8,128)(2,1)S(1)}, u32[]{:S(2)}, u32[]{:S(2)}) %collective-permute-start.25) | collective-permute-done | bytes 589856 | tf_op jit(solution)/shard_map/ppermute | solution.py:25
  133.7 4.1 %collective-permute-done.18.c = bf16[384,512]{1,0:T(8,128)(2,1)S(1)} collective-permute-done((bf16[384,512]{1,0:T(8,128)(2,1)S(1)}, bf16[384,512]{1,0:T(8,128)(2,1)S(1)}, u32[]{:S(2)}, u32[]{:S(2)}) %collective-permute-start.18) | collective-permute-done | bytes 393248 | tf_op jit(solution)/shard_map/ppermute | solution.py:38
  137.8 3.7 %collective-permute-done.16.a = bf16[384,512]{1,0:T(8,128)(2,1)S(1)} collective-permute-done((bf16[384,512]{1,0:T(8,128)(2,1)S(1)}, bf16[384,512]{1,0:T(8,128)(2,1)S(1)}, u32[]{:S(2)}, u32[]{:S(2)}) %collective-permute-start.16) | collective-permute-done | bytes 393248 | tf_op jit(solution)/shard_map/ppermute | solution.py:38
  (56 shorter events, 21.7 us)
Async XLA Ops:
  0.6 11.8 %collective-permute-start.4 = (bf16[192,1536]{1,0:T(8,128)(2,1)}, bf16[192,1536]{1,0:T(8,128)(2,1)S(1)}, u32[]{:S(2)}, u32[]{:S(2)}) collective-permute-start(bf16[192,1536]{1,0:T(8,128)(2,1)} %param.4), channel_id=1, source_target_pairs={{0,16},{1,65},{2,18},{3,67},{4,20},{5,69},{6,22},{7,71},{8,24},{9,... | collective-permute-start | bytes 1769480 | tf_op jit(solution)/shard_map/ppermute | solution.py:25
  2.1 14.3 %collective-permute-start.6 = (bf16[192,1536]{1,0:T(8,128)(2,1)}, bf16[192,1536]{1,0:T(8,128)(2,1)S(1)}, u32[]{:S(2)}, u32[]{:S(2)}) collective-permute-start(bf16[192,1536]{1,0:T(8,128)(2,1)} %param.4), channel_id=1, source_target_pairs={{0,8},{1,33},{2,10},{3,35},{4,12},{5,37},{6,14},{7,39},{8,16},{9,4... | collective-permute-start | bytes 1769480 | tf_op jit(solution)/shard_map/ppermute | solution.py:25
  4.2 14.4 %collective-permute-start.5 = (bf16[192,1536]{1,0:T(8,128)(2,1)}, bf16[192,1536]{1,0:T(8,128)(2,1)S(1)}, u32[]{:S(2)}, u32[]{:S(2)}) collective-permute-start(bf16[192,1536]{1,0:T(8,128)(2,1)} %param.4), channel_id=1, source_target_pairs={{0,24},{1,97},{2,26},{3,99},{4,28},{5,101},{6,30},{7,103},{8,0},{9... | collective-permute-start | bytes 1769480 | tf_op jit(solution)/shard_map/ppermute | solution.py:25
  4.2 1.0 copy-start.3
  5.2 13.4 %copy-start.4 = (bf16[192,1536]{1,0:T(8,128)(2,1)S(1)}, bf16[192,1536]{1,0:T(8,128)(2,1)}, u32[]{:S(2)}) copy-start(bf16[192,1536]{1,0:T(8,128)(2,1)} %param.4) | copy-start | bytes 1769476
  5.4 3.4 %collective-permute-start = (bf16[384,512]{1,0:T(8,128)(2,1)S(1)}, bf16[384,512]{1,0:T(8,128)(2,1)S(1)}, u32[]{:S(2)}, u32[]{:S(2)}) collective-permute-start(bf16[384,512]{1,0:T(8,128)(2,1)S(1)} %shard_map.58), channel_id=1, source_target_pairs={{0,1},{1,0},{2,3},{3,2},{4,5},{5,4},{6,7},{7,6},{8,9},{9,8},{10,11... | collective-permute-start | bytes 1179656 | tf_op jit(solution)/shard_map/ppermute | solution.py:48
  8.8 13.1 %copy-start = (bf16[2,384,512]{2,1,0:T(8,128)(2,1)}, bf16[2,384,512]{2,1,0:T(8,128)(2,1)S(1)}, u32[]{:S(2)}) copy-start(bf16[2,384,512]{2,1,0:T(8,128)(2,1)S(1)} %pad_maximum_fusion.2.here) | copy-start | bytes 2359300
  8.8 14.1 %collective-permute-start.1 = (bf16[2,384,512]{2,1,0:T(8,128)(2,1)S(1)}, bf16[2,384,512]{2,1,0:T(8,128)(2,1)S(1)}, u32[]{:S(2)}, u32[]{:S(2)}) collective-permute-start(bf16[2,384,512]{2,1,0:T(8,128)(2,1)S(1)} %pad_maximum_fusion.2.here), channel_id=1, source_target_pairs={{0,2},{1,7},{2,4},{3,1},{4,6},{5,3},{6,0},{7,5},{8,10},{9,15},{10,... | collective-permute-start | bytes 2359304 | tf_op jit(solution)/shard_map/ppermute | solution.py:43
  18.7 17.2 %collective-permute-start.7 = (bf16[2,192,1536]{2,1,0:T(8,128)(2,1)S(1)}, bf16[2,192,1536]{2,1,0:T(8,128)(2,1)}, u32[]{:S(2)}, u32[]{:S(2)}) collective-permute-start(bf16[2,192,1536]{2,1,0:T(8,128)(2,1)S(1)} %pad_maximum_fusion.refs_0_), channel_id=1, source_target_pairs={{0,96},{1,25},{2,98},{3,27},{4,100},{5,29},{6,102},{7,31},{8,104},... | collective-permute-start | bytes 3538952 | tf_op jit(solution)/shard_map/ppermute | solution.py:25
  21.9 17.6 %collective-permute-start.8 = (bf16[2,192,1536]{2,1,0:T(8,128)(2,1)S(1)}, bf16[2,192,1536]{2,1,0:T(8,128)(2,1)}, u32[]{:S(2)}, u32[]{:S(2)}) collective-permute-start(bf16[2,192,1536]{2,1,0:T(8,128)(2,1)S(1)} %pad_maximum_fusion.1.refs_1_), channel_id=1, source_target_pairs={{0,32},{1,9},{2,34},{3,11},{4,36},{5,13},{6,38},{7,15},{8,40},{9,1... | collective-permute-start | bytes 3538952 | tf_op jit(solution)/shard_map/ppermute | solution.py:25
  22.9 9.1 %collective-permute-start.2 = (bf16[1,384,512]{2,1,0:T(8,128)(2,1)S(1)}, bf16[1,384,512]{2,1,0:T(8,128)(2,1)S(1)}, u32[]{:S(2)}, u32[]{:S(2)}) collective-permute-start(bf16[1,384,512]{2,1,0:T(8,128)(2,1)S(1)} %slice.48), channel_id=1, source_target_pairs={{0,2},{1,7},{2,4},{3,1},{4,6},{5,3},{6,0},{7,5},{8,10},{9,15},{10,... | collective-permute-start | bytes 1179656 | tf_op jit(solution)/shard_map/ppermute | solution.py:43
  32.7 6.9 %collective-permute-start.3 = (bf16[3,384,512]{2,1,0:T(8,128)(2,1)}, bf16[3,384,512]{2,1,0:T(8,128)(2,1)}, u32[]{:S(2)}, u32[]{:S(2)}) collective-permute-start(bf16[3,384,512]{2,1,0:T(8,128)(2,1)} %constant_dynamic-update-slice_fusion.got), channel_id=1, source_target_pairs={{0,1},{1,0},{2,3},{3,2},{4,5},{5,4},{6,7},{7,6},{8,9},{9,8},{10,11... | collective-permute-start | bytes 3538952 | tf_op jit(solution)/shard_map/ppermute | solution.py:48
  32.7 19.3 %collective-permute-start.10 = (bf16[2,192,1536]{2,1,0:T(8,128)(2,1)S(1)}, bf16[2,192,1536]{2,1,0:T(8,128)(2,1)S(1)}, u32[]{:S(2)}, u32[]{:S(2)}) collective-permute-start(bf16[2,192,1536]{2,1,0:T(8,128)(2,1)S(1)} %pad_maximum_fusion.refs_0_), channel_id=1, source_target_pairs={{0,32},{1,9},{2,34},{3,11},{4,36},{5,13},{6,38},{7,15},{8,40},{9,1... | collective-permute-start | bytes 3538952 | tf_op jit(solution)/shard_map/ppermute | solution.py:25
  33.3 18.8 %collective-permute-start.9 = (bf16[2,192,1536]{2,1,0:T(8,128)(2,1)S(1)}, bf16[2,192,1536]{2,1,0:T(8,128)(2,1)}, u32[]{:S(2)}, u32[]{:S(2)}) collective-permute-start(bf16[2,192,1536]{2,1,0:T(8,128)(2,1)S(1)} %pad_maximum_fusion.1.refs_1_), channel_id=1, source_target_pairs={{0,96},{1,25},{2,98},{3,27},{4,100},{5,29},{6,102},{7,31},{8,104},... | collective-permute-start | bytes 3538952 | tf_op jit(solution)/shard_map/ppermute | solution.py:25
  36.0 26.5 %collective-permute-start.11 = (bf16[2,192,1536]{2,1,0:T(8,128)(2,1)}, bf16[2,192,1536]{2,1,0:T(8,128)(2,1)}, u32[]{:S(2)}, u32[]{:S(2)}) collective-permute-start(bf16[2,192,1536]{2,1,0:T(8,128)(2,1)} %collective-permute-done.7.refs_2_), channel_id=1, source_target_pairs={{0,96},{1,25},{2,98},{3,27},{4,100},{5,29},{6,102},{7,31},{8,104},... | collective-permute-start | bytes 3538952 | tf_op jit(solution)/shard_map/ppermute | solution.py:25
  39.5 25.3 %collective-permute-start.12 = (bf16[2,192,1536]{2,1,0:T(8,128)(2,1)}, bf16[2,192,1536]{2,1,0:T(8,128)(2,1)}, u32[]{:S(2)}, u32[]{:S(2)}) collective-permute-start(bf16[2,192,1536]{2,1,0:T(8,128)(2,1)} %collective-permute-done.8.refs_3_), channel_id=1, source_target_pairs={{0,32},{1,9},{2,34},{3,11},{4,36},{5,13},{6,38},{7,15},{8,40},{9,1... | collective-permute-start | bytes 3538952 | tf_op jit(solution)/shard_map/ppermute | solution.py:25
  39.6 1.1 copy-start.1
  49.5 15.4 %copy-start.2 = (bf16[512,1536]{1,0:T(8,128)(2,1)S(1)}, bf16[512,1536]{1,0:T(8,128)(2,1)}, u32[]{:S(2)}) copy-start(bf16[512,1536]{1,0:T(8,128)(2,1)} %cot.1) | copy-start | bytes 4718596
  70.4 17.9 %collective-permute-start.13 = (bf16[2,192,1536]{2,1,0:T(8,128)(2,1)S(1)}, bf16[2,192,1536]{2,1,0:T(8,128)(2,1)S(1)}, u32[]{:S(2)}, u32[]{:S(2)}) collective-permute-start(bf16[2,192,1536]{2,1,0:T(8,128)(2,1)S(1)} %convolution_convert_fusion.3), channel_id=1, source_target_pairs={{0,32},{1,9},{2,34},{3,11},{4,36},{5,13},{6,38},{7,15},{8,40},{9,1... | collective-permute-start | bytes 3538952 | tf_op jit(solution)/shard_map/ppermute | solution.py:25
  70.5 17.8 %collective-permute-start.14 = (bf16[2,192,1536]{2,1,0:T(8,128)(2,1)S(1)}, bf16[2,192,1536]{2,1,0:T(8,128)(2,1)S(1)}, u32[]{:S(2)}, u32[]{:S(2)}) collective-permute-start(bf16[2,192,1536]{2,1,0:T(8,128)(2,1)S(1)} %convolution_convert_fusion.2), channel_id=1, source_target_pairs={{0,96},{1,25},{2,98},{3,27},{4,100},{5,29},{6,102},{7,31},{8,104},... | collective-permute-start | bytes 3538952 | tf_op jit(solution)/shard_map/ppermute | solution.py:25
  74.5 25.6 %collective-permute-start.21 = (bf16[2,192,1536]{2,1,0:T(8,128)(2,1)S(1)}, bf16[2,192,1536]{2,1,0:T(8,128)(2,1)S(1)}, u32[]{:S(2)}, u32[]{:S(2)}) collective-permute-start(bf16[2,192,1536]{2,1,0:T(8,128)(2,1)S(1)} %convolution_convert_fusion), channel_id=1, source_target_pairs={{0,96},{1,25},{2,98},{3,27},{4,100},{5,29},{6,102},{7,31},{8,104},... | collective-permute-start | bytes 3538952 | tf_op jit(solution)/shard_map/ppermute | solution.py:25
  75.4 25.1 %collective-permute-start.20 = (bf16[2,192,1536]{2,1,0:T(8,128)(2,1)S(1)}, bf16[2,192,1536]{2,1,0:T(8,128)(2,1)S(1)}, u32[]{:S(2)}, u32[]{:S(2)}) collective-permute-start(bf16[2,192,1536]{2,1,0:T(8,128)(2,1)S(1)} %convolution_convert_fusion.1), channel_id=1, source_target_pairs={{0,32},{1,9},{2,34},{3,11},{4,36},{5,13},{6,38},{7,15},{8,40},{9,1... | collective-permute-start | bytes 3538952 | tf_op jit(solution)/shard_map/ppermute | solution.py:25
  88.3 30.0 %collective-permute-start.15 = (bf16[1536,512]{1,0:T(8,128)(2,1)S(1)}, bf16[1536,512]{1,0:T(8,128)(2,1)S(1)}, u32[]{:S(2)}, u32[]{:S(2)}) collective-permute-start(bf16[1536,512]{1,0:T(8,128)(2,1)S(1)} %get-tuple-element.28), channel_id=1, source_target_pairs={{0,1},{1,0},{2,3},{3,2},{4,5},{5,4},{6,7},{7,6},{8,9},{9,8},{10,11... | collective-permute-start | bytes 4718600 | tf_op jit(solution)/shard_map/ppermute | solution.py:48
  90.0 22.7 %collective-permute-start.22 = (bf16[2,192,1536]{2,1,0:T(8,128)(2,1)S(1)}, bf16[2,192,1536]{2,1,0:T(8,128)(2,1)S(1)}, u32[]{:S(2)}, u32[]{:S(2)}) collective-permute-start(bf16[2,192,1536]{2,1,0:T(8,128)(2,1)S(1)} %fusion.1), channel_id=1, source_target_pairs={{0,96},{1,25},{2,98},{3,27},{4,100},{5,29},{6,102},{7,31},{8,104},... | collective-permute-start | bytes 3538952 | tf_op jit(solution)/shard_map/ppermute | solution.py:25
  92.7 20.4 %collective-permute-start.19 = (bf16[2,192,1536]{2,1,0:T(8,128)(2,1)S(1)}, bf16[2,192,1536]{2,1,0:T(8,128)(2,1)S(1)}, u32[]{:S(2)}, u32[]{:S(2)}) collective-permute-start(bf16[2,192,1536]{2,1,0:T(8,128)(2,1)S(1)} %fusion), channel_id=1, source_target_pairs={{0,32},{1,9},{2,34},{3,11},{4,36},{5,13},{6,38},{7,15},{8,40},{9,1... | collective-permute-start | bytes 3538952 | tf_op jit(solution)/shard_map/ppermute | solution.py:25
  114.7 11.6 %collective-permute-start.23 = (bf16[192,1536]{1,0:T(8,128)(2,1)S(1)}, bf16[192,1536]{1,0:T(8,128)(2,1)S(1)}, u32[]{:S(2)}, u32[]{:S(2)}) collective-permute-start(bf16[192,1536]{1,0:T(8,128)(2,1)S(1)} %get-tuple-element.32), channel_id=1, source_target_pairs={{0,16},{1,65},{2,18},{3,67},{4,20},{5,69},{6,22},{7,71},{8,24},{9,... | collective-permute-start | bytes 1769480 | tf_op jit(solution)/shard_map/ppermute | solution.py:25
  116.3 14.2 %collective-permute-start.24 = (bf16[192,1536]{1,0:T(8,128)(2,1)S(1)}, bf16[192,1536]{1,0:T(8,128)(2,1)S(1)}, u32[]{:S(2)}, u32[]{:S(2)}) collective-permute-start(bf16[192,1536]{1,0:T(8,128)(2,1)S(1)} %get-tuple-element.33), channel_id=1, source_target_pairs={{0,8},{1,33},{2,10},{3,35},{4,12},{5,37},{6,14},{7,39},{8,16},{9,4... | collective-permute-start | bytes 1769480 | tf_op jit(solution)/shard_map/ppermute | solution.py:25
  117.4 15.0 %collective-permute-start.25 = (bf16[192,1536]{1,0:T(8,128)(2,1)S(1)}, bf16[192,1536]{1,0:T(8,128)(2,1)S(1)}, u32[]{:S(2)}, u32[]{:S(2)}) collective-permute-start(bf16[192,1536]{1,0:T(8,128)(2,1)S(1)} %get-tuple-element.34), channel_id=1, source_target_pairs={{0,24},{1,97},{2,26},{3,99},{4,28},{5,101},{6,30},{7,103},{8,0},{9... | collective-permute-start | bytes 1769480 | tf_op jit(solution)/shard_map/ppermute | solution.py:25
  119.0 18.8 %collective-permute-start.18 = (bf16[384,512]{1,0:T(8,128)(2,1)S(1)}, bf16[384,512]{1,0:T(8,128)(2,1)S(1)}, u32[]{:S(2)}, u32[]{:S(2)}) collective-permute-start(bf16[384,512]{1,0:T(8,128)(2,1)S(1)} %get-tuple-element.37), channel_id=1, source_target_pairs={{0,6},{1,7},{2,0},{3,1},{4,2},{5,3},{6,4},{7,5},{8,14},{9,15},{10,... | collective-permute-start | bytes 1179656 | tf_op jit(solution)/shard_map/ppermute | solution.py:38
  123.1 14.7 %collective-permute-start.17 = (bf16[384,512]{1,0:T(8,128)(2,1)S(1)}, bf16[384,512]{1,0:T(8,128)(2,1)S(1)}, u32[]{:S(2)}, u32[]{:S(2)}) collective-permute-start(bf16[384,512]{1,0:T(8,128)(2,1)S(1)} %get-tuple-element.38), channel_id=1, source_target_pairs={{0,4},{1,5},{2,6},{3,7},{4,0},{5,1},{6,2},{7,3},{8,12},{9,13},{10,... | collective-permute-start | bytes 1179656 | tf_op jit(solution)/shard_map/ppermute | solution.py:38
  126.3 15.2 %collective-permute-start.16 = (bf16[384,512]{1,0:T(8,128)(2,1)S(1)}, bf16[384,512]{1,0:T(8,128)(2,1)S(1)}, u32[]{:S(2)}, u32[]{:S(2)}) collective-permute-start(bf16[384,512]{1,0:T(8,128)(2,1)S(1)} %get-tuple-element.39), channel_id=1, source_target_pairs={{0,2},{1,3},{2,4},{3,5},{4,6},{5,7},{6,0},{7,1},{8,10},{9,11},{10,... | collective-permute-start | bytes 1179656 | tf_op jit(solution)/shard_map/ppermute | solution.py:38

commit v5 on v4

--- a/solution.py
+++ b/solution.py
@@ -195,6 +195,40 @@
     )(rel, sums, cot, *pieces.values())
 
 
+def second_kernel(i, h, rel, g, got, out):
+    for k in (0, 1):
+        out[k] = (dot(rel[i, 2 * h + k], g[...], 1, 0) + got[k].astype(F32)).astype(BF)
+
+
+def second(i, h, rel, g, got):
+    return pl.pallas_call(
+        functools.partial(second_kernel, i, h),
+        out_shape=jax.ShapeDtypeStruct(got.shape, BF),
+        in_specs=whole(3),
+        out_specs=whole(1)[0],
+        **limits(0),
+    )(rel, g, got)
+
+
+def mix_kernel(kept, other, base, one, two, three):
+    rows = base.shape[0]
+    for k, out in enumerate((base, one, two, three)):
+        at = slice(k * rows, (k + 1) * rows)
+        out[...] = (kept[at] + other[at].astype(F32)).astype(out.dtype)
+
+
+def mix(kept, other):
+    rows, count = kept.shape[0] // N, kept.shape[1]
+    block = jax.ShapeDtypeStruct((rows, count), BF)
+    return pl.pallas_call(
+        mix_kernel,
+        out_shape=(jax.ShapeDtypeStruct((rows, count), F32), block, block, block),
+        in_specs=whole(2),
+        out_specs=tuple(whole(4)),
+        **limits(0),
+    )(kept, other)
+
+
 def own_kernel(rel, g, up_low, up_high, down_low, down_high, kept, *sent):
     for j in (2, 1, 3, 0):
         total = dot(rel[0, j], g[...], 1, 0)
@@ -315,17 +349,13 @@
     kept, given = input_partial(place, g, w)
     to_up, to_down, kept, given, held = tied(to_up, to_down, kept, given, held)
     activated = held.astype(BF)
-    up_low = (part(1, 0) + to_up.astype(F32)).astype(BF)
-    down_high = (part(3, 1) + to_down.astype(F32)).astype(BF)
-    up_low, down_high = big(up_low, 1), big(down_high, -1)
-
-    sums = (kept + swap_core(given).astype(F32)).reshape(N, 2 * depth, -1)
-    sent = sums.astype(BF)
-    z1, z3, z2 = shift_z(sent[1], 1), shift_z(sent[3], -1), shift_z(sent[2], 2)
-
+    up_low, down_high = big(second(1, 0, rel, g, to_up), 1), big(second(3, 1, rel, g, to_down), -1)
+
+    base, z1, z2, z3 = mix(kept, swap_core(given))
+    z1, z3, z2 = shift_z(z1, 1), shift_z(z3, -1), shift_z(z2, 2)
     total, sent_1, sent_2, sent_3 = own(rel, g, up_low, up_high, down_low, down_high)
     weight_grad = add_all(total, small(sent_2, 2), small(sent_1, 1), small(sent_3, -1))
-    input_grad = join(sums[0], z1, z2, z3)
+    input_grad = join(base, z1, z2, z3)
     return (activated, input_grad, weight_grad)
 
 

time: 143 us -> 141 us (0.986)
  waiting for transfers between devices: 63.6 us -> 58.8 us
  starting transfers between devices: 36.4 us -> 40 us
  Pallas kernels: 30.6 us -> 32.5 us
  matrix products: 4.65 us -> 3.08 us
    ppermute x3, starting transfers between devices: 6.01 us -> 9.59 us  [shift_z(): return lax.ppermute(block, 'col', pairs)]
    ppermute x18, waiting for transfers between devices: 46.7 us -> 43.5 us  [shift(): return lax.ppermute(block, ('row', 'col'), pairs)]
    pallas_call x0 -> x3, Pallas kernels: none -> 1.89 us  [the longest x2 1.56 us: second(): pl.pallas_call(functools.partial(second_kernel, i, h), out_shape=jax.Shap...]
    ppermute x3, waiting for transfers between devices: 7.73 us -> 6.07 us  [shift_z(): return lax.ppermute(block, 'col', pairs)]
    dot_general x6 -> x4, matrix products: 4.65 us -> 3.08 us  [dot(): lax.dot_general(a, b, (((ca,), (cb,)), ((), ())), preferred_element_type=...]
  transfers between devices with their start and end apart: 26 -> 26, of which waited for: 19 -> 19; matrix products, arithmetic and copies ran while one was open for 5% -> 4% of each run, Pallas kernels for 18% -> 20%
where the time goes in v5:
time: 141 us
  waiting for transfers between devices  58.8 us (42%)
  starting transfers between devices  40 us (28%)
  Pallas kernels  32.5 us (23%)
  local copies, waits for them, and re-layouts  3.88 us (3%)
  matrix products  3.08 us (2%)
  other arithmetic  1.69 us (1%)
    ppermute x18, waiting for transfers between devices, shift(): return lax.ppermute(block, ('row', 'col'), pairs)  43.5 us
    ppermute x18, starting transfers between devices, shift(): return lax.ppermute(block, ('row', 'col'), pairs)  25.3 us
    pallas_call x1, Pallas kernels, input_partial(): pl.pallas_call(functools.partial(input_kernel, tuple(pieces)), out_shape=...  10.9 us
    ppermute x3, starting transfers between devices, shift_z(): return lax.ppermute(block, 'col', pairs)  9.59 us
    pallas_call x2, Pallas kernels, add_sums(): pl.pallas_call(functools.partial(sum_kernel, tuple(pieces), len(firsts)),...  8.21 us
    ppermute x2, waiting for transfers between devices, spread_z(): return lax.ppermute(block, 'col', pairs)  7.83 us
    ppermute x3, waiting for transfers between devices, shift_z(): return lax.ppermute(block, 'col', pairs)  6.07 us
    pallas_call x1, Pallas kernels, finish(): pl.pallas_call(functools.partial(late_kernel, tuple(pieces)), out_shape=(...  3.99 us
  transfers between devices with their start and end apart: 26, of which 19 were waited for; matrix products, arithmetic and copies ran while one was open for 4% of the time, Pallas kernels for 20%

profile of v5, /device:TPU:6, one launch (start us, length us, event | category | flops | bytes accessed | tf_op | source)
XLA Modules:
  0.0 140.8 jit_solution(6016424627941412942)
XLA Ops:
  0.6 1.5 %collective-permute-start.4 = (bf16[192,1536]{1,0:T(8,128)(2,1)}, bf16[192,1536]{1,0:T(8,128)(2,1)S(1)}, u32[]{:S(2)}, u32[]{:S(2)}) collective-permute-start(bf16[192,1536]{1,0:T(8,128)(2,1)} %param.4), channel_id=1, source_target_pairs={{0,16},{1,65},{2,18},{3,67},{4,20},{5,69},{6,22},{7,71},{8,24},{9,... | collective-permute-start | bytes 1769480 | tf_op jit(solution)/shard_map/ppermute | solution.py:25
  2.1 2.1 %collective-permute-start.6 = (bf16[192,1536]{1,0:T(8,128)(2,1)}, bf16[192,1536]{1,0:T(8,128)(2,1)S(1)}, u32[]{:S(2)}, u32[]{:S(2)}) collective-permute-start(bf16[192,1536]{1,0:T(8,128)(2,1)} %param.4), channel_id=1, source_target_pairs={{0,8},{1,33},{2,10},{3,35},{4,12},{5,37},{6,14},{7,39},{8,16},{9,4... | collective-permute-start | bytes 1769480 | tf_op jit(solution)/shard_map/ppermute | solution.py:25
  5.4 2.0 %collective-permute-start = (bf16[384,512]{1,0:T(8,128)(2,1)S(1)}, bf16[384,512]{1,0:T(8,128)(2,1)S(1)}, u32[]{:S(2)}, u32[]{:S(2)}) collective-permute-start(bf16[384,512]{1,0:T(8,128)(2,1)S(1)} %shard_map.58), channel_id=1, source_target_pairs={{0,1},{1,0},{2,3},{3,2},{4,5},{5,4},{6,7},{7,6},{8,9},{9,8},{10,11... | collective-permute-start | bytes 1179656 | tf_op jit(solution)/shard_map/ppermute | solution.py:48
  7.4 1.3 collective-permute-done
  8.8 2.0 %collective-permute-start.1 = (bf16[2,384,512]{2,1,0:T(8,128)(2,1)S(1)}, bf16[2,384,512]{2,1,0:T(8,128)(2,1)S(1)}, u32[]{:S(2)}, u32[]{:S(2)}) collective-permute-start(bf16[2,384,512]{2,1,0:T(8,128)(2,1)S(1)} %pad_maximum_fusion.2.here), channel_id=1, source_target_pairs={{0,2},{1,7},{2,4},{3,1},{4,6},{5,3},{6,0},{7,5},{8,10},{9,15},{10,... | collective-permute-start | bytes 2359304 | tf_op jit(solution)/shard_map/ppermute | solution.py:43
  10.8 1.6 %collective-permute-done.4 = bf16[192,1536]{1,0:T(8,128)(2,1)S(1)} collective-permute-done((bf16[192,1536]{1,0:T(8,128)(2,1)}, bf16[192,1536]{1,0:T(8,128)(2,1)S(1)}, u32[]{:S(2)}, u32[]{:S(2)}) %collective-permute-start.4) | collective-permute-done | bytes 589856 | tf_op jit(solution)/shard_map/ppermute | solution.py:25
  12.4 4.0 %collective-permute-done.6 = bf16[192,1536]{1,0:T(8,128)(2,1)S(1)} collective-permute-done((bf16[192,1536]{1,0:T(8,128)(2,1)}, bf16[192,1536]{1,0:T(8,128)(2,1)S(1)}, u32[]{:S(2)}, u32[]{:S(2)}) %collective-permute-start.6) | collective-permute-done | bytes 589856 | tf_op jit(solution)/shard_map/ppermute | solution.py:25
  16.4 2.2 %collective-permute-done.5 = bf16[192,1536]{1,0:T(8,128)(2,1)S(1)} collective-permute-done((bf16[192,1536]{1,0:T(8,128)(2,1)}, bf16[192,1536]{1,0:T(8,128)(2,1)S(1)}, u32[]{:S(2)}, u32[]{:S(2)}) %collective-permute-start.5) | collective-permute-done | bytes 589856 | tf_op jit(solution)/shard_map/ppermute | solution.py:25
  18.8 3.1 %collective-permute-start.7 = (bf16[2,192,1536]{2,1,0:T(8,128)(2,1)S(1)}, bf16[2,192,1536]{2,1,0:T(8,128)(2,1)}, u32[]{:S(2)}, u32[]{:S(2)}) collective-permute-start(bf16[2,192,1536]{2,1,0:T(8,128)(2,1)S(1)} %pad_maximum_fusion.refs_0_), channel_id=1, source_target_pairs={{0,96},{1,25},{2,98},{3,27},{4,100},{5,29},{6,102},{7,31},{8,104},... | collective-permute-start | bytes 3538952 | tf_op jit(solution)/shard_map/ppermute | solution.py:25
  25.0 7.0 %collective-permute-done.2 = bf16[1,384,512]{2,1,0:T(8,128)(2,1)S(1)} collective-permute-done((bf16[1,384,512]{2,1,0:T(8,128)(2,1)S(1)}, bf16[1,384,512]{2,1,0:T(8,128)(2,1)S(1)}, u32[]{:S(2)}, u32[]{:S(2)}) %collective-permute-start.2) | collective-permute-done | bytes 393248 | tf_op jit(solution)/shard_map/ppermute | solution.py:43
  33.3 2.7 %collective-permute-start.9 = (bf16[2,192,1536]{2,1,0:T(8,128)(2,1)S(1)}, bf16[2,192,1536]{2,1,0:T(8,128)(2,1)}, u32[]{:S(2)}, u32[]{:S(2)}) collective-permute-start(bf16[2,192,1536]{2,1,0:T(8,128)(2,1)S(1)} %pad_maximum_fusion.1.refs_1_), channel_id=1, source_target_pairs={{0,96},{1,25},{2,98},{3,27},{4,100},{5,29},{6,102},{7,31},{8,104},... | collective-permute-start | bytes 3538952 | tf_op jit(solution)/shard_map/ppermute | solution.py:25
  36.0 3.4 %collective-permute-start.11 = (bf16[2,192,1536]{2,1,0:T(8,128)(2,1)}, bf16[2,192,1536]{2,1,0:T(8,128)(2,1)}, u32[]{:S(2)}, u32[]{:S(2)}) collective-permute-start(bf16[2,192,1536]{2,1,0:T(8,128)(2,1)} %collective-permute-done.7.refs_2_), channel_id=1, source_target_pairs={{0,96},{1,25},{2,98},{3,27},{4,100},{5,29},{6,102},{7,31},{8,104},... | collective-permute-start | bytes 3538952 | tf_op jit(solution)/shard_map/ppermute | solution.py:25
  40.8 3.6 %shard_map.59.rel = bf16[4,4,192,512]{3,2,1,0:T(8,128)(2,1)S(1)} custom-call(s32[4]{0:T(128)S(1)} %pad_add_fusion.place, bf16[2,384,512]{2,1,0:T(8,128)(2,1)S(1)} %copy-done.1, bf16[3,384,512]{2,1,0:T(8,128)(2,1)} %constant_dynamic-update-slice_fusion.got, bf16[3,384,512]{2,1,0:T(8,128)(2,1)} %collective-permute-done.3.other), custom_call_target="tpu_custom_call" | custom-call | tf_op jit(solution)/shard_map/pallas_call | solution.py:125
  44.4 5.1 %shard_map.60.refs_0_ = f32[512,1536]{1,0:T(8,128)S(1)} custom-call(bf16[4,4,192,512]{3,2,1,0:T(8,128)(2,1)S(1)} %shard_map.59.rel, bf16[2,192,1536]{2,1,0:T(8,128)(2,1)S(1)} %pad_maximum_fusion.refs_0_, bf16[2,192,1536]{2,1,0:T(8,128)(2,1)S(1)} %pad_maximum_fusion.1.refs_1_, bf16[2,192,1536]{2,1,0:T(8,128)(2,1)} %collective-permute-done.7.refs_2_, ...), custom_call_target="tpu_custom_call" | custom-call | tf_op jit(solution)/shard_map/pallas_call | solution.py:161
  49.5 2.6 %collective-permute-done.10.refs_2_.refs_5_ = bf16[2,192,1536]{2,1,0:T(8,128)(2,1)S(1)} collective-permute-done((bf16[2,192,1536]{2,1,0:T(8,128)(2,1)S(1)}, bf16[2,192,1536]{2,1,0:T(8,128)(2,1)S(1)}, u32[]{:S(2)}, u32[]{:S(2)}) %collective-permute-start.10) | collective-permute-done | bytes 1179680 | tf_op jit(solution)/shard_map/ppermute | solution.py:25
  52.1 3.1 %shard_map.61.sums = f32[512,1536]{1,0:T(8,128)S(1)} custom-call(bf16[4,4,192,512]{3,2,1,0:T(8,128)(2,1)S(1)} %shard_map.59.rel, f32[512,1536]{1,0:T(8,128)S(1)} %shard_map.60.refs_0_, bf16[2,192,1536]{2,1,0:T(8,128)(2,1)} %collective-permute-done.9.refs_1_.refs_4_, bf16[2,192,1536]{2,1,0:T(8,128)(2,1)S(1)} %collective-permute-done.10.refs_2_.refs_5_), custom_call_target="tpu_custom_call" | custom-call | tf_op jit(solution)/shard_map/pallas_call | solution.py:161
  55.2 7.2 %collective-permute-done.11.refs_0_.refs_6_ = bf16[2,192,1536]{2,1,0:T(8,128)(2,1)} collective-permute-done((bf16[2,192,1536]{2,1,0:T(8,128)(2,1)}, bf16[2,192,1536]{2,1,0:T(8,128)(2,1)}, u32[]{:S(2)}, u32[]{:S(2)}) %collective-permute-start.11) | collective-permute-done | bytes 1179680 | tf_op jit(solution)/shard_map/ppermute | solution.py:25
  62.5 2.4 %collective-permute-done.12.refs_1_.refs_7_ = bf16[2,192,1536]{2,1,0:T(8,128)(2,1)} collective-permute-done((bf16[2,192,1536]{2,1,0:T(8,128)(2,1)}, bf16[2,192,1536]{2,1,0:T(8,128)(2,1)}, u32[]{:S(2)}, u32[]{:S(2)}) %collective-permute-start.12) | collective-permute-done | bytes 1179680 | tf_op jit(solution)/shard_map/ppermute | solution.py:25
  64.8 4.0 %shard_map.62 = (f32[512,1536]{1,0:T(8,128)S(1)}, bf16[512,1536]{1,0:T(8,128)(2,1)S(1)}) custom-call(bf16[4,4,192,512]{3,2,1,0:T(8,128)(2,1)S(1)} %shard_map.59.rel, f32[512,1536]{1,0:T(8,128)S(1)} %shard_map.61.sums, bf16[512,1536]{1,0:T(8,128)(2,1)S(1)} %copy-done.2, bf16[2,192,1536]{2,1,0:T(8,128)(2,1)} %collective-permute-done.11.refs_0_.refs_6_, ...), custom_call_target="tpu_custom_call" | custom-call | tf_op jit(solution)/shard_map/pallas_call | solution.py:189
  70.5 3.2 %collective-permute-start.14 = (bf16[2,192,1536]{2,1,0:T(8,128)(2,1)S(1)}, bf16[2,192,1536]{2,1,0:T(8,128)(2,1)S(1)}, u32[]{:S(2)}, u32[]{:S(2)}) collective-permute-start(bf16[2,192,1536]{2,1,0:T(8,128)(2,1)S(1)} %convolution_convert_fusion.2), channel_id=1, source_target_pairs={{0,96},{1,25},{2,98},{3,27},{4,100},{5,29},{6,102},{7,31},{8,104},... | collective-permute-start | bytes 3538952 | tf_op jit(solution)/shard_map/ppermute | solution.py:25
  75.4 2.0 %collective-permute-start.20 = (bf16[2,192,1536]{2,1,0:T(8,128)(2,1)S(1)}, bf16[2,192,1536]{2,1,0:T(8,128)(2,1)S(1)}, u32[]{:S(2)}, u32[]{:S(2)}) collective-permute-start(bf16[2,192,1536]{2,1,0:T(8,128)(2,1)S(1)} %convolution_convert_fusion.1), channel_id=1, source_target_pairs={{0,32},{1,9},{2,34},{3,11},{4,36},{5,13},{6,38},{7,15},{8,40},{9,1... | collective-permute-start | bytes 3538952 | tf_op jit(solution)/shard_map/ppermute | solution.py:25
  77.4 10.9 %shard_map.63 = (f32[1536,512]{1,0:T(8,128)S(1)}, bf16[1536,512]{1,0:T(8,128)(2,1)S(1)}) custom-call(s32[4]{0:T(128)S(1)} %pad_add_fusion.place, bf16[512,1536]{1,0:T(8,128)(2,1)S(1)} %get-tuple-element.26.g, bf16[2,192,1536]{2,1,0:T(8,128)(2,1)S(1)} %pad_maximum_fusion.refs_0_, bf16[2,192,1536]{2,1,0:T(8,128)(2,1)S(1)} %pad_maximum_fusion.1.refs_1_, ...), custom_call_target="tpu_custom_call" | custom-call | tf_op jit(solution)/shard_map/pallas_call | solution.py:310
  89.9 2.9 %collective-permute-start.22 = (bf16[2,192,1536]{2,1,0:T(8,128)(2,1)S(1)}, bf16[2,192,1536]{2,1,0:T(8,128)(2,1)S(1)}, u32[]{:S(2)}, u32[]{:S(2)}) collective-permute-start(bf16[2,192,1536]{2,1,0:T(8,128)(2,1)S(1)} %shard_map.67), channel_id=1, source_target_pairs={{0,96},{1,25},{2,98},{3,27},{4,100},{5,29},{6,102},{7,31},{8,104},... | collective-permute-start | bytes 3538952 | tf_op jit(solution)/shard_map/ppermute | solution.py:25
  92.7 7.3 %collective-permute-done.21.down_low = bf16[2,192,1536]{2,1,0:T(8,128)(2,1)S(1)} collective-permute-done((bf16[2,192,1536]{2,1,0:T(8,128)(2,1)S(1)}, bf16[2,192,1536]{2,1,0:T(8,128)(2,1)S(1)}, u32[]{:S(2)}, u32[]{:S(2)}) %collective-permute-start.21) | collective-permute-done | bytes 1179680 | tf_op jit(solution)/shard_map/ppermute | solution.py:25
  100.5 12.2 %collective-permute-done.22.down_high = bf16[2,192,1536]{2,1,0:T(8,128)(2,1)S(1)} collective-permute-done((bf16[2,192,1536]{2,1,0:T(8,128)(2,1)S(1)}, bf16[2,192,1536]{2,1,0:T(8,128)(2,1)S(1)}, u32[]{:S(2)}, u32[]{:S(2)}) %collective-permute-start.22) | collective-permute-done | bytes 1179680 | tf_op jit(solution)/shard_map/ppermute | solution.py:25
  113.1 1.6 %shard_map.68 = (f32[192,1536]{1,0:T(8,128)S(1)}, bf16[192,1536]{1,0:T(8,128)(2,1)S(1)}, bf16[192,1536]{1,0:T(8,128)(2,1)S(1)}, bf16[192,1536]{1,0:T(8,128)(2,1)S(1)}) custom-call(bf16[4,4,192,512]{3,2,1,0:T(8,128)(2,1)S(1)} %shard_map.59.rel, bf16[512,1536]{1,0:T(8,128)(2,1)S(1)} %get-tuple-element.26.g, ...), custom_call_target="tpu_custom_call" | custom-call | tf_op jit(solution)/shard_map/pallas_call | solution.py:246
  114.7 1.6 %collective-permute-start.23 = (bf16[192,1536]{1,0:T(8,128)(2,1)S(1)}, bf16[192,1536]{1,0:T(8,128)(2,1)S(1)}, u32[]{:S(2)}, u32[]{:S(2)}) collective-permute-start(bf16[192,1536]{1,0:T(8,128)(2,1)S(1)} %get-tuple-element.40), channel_id=1, source_target_pairs={{0,16},{1,65},{2,18},{3,67},{4,20},{5,69},{6,22},{7,71},{8,24},{9,... | collective-permute-start | bytes 1769480 | tf_op jit(solution)/shard_map/ppermute | solution.py:25
  118.7 2.0 %collective-permute-start.16 = (bf16[384,512]{1,0:T(8,128)(2,1)S(1)}, bf16[384,512]{1,0:T(8,128)(2,1)S(1)}, u32[]{:S(2)}, u32[]{:S(2)}) collective-permute-start(bf16[384,512]{1,0:T(8,128)(2,1)S(1)} %get-tuple-element.34), channel_id=1, source_target_pairs={{0,2},{1,3},{2,4},{3,5},{4,6},{5,7},{6,0},{7,1},{8,10},{9,11},{10,... | collective-permute-start | bytes 1179656 | tf_op jit(solution)/shard_map/ppermute | solution.py:38
  120.6 3.6 %collective-permute-start.17 = (bf16[384,512]{1,0:T(8,128)(2,1)S(1)}, bf16[384,512]{1,0:T(8,128)(2,1)S(1)}, u32[]{:S(2)}, u32[]{:S(2)}) collective-permute-start(bf16[384,512]{1,0:T(8,128)(2,1)S(1)} %get-tuple-element.35), channel_id=1, source_target_pairs={{0,4},{1,5},{2,6},{3,7},{4,0},{5,1},{6,2},{7,3},{8,12},{9,13},{10,... | collective-permute-start | bytes 1179656 | tf_op jit(solution)/shard_map/ppermute | solution.py:38
  124.2 2.1 %collective-permute-done.23.a = bf16[192,1536]{1,0:T(8,128)(2,1)S(1)} collective-permute-done((bf16[192,1536]{1,0:T(8,128)(2,1)S(1)}, bf16[192,1536]{1,0:T(8,128)(2,1)S(1)}, u32[]{:S(2)}, u32[]{:S(2)}) %collective-permute-start.23) | collective-permute-done | bytes 589856 | tf_op jit(solution)/shard_map/ppermute | solution.py:25
  126.3 4.0 %collective-permute-start.18 = (bf16[384,512]{1,0:T(8,128)(2,1)S(1)}, bf16[384,512]{1,0:T(8,128)(2,1)S(1)}, u32[]{:S(2)}, u32[]{:S(2)}) collective-permute-start(bf16[384,512]{1,0:T(8,128)(2,1)S(1)} %get-tuple-element.36), channel_id=1, source_target_pairs={{0,6},{1,7},{2,0},{3,1},{4,2},{5,3},{6,4},{7,5},{8,14},{9,15},{10,... | collective-permute-start | bytes 1179656 | tf_op jit(solution)/shard_map/ppermute | solution.py:38
  134.1 5.2 %collective-permute-done.17.b = bf16[384,512]{1,0:T(8,128)(2,1)S(1)} collective-permute-done((bf16[384,512]{1,0:T(8,128)(2,1)S(1)}, bf16[384,512]{1,0:T(8,128)(2,1)S(1)}, u32[]{:S(2)}, u32[]{:S(2)}) %collective-permute-start.17) | collective-permute-done | bytes 393248 | tf_op jit(solution)/shard_map/ppermute | solution.py:38
  (54 shorter events, 20.6 us)
Async XLA Ops:
  0.6 11.8 %collective-permute-start.4 = (bf16[192,1536]{1,0:T(8,128)(2,1)}, bf16[192,1536]{1,0:T(8,128)(2,1)S(1)}, u32[]{:S(2)}, u32[]{:S(2)}) collective-permute-start(bf16[192,1536]{1,0:T(8,128)(2,1)} %param.4), channel_id=1, source_target_pairs={{0,16},{1,65},{2,18},{3,67},{4,20},{5,69},{6,22},{7,71},{8,24},{9,... | collective-permute-start | bytes 1769480 | tf_op jit(solution)/shard_map/ppermute | solution.py:25
  2.1 14.3 %collective-permute-start.6 = (bf16[192,1536]{1,0:T(8,128)(2,1)}, bf16[192,1536]{1,0:T(8,128)(2,1)S(1)}, u32[]{:S(2)}, u32[]{:S(2)}) collective-permute-start(bf16[192,1536]{1,0:T(8,128)(2,1)} %param.4), channel_id=1, source_target_pairs={{0,8},{1,33},{2,10},{3,35},{4,12},{5,37},{6,14},{7,39},{8,16},{9,4... | collective-permute-start | bytes 1769480 | tf_op jit(solution)/shard_map/ppermute | solution.py:25
  4.2 14.4 %collective-permute-start.5 = (bf16[192,1536]{1,0:T(8,128)(2,1)}, bf16[192,1536]{1,0:T(8,128)(2,1)S(1)}, u32[]{:S(2)}, u32[]{:S(2)}) collective-permute-start(bf16[192,1536]{1,0:T(8,128)(2,1)} %param.4), channel_id=1, source_target_pairs={{0,24},{1,97},{2,26},{3,99},{4,28},{5,101},{6,30},{7,103},{8,0},{9... | collective-permute-start | bytes 1769480 | tf_op jit(solution)/shard_map/ppermute | solution.py:25
  4.2 1.0 copy-start.3
  5.2 13.4 %copy-start.4 = (bf16[192,1536]{1,0:T(8,128)(2,1)S(1)}, bf16[192,1536]{1,0:T(8,128)(2,1)}, u32[]{:S(2)}) copy-start(bf16[192,1536]{1,0:T(8,128)(2,1)} %param.4) | copy-start | bytes 1769476
  5.4 3.4 %collective-permute-start = (bf16[384,512]{1,0:T(8,128)(2,1)S(1)}, bf16[384,512]{1,0:T(8,128)(2,1)S(1)}, u32[]{:S(2)}, u32[]{:S(2)}) collective-permute-start(bf16[384,512]{1,0:T(8,128)(2,1)S(1)} %shard_map.58), channel_id=1, source_target_pairs={{0,1},{1,0},{2,3},{3,2},{4,5},{5,4},{6,7},{7,6},{8,9},{9,8},{10,11... | collective-permute-start | bytes 1179656 | tf_op jit(solution)/shard_map/ppermute | solution.py:48
  8.8 9.9 %copy-start = (bf16[2,384,512]{2,1,0:T(8,128)(2,1)}, bf16[2,384,512]{2,1,0:T(8,128)(2,1)S(1)}, u32[]{:S(2)}) copy-start(bf16[2,384,512]{2,1,0:T(8,128)(2,1)S(1)} %pad_maximum_fusion.2.here) | copy-start | bytes 2359300
  8.8 14.1 %collective-permute-start.1 = (bf16[2,384,512]{2,1,0:T(8,128)(2,1)S(1)}, bf16[2,384,512]{2,1,0:T(8,128)(2,1)S(1)}, u32[]{:S(2)}, u32[]{:S(2)}) collective-permute-start(bf16[2,384,512]{2,1,0:T(8,128)(2,1)S(1)} %pad_maximum_fusion.2.here), channel_id=1, source_target_pairs={{0,2},{1,7},{2,4},{3,1},{4,6},{5,3},{6,0},{7,5},{8,10},{9,15},{10,... | collective-permute-start | bytes 2359304 | tf_op jit(solution)/shard_map/ppermute | solution.py:43
  18.8 17.2 %collective-permute-start.7 = (bf16[2,192,1536]{2,1,0:T(8,128)(2,1)S(1)}, bf16[2,192,1536]{2,1,0:T(8,128)(2,1)}, u32[]{:S(2)}, u32[]{:S(2)}) collective-permute-start(bf16[2,192,1536]{2,1,0:T(8,128)(2,1)S(1)} %pad_maximum_fusion.refs_0_), channel_id=1, source_target_pairs={{0,96},{1,25},{2,98},{3,27},{4,100},{5,29},{6,102},{7,31},{8,104},... | collective-permute-start | bytes 3538952 | tf_op jit(solution)/shard_map/ppermute | solution.py:25
  21.9 17.6 %collective-permute-start.8 = (bf16[2,192,1536]{2,1,0:T(8,128)(2,1)S(1)}, bf16[2,192,1536]{2,1,0:T(8,128)(2,1)}, u32[]{:S(2)}, u32[]{:S(2)}) collective-permute-start(bf16[2,192,1536]{2,1,0:T(8,128)(2,1)S(1)} %pad_maximum_fusion.1.refs_1_), channel_id=1, source_target_pairs={{0,32},{1,9},{2,34},{3,11},{4,36},{5,13},{6,38},{7,15},{8,40},{9,1... | collective-permute-start | bytes 3538952 | tf_op jit(solution)/shard_map/ppermute | solution.py:25
  22.9 9.1 %collective-permute-start.2 = (bf16[1,384,512]{2,1,0:T(8,128)(2,1)S(1)}, bf16[1,384,512]{2,1,0:T(8,128)(2,1)S(1)}, u32[]{:S(2)}, u32[]{:S(2)}) collective-permute-start(bf16[1,384,512]{2,1,0:T(8,128)(2,1)S(1)} %slice.20), channel_id=1, source_target_pairs={{0,2},{1,7},{2,4},{3,1},{4,6},{5,3},{6,0},{7,5},{8,10},{9,15},{10,... | collective-permute-start | bytes 1179656 | tf_op jit(solution)/shard_map/ppermute | solution.py:43
  32.7 6.9 %collective-permute-start.3 = (bf16[3,384,512]{2,1,0:T(8,128)(2,1)}, bf16[3,384,512]{2,1,0:T(8,128)(2,1)}, u32[]{:S(2)}, u32[]{:S(2)}) collective-permute-start(bf16[3,384,512]{2,1,0:T(8,128)(2,1)} %constant_dynamic-update-slice_fusion.got), channel_id=1, source_target_pairs={{0,1},{1,0},{2,3},{3,2},{4,5},{5,4},{6,7},{7,6},{8,9},{9,8},{10,11... | collective-permute-start | bytes 3538952 | tf_op jit(solution)/shard_map/ppermute | solution.py:48
  32.7 19.3 %collective-permute-start.10 = (bf16[2,192,1536]{2,1,0:T(8,128)(2,1)S(1)}, bf16[2,192,1536]{2,1,0:T(8,128)(2,1)S(1)}, u32[]{:S(2)}, u32[]{:S(2)}) collective-permute-start(bf16[2,192,1536]{2,1,0:T(8,128)(2,1)S(1)} %pad_maximum_fusion.refs_0_), channel_id=1, source_target_pairs={{0,32},{1,9},{2,34},{3,11},{4,36},{5,13},{6,38},{7,15},{8,40},{9,1... | collective-permute-start | bytes 3538952 | tf_op jit(solution)/shard_map/ppermute | solution.py:25
  33.3 18.8 %collective-permute-start.9 = (bf16[2,192,1536]{2,1,0:T(8,128)(2,1)S(1)}, bf16[2,192,1536]{2,1,0:T(8,128)(2,1)}, u32[]{:S(2)}, u32[]{:S(2)}) collective-permute-start(bf16[2,192,1536]{2,1,0:T(8,128)(2,1)S(1)} %pad_maximum_fusion.1.refs_1_), channel_id=1, source_target_pairs={{0,96},{1,25},{2,98},{3,27},{4,100},{5,29},{6,102},{7,31},{8,104},... | collective-permute-start | bytes 3538952 | tf_op jit(solution)/shard_map/ppermute | solution.py:25
  36.0 26.5 %collective-permute-start.11 = (bf16[2,192,1536]{2,1,0:T(8,128)(2,1)}, bf16[2,192,1536]{2,1,0:T(8,128)(2,1)}, u32[]{:S(2)}, u32[]{:S(2)}) collective-permute-start(bf16[2,192,1536]{2,1,0:T(8,128)(2,1)} %collective-permute-done.7.refs_2_), channel_id=1, source_target_pairs={{0,96},{1,25},{2,98},{3,27},{4,100},{5,29},{6,102},{7,31},{8,104},... | collective-permute-start | bytes 3538952 | tf_op jit(solution)/shard_map/ppermute | solution.py:25
  39.5 25.3 %collective-permute-start.12 = (bf16[2,192,1536]{2,1,0:T(8,128)(2,1)}, bf16[2,192,1536]{2,1,0:T(8,128)(2,1)}, u32[]{:S(2)}, u32[]{:S(2)}) collective-permute-start(bf16[2,192,1536]{2,1,0:T(8,128)(2,1)} %collective-permute-done.8.refs_3_), channel_id=1, source_target_pairs={{0,32},{1,9},{2,34},{3,11},{4,36},{5,13},{6,38},{7,15},{8,40},{9,1... | collective-permute-start | bytes 3538952 | tf_op jit(solution)/shard_map/ppermute | solution.py:25
  39.6 1.1 copy-start.1
  49.5 15.4 %copy-start.2 = (bf16[512,1536]{1,0:T(8,128)(2,1)S(1)}, bf16[512,1536]{1,0:T(8,128)(2,1)}, u32[]{:S(2)}) copy-start(bf16[512,1536]{1,0:T(8,128)(2,1)} %cot.1) | copy-start | bytes 4718596
  70.4 17.9 %collective-permute-start.13 = (bf16[2,192,1536]{2,1,0:T(8,128)(2,1)S(1)}, bf16[2,192,1536]{2,1,0:T(8,128)(2,1)S(1)}, u32[]{:S(2)}, u32[]{:S(2)}) collective-permute-start(bf16[2,192,1536]{2,1,0:T(8,128)(2,1)S(1)} %convolution_convert_fusion.3), channel_id=1, source_target_pairs={{0,32},{1,9},{2,34},{3,11},{4,36},{5,13},{6,38},{7,15},{8,40},{9,1... | collective-permute-start | bytes 3538952 | tf_op jit(solution)/shard_map/ppermute | solution.py:25
  70.5 17.8 %collective-permute-start.14 = (bf16[2,192,1536]{2,1,0:T(8,128)(2,1)S(1)}, bf16[2,192,1536]{2,1,0:T(8,128)(2,1)S(1)}, u32[]{:S(2)}, u32[]{:S(2)}) collective-permute-start(bf16[2,192,1536]{2,1,0:T(8,128)(2,1)S(1)} %convolution_convert_fusion.2), channel_id=1, source_target_pairs={{0,96},{1,25},{2,98},{3,27},{4,100},{5,29},{6,102},{7,31},{8,104},... | collective-permute-start | bytes 3538952 | tf_op jit(solution)/shard_map/ppermute | solution.py:25
  74.5 25.6 %collective-permute-start.21 = (bf16[2,192,1536]{2,1,0:T(8,128)(2,1)S(1)}, bf16[2,192,1536]{2,1,0:T(8,128)(2,1)S(1)}, u32[]{:S(2)}, u32[]{:S(2)}) collective-permute-start(bf16[2,192,1536]{2,1,0:T(8,128)(2,1)S(1)} %convolution_convert_fusion), channel_id=1, source_target_pairs={{0,96},{1,25},{2,98},{3,27},{4,100},{5,29},{6,102},{7,31},{8,104},... | collective-permute-start | bytes 3538952 | tf_op jit(solution)/shard_map/ppermute | solution.py:25
  75.4 25.1 %collective-permute-start.20 = (bf16[2,192,1536]{2,1,0:T(8,128)(2,1)S(1)}, bf16[2,192,1536]{2,1,0:T(8,128)(2,1)S(1)}, u32[]{:S(2)}, u32[]{:S(2)}) collective-permute-start(bf16[2,192,1536]{2,1,0:T(8,128)(2,1)S(1)} %convolution_convert_fusion.1), channel_id=1, source_target_pairs={{0,32},{1,9},{2,34},{3,11},{4,36},{5,13},{6,38},{7,15},{8,40},{9,1... | collective-permute-start | bytes 3538952 | tf_op jit(solution)/shard_map/ppermute | solution.py:25
  89.9 22.8 %collective-permute-start.22 = (bf16[2,192,1536]{2,1,0:T(8,128)(2,1)S(1)}, bf16[2,192,1536]{2,1,0:T(8,128)(2,1)S(1)}, u32[]{:S(2)}, u32[]{:S(2)}) collective-permute-start(bf16[2,192,1536]{2,1,0:T(8,128)(2,1)S(1)} %shard_map.67), channel_id=1, source_target_pairs={{0,96},{1,25},{2,98},{3,27},{4,100},{5,29},{6,102},{7,31},{8,104},... | collective-permute-start | bytes 3538952 | tf_op jit(solution)/shard_map/ppermute | solution.py:25
  92.7 20.4 %collective-permute-start.19 = (bf16[2,192,1536]{2,1,0:T(8,128)(2,1)S(1)}, bf16[2,192,1536]{2,1,0:T(8,128)(2,1)S(1)}, u32[]{:S(2)}, u32[]{:S(2)}) collective-permute-start(bf16[2,192,1536]{2,1,0:T(8,128)(2,1)S(1)} %shard_map.66), channel_id=1, source_target_pairs={{0,32},{1,9},{2,34},{3,11},{4,36},{5,13},{6,38},{7,15},{8,40},{9,1... | collective-permute-start | bytes 3538952 | tf_op jit(solution)/shard_map/ppermute | solution.py:25
  92.7 25.6 %collective-permute-start.15 = (bf16[1536,512]{1,0:T(8,128)(2,1)S(1)}, bf16[1536,512]{1,0:T(8,128)(2,1)S(1)}, u32[]{:S(2)}, u32[]{:S(2)}) collective-permute-start(bf16[1536,512]{1,0:T(8,128)(2,1)S(1)} %get-tuple-element.32), channel_id=1, source_target_pairs={{0,1},{1,0},{2,3},{3,2},{4,5},{5,4},{6,7},{7,6},{8,9},{9,8},{10,11... | collective-permute-start | bytes 4718600 | tf_op jit(solution)/shard_map/ppermute | solution.py:48
  114.7 11.6 %collective-permute-start.23 = (bf16[192,1536]{1,0:T(8,128)(2,1)S(1)}, bf16[192,1536]{1,0:T(8,128)(2,1)S(1)}, u32[]{:S(2)}, u32[]{:S(2)}) collective-permute-start(bf16[192,1536]{1,0:T(8,128)(2,1)S(1)} %get-tuple-element.40), channel_id=1, source_target_pairs={{0,16},{1,65},{2,18},{3,67},{4,20},{5,69},{6,22},{7,71},{8,24},{9,... | collective-permute-start | bytes 1769480 | tf_op jit(solution)/shard_map/ppermute | solution.py:25
  116.3 15.4 %collective-permute-start.24 = (bf16[192,1536]{1,0:T(8,128)(2,1)S(1)}, bf16[192,1536]{1,0:T(8,128)(2,1)S(1)}, u32[]{:S(2)}, u32[]{:S(2)}) collective-permute-start(bf16[192,1536]{1,0:T(8,128)(2,1)S(1)} %get-tuple-element.41), channel_id=1, source_target_pairs={{0,8},{1,33},{2,10},{3,35},{4,12},{5,37},{6,14},{7,39},{8,16},{9,4... | collective-permute-start | bytes 1769480 | tf_op jit(solution)/shard_map/ppermute | solution.py:25
  117.5 15.0 %collective-permute-start.25 = (bf16[192,1536]{1,0:T(8,128)(2,1)S(1)}, bf16[192,1536]{1,0:T(8,128)(2,1)S(1)}, u32[]{:S(2)}, u32[]{:S(2)}) collective-permute-start(bf16[192,1536]{1,0:T(8,128)(2,1)S(1)} %get-tuple-element.42), channel_id=1, source_target_pairs={{0,24},{1,97},{2,26},{3,99},{4,28},{5,101},{6,30},{7,103},{8,0},{9... | collective-permute-start | bytes 1769480 | tf_op jit(solution)/shard_map/ppermute | solution.py:25
  118.7 15.4 %collective-permute-start.16 = (bf16[384,512]{1,0:T(8,128)(2,1)S(1)}, bf16[384,512]{1,0:T(8,128)(2,1)S(1)}, u32[]{:S(2)}, u32[]{:S(2)}) collective-permute-start(bf16[384,512]{1,0:T(8,128)(2,1)S(1)} %get-tuple-element.34), channel_id=1, source_target_pairs={{0,2},{1,3},{2,4},{3,5},{4,6},{5,7},{6,0},{7,1},{8,10},{9,11},{10,... | collective-permute-start | bytes 1179656 | tf_op jit(solution)/shard_map/ppermute | solution.py:38
  120.6 18.7 %collective-permute-start.17 = (bf16[384,512]{1,0:T(8,128)(2,1)S(1)}, bf16[384,512]{1,0:T(8,128)(2,1)S(1)}, u32[]{:S(2)}, u32[]{:S(2)}) collective-permute-start(bf16[384,512]{1,0:T(8,128)(2,1)S(1)} %get-tuple-element.35), channel_id=1, source_target_pairs={{0,4},{1,5},{2,6},{3,7},{4,0},{5,1},{6,2},{7,3},{8,12},{9,13},{10,... | collective-permute-start | bytes 1179656 | tf_op jit(solution)/shard_map/ppermute | solution.py:38
  126.3 13.5 %collective-permute-start.18 = (bf16[384,512]{1,0:T(8,128)(2,1)S(1)}, bf16[384,512]{1,0:T(8,128)(2,1)S(1)}, u32[]{:S(2)}, u32[]{:S(2)}) collective-permute-start(bf16[384,512]{1,0:T(8,128)(2,1)S(1)} %get-tuple-element.36), channel_id=1, source_target_pairs={{0,6},{1,7},{2,0},{3,1},{4,2},{5,3},{6,4},{7,5},{8,14},{9,15},{10,... | collective-permute-start | bytes 1179656 | tf_op jit(solution)/shard_map/ppermute | solution.py:38

commit v6 on v5

--- a/solution.py
+++ b/solution.py
@@ -38,8 +38,8 @@
     return lax.ppermute(block, "col", pairs)
 
 
-def spread_z(block):
-    pairs = [(2 * z + core, 2 * ((z + 1 - 2 * core) % N) + core) for z in range(N) for core in range(2)]
+def spread_z(block, step=1):
+    pairs = [(2 * z + core, 2 * ((z + step - 2 * step * core) % N) + core) for z in range(N) for core in range(2)]
     return lax.ppermute(block, "col", pairs)
 
 
@@ -210,23 +210,24 @@
     )(rel, g, got)
 
 
-def mix_kernel(kept, other, base, one, two, three):
+def mix_kernel(place, kept, other, base, one, two, three):
     rows = base.shape[0]
-    for k, out in enumerate((base, one, two, three)):
-        at = slice(k * rows, (k + 1) * rows)
+    core = place[3]
+    for k, out in ((0, base), (1 + 2 * core, one), (2, two), (3 - 2 * core, three)):
+        at = pl.ds(pl.multiple_of(k * rows, rows), rows)
         out[...] = (kept[at] + other[at].astype(F32)).astype(out.dtype)
 
 
-def mix(kept, other):
+def mix(place, kept, other):
     rows, count = kept.shape[0] // N, kept.shape[1]
     block = jax.ShapeDtypeStruct((rows, count), BF)
     return pl.pallas_call(
         mix_kernel,
         out_shape=(jax.ShapeDtypeStruct((rows, count), F32), block, block, block),
-        in_specs=whole(2),
+        in_specs=[pl.BlockSpec(memory_space=pltpu.SMEM)] + whole(2),
         out_specs=tuple(whole(4)),
         **limits(0),
-    )(kept, other)
+    )(place, kept, other)
 
 
 def own_kernel(rel, g, up_low, up_high, down_low, down_high, kept, *sent):
@@ -351,8 +352,8 @@
     activated = held.astype(BF)
     up_low, down_high = big(second(1, 0, rel, g, to_up), 1), big(second(3, 1, rel, g, to_down), -1)
 
-    base, z1, z2, z3 = mix(kept, swap_core(given))
-    z1, z3, z2 = shift_z(z1, 1), shift_z(z3, -1), shift_z(z2, 2)
+    base, z1, z2, z3 = mix(place, kept, swap_core(given))
+    z1, z2, z3 = spread_z(z1), shift_z(z2, 2), spread_z(z3, -1)
     total, sent_1, sent_2, sent_3 = own(rel, g, up_low, up_high, down_low, down_high)
     weight_grad = add_all(total, small(sent_2, 2), small(sent_1, 1), small(sent_3, -1))
     input_grad = join(base, z1, z2, z3)

time: 141 us -> 143 us (1.014)
    ppermute x2 -> x4, starting transfers between devices: 3.13 us -> 9.15 us  [spread_z(): return lax.ppermute(block, 'col', pairs)]
    ppermute x3 -> x1, starting transfers between devices: 9.59 us -> 3.58 us  [shift_z(): return lax.ppermute(block, 'col', pairs)]
    ppermute x2 -> x4, waiting for transfers between devices: 7.83 us -> 12.6 us  [spread_z(): return lax.ppermute(block, 'col', pairs)]
    ppermute x3 -> x1, waiting for transfers between devices: 6.07 us -> 3 us  [shift_z(): return lax.ppermute(block, 'col', pairs)]
  transfers between devices with their start and end apart: 26 -> 26, of which waited for: 19 -> 18; matrix products, arithmetic and copies ran while one was open for 4% -> 3% of each run, Pallas kernels for 20% -> 20%
where the time goes in v6:
time: 143 us
  waiting for transfers between devices  60 us (42%)
  starting transfers between devices  40 us (28%)
  Pallas kernels  33 us (23%)
  local copies, waits for them, and re-layouts  3.88 us (3%)
  matrix products  3.08 us (2%)
  other arithmetic  1.69 us (1%)
    ppermute x18, waiting for transfers between devices, shift(): return lax.ppermute(block, ('row', 'col'), pairs)  43.1 us
    ppermute x18, starting transfers between devices, shift(): return lax.ppermute(block, ('row', 'col'), pairs)  25.3 us
    ppermute x4, waiting for transfers between devices, spread_z(): return lax.ppermute(block, 'col', pairs)  12.6 us
    pallas_call x1, Pallas kernels, input_partial(): pl.pallas_call(functools.partial(input_kernel, tuple(pieces)), out_shape=...  10.9 us
    ppermute x4, starting transfers between devices, spread_z(): return lax.ppermute(block, 'col', pairs)  9.15 us
    pallas_call x2, Pallas kernels, add_sums(): pl.pallas_call(functools.partial(sum_kernel, tuple(pieces), len(firsts)),...  8.21 us
    pallas_call x1, Pallas kernels, finish(): pl.pallas_call(functools.partial(late_kernel, tuple(pieces)), out_shape=(...  3.99 us
    pallas_call x1, Pallas kernels, arrange(): pl.pallas_call(arrange_kernel, out_shape=jax.ShapeDtypeStruct((N, N, rows...  3.61 us
  transfers between devices with their start and end apart: 26, of which 18 were waited for; matrix products, arithmetic and copies ran while one was open for 3% of the time, Pallas kernels for 20%

profile of v6, /device:TPU:6, one launch (start us, length us, event | category | flops | bytes accessed | tf_op | source)
XLA Modules:
  0.0 142.6 jit_solution(4961496618033595042)
XLA Ops:
  0.6 1.5 %collective-permute-start.4 = (bf16[192,1536]{1,0:T(8,128)(2,1)}, bf16[192,1536]{1,0:T(8,128)(2,1)S(1)}, u32[]{:S(2)}, u32[]{:S(2)}) collective-permute-start(bf16[192,1536]{1,0:T(8,128)(2,1)} %param.4), channel_id=1, source_target_pairs={{0,16},{1,65},{2,18},{3,67},{4,20},{5,69},{6,22},{7,71},{8,24},{9,... | collective-permute-start | bytes 1769480 | tf_op jit(solution)/shard_map/ppermute | solution.py:25
  2.1 2.1 %collective-permute-start.6 = (bf16[192,1536]{1,0:T(8,128)(2,1)}, bf16[192,1536]{1,0:T(8,128)(2,1)S(1)}, u32[]{:S(2)}, u32[]{:S(2)}) collective-permute-start(bf16[192,1536]{1,0:T(8,128)(2,1)} %param.4), channel_id=1, source_target_pairs={{0,8},{1,33},{2,10},{3,35},{4,12},{5,37},{6,14},{7,39},{8,16},{9,4... | collective-permute-start | bytes 1769480 | tf_op jit(solution)/shard_map/ppermute | solution.py:25
  5.4 2.0 %collective-permute-start = (bf16[384,512]{1,0:T(8,128)(2,1)S(1)}, bf16[384,512]{1,0:T(8,128)(2,1)S(1)}, u32[]{:S(2)}, u32[]{:S(2)}) collective-permute-start(bf16[384,512]{1,0:T(8,128)(2,1)S(1)} %shard_map.58), channel_id=1, source_target_pairs={{0,1},{1,0},{2,3},{3,2},{4,5},{5,4},{6,7},{7,6},{8,9},{9,8},{10,11... | collective-permute-start | bytes 1179656 | tf_op jit(solution)/shard_map/ppermute | solution.py:48
  8.8 2.0 %collective-permute-start.1 = (bf16[2,384,512]{2,1,0:T(8,128)(2,1)S(1)}, bf16[2,384,512]{2,1,0:T(8,128)(2,1)S(1)}, u32[]{:S(2)}, u32[]{:S(2)}) collective-permute-start(bf16[2,384,512]{2,1,0:T(8,128)(2,1)S(1)} %pad_maximum_fusion.2.here), channel_id=1, source_target_pairs={{0,2},{1,7},{2,4},{3,1},{4,6},{5,3},{6,0},{7,5},{8,10},{9,15},{10,... | collective-permute-start | bytes 2359304 | tf_op jit(solution)/shard_map/ppermute | solution.py:43
  10.8 1.6 %collective-permute-done.4 = bf16[192,1536]{1,0:T(8,128)(2,1)S(1)} collective-permute-done((bf16[192,1536]{1,0:T(8,128)(2,1)}, bf16[192,1536]{1,0:T(8,128)(2,1)S(1)}, u32[]{:S(2)}, u32[]{:S(2)}) %collective-permute-start.4) | collective-permute-done | bytes 589856 | tf_op jit(solution)/shard_map/ppermute | solution.py:25
  12.4 4.0 %collective-permute-done.6 = bf16[192,1536]{1,0:T(8,128)(2,1)S(1)} collective-permute-done((bf16[192,1536]{1,0:T(8,128)(2,1)}, bf16[192,1536]{1,0:T(8,128)(2,1)S(1)}, u32[]{:S(2)}, u32[]{:S(2)}) %collective-permute-start.6) | collective-permute-done | bytes 589856 | tf_op jit(solution)/shard_map/ppermute | solution.py:25
  16.4 2.2 %collective-permute-done.5 = bf16[192,1536]{1,0:T(8,128)(2,1)S(1)} collective-permute-done((bf16[192,1536]{1,0:T(8,128)(2,1)}, bf16[192,1536]{1,0:T(8,128)(2,1)S(1)}, u32[]{:S(2)}, u32[]{:S(2)}) %collective-permute-start.5) | collective-permute-done | bytes 589856 | tf_op jit(solution)/shard_map/ppermute | solution.py:25
  18.8 3.1 %collective-permute-start.7 = (bf16[2,192,1536]{2,1,0:T(8,128)(2,1)S(1)}, bf16[2,192,1536]{2,1,0:T(8,128)(2,1)}, u32[]{:S(2)}, u32[]{:S(2)}) collective-permute-start(bf16[2,192,1536]{2,1,0:T(8,128)(2,1)S(1)} %pad_maximum_fusion.refs_0_), channel_id=1, source_target_pairs={{0,96},{1,25},{2,98},{3,27},{4,100},{5,29},{6,102},{7,31},{8,104},... | collective-permute-start | bytes 3538952 | tf_op jit(solution)/shard_map/ppermute | solution.py:25
  25.0 7.0 %collective-permute-done.2 = bf16[1,384,512]{2,1,0:T(8,128)(2,1)S(1)} collective-permute-done((bf16[1,384,512]{2,1,0:T(8,128)(2,1)S(1)}, bf16[1,384,512]{2,1,0:T(8,128)(2,1)S(1)}, u32[]{:S(2)}, u32[]{:S(2)}) %collective-permute-start.2) | collective-permute-done | bytes 393248 | tf_op jit(solution)/shard_map/ppermute | solution.py:43
  33.3 2.7 %collective-permute-start.9 = (bf16[2,192,1536]{2,1,0:T(8,128)(2,1)S(1)}, bf16[2,192,1536]{2,1,0:T(8,128)(2,1)}, u32[]{:S(2)}, u32[]{:S(2)}) collective-permute-start(bf16[2,192,1536]{2,1,0:T(8,128)(2,1)S(1)} %pad_maximum_fusion.1.refs_1_), channel_id=1, source_target_pairs={{0,96},{1,25},{2,98},{3,27},{4,100},{5,29},{6,102},{7,31},{8,104},... | collective-permute-start | bytes 3538952 | tf_op jit(solution)/shard_map/ppermute | solution.py:25
  36.0 3.4 %collective-permute-start.11 = (bf16[2,192,1536]{2,1,0:T(8,128)(2,1)}, bf16[2,192,1536]{2,1,0:T(8,128)(2,1)}, u32[]{:S(2)}, u32[]{:S(2)}) collective-permute-start(bf16[2,192,1536]{2,1,0:T(8,128)(2,1)} %collective-permute-done.7.refs_2_), channel_id=1, source_target_pairs={{0,96},{1,25},{2,98},{3,27},{4,100},{5,29},{6,102},{7,31},{8,104},... | collective-permute-start | bytes 3538952 | tf_op jit(solution)/shard_map/ppermute | solution.py:25
  40.8 3.6 %shard_map.59.rel = bf16[4,4,192,512]{3,2,1,0:T(8,128)(2,1)S(1)} custom-call(s32[4]{0:T(128)S(1)} %pad_add_fusion.place, bf16[2,384,512]{2,1,0:T(8,128)(2,1)S(1)} %copy-done.1, bf16[3,384,512]{2,1,0:T(8,128)(2,1)} %constant_dynamic-update-slice_fusion.got, bf16[3,384,512]{2,1,0:T(8,128)(2,1)} %collective-permute-done.3.other), custom_call_target="tpu_custom_call" | custom-call | tf_op jit(solution)/shard_map/pallas_call | solution.py:125
  44.4 5.1 %shard_map.60.refs_0_ = f32[512,1536]{1,0:T(8,128)S(1)} custom-call(bf16[4,4,192,512]{3,2,1,0:T(8,128)(2,1)S(1)} %shard_map.59.rel, bf16[2,192,1536]{2,1,0:T(8,128)(2,1)S(1)} %pad_maximum_fusion.refs_0_, bf16[2,192,1536]{2,1,0:T(8,128)(2,1)S(1)} %pad_maximum_fusion.1.refs_1_, bf16[2,192,1536]{2,1,0:T(8,128)(2,1)} %collective-permute-done.7.refs_2_, ...), custom_call_target="tpu_custom_call" | custom-call | tf_op jit(solution)/shard_map/pallas_call | solution.py:161
  49.5 2.6 %collective-permute-done.10.refs_2_.refs_5_ = bf16[2,192,1536]{2,1,0:T(8,128)(2,1)S(1)} collective-permute-done((bf16[2,192,1536]{2,1,0:T(8,128)(2,1)S(1)}, bf16[2,192,1536]{2,1,0:T(8,128)(2,1)S(1)}, u32[]{:S(2)}, u32[]{:S(2)}) %collective-permute-start.10) | collective-permute-done | bytes 1179680 | tf_op jit(solution)/shard_map/ppermute | solution.py:25
  52.1 3.1 %shard_map.61.sums = f32[512,1536]{1,0:T(8,128)S(1)} custom-call(bf16[4,4,192,512]{3,2,1,0:T(8,128)(2,1)S(1)} %shard_map.59.rel, f32[512,1536]{1,0:T(8,128)S(1)} %shard_map.60.refs_0_, bf16[2,192,1536]{2,1,0:T(8,128)(2,1)} %collective-permute-done.9.refs_1_.refs_4_, bf16[2,192,1536]{2,1,0:T(8,128)(2,1)S(1)} %collective-permute-done.10.refs_2_.refs_5_), custom_call_target="tpu_custom_call" | custom-call | tf_op jit(solution)/shard_map/pallas_call | solution.py:161
  55.2 7.2 %collective-permute-done.11.refs_0_.refs_6_ = bf16[2,192,1536]{2,1,0:T(8,128)(2,1)} collective-permute-done((bf16[2,192,1536]{2,1,0:T(8,128)(2,1)}, bf16[2,192,1536]{2,1,0:T(8,128)(2,1)}, u32[]{:S(2)}, u32[]{:S(2)}) %collective-permute-start.11) | collective-permute-done | bytes 1179680 | tf_op jit(solution)/shard_map/ppermute | solution.py:25
  62.5 2.4 %collective-permute-done.12.refs_1_.refs_7_ = bf16[2,192,1536]{2,1,0:T(8,128)(2,1)} collective-permute-done((bf16[2,192,1536]{2,1,0:T(8,128)(2,1)}, bf16[2,192,1536]{2,1,0:T(8,128)(2,1)}, u32[]{:S(2)}, u32[]{:S(2)}) %collective-permute-start.12) | collective-permute-done | bytes 1179680 | tf_op jit(solution)/shard_map/ppermute | solution.py:25
  64.8 4.0 %shard_map.62 = (f32[512,1536]{1,0:T(8,128)S(1)}, bf16[512,1536]{1,0:T(8,128)(2,1)S(1)}) custom-call(bf16[4,4,192,512]{3,2,1,0:T(8,128)(2,1)S(1)} %shard_map.59.rel, f32[512,1536]{1,0:T(8,128)S(1)} %shard_map.61.sums, bf16[512,1536]{1,0:T(8,128)(2,1)S(1)} %copy-done.2, bf16[2,192,1536]{2,1,0:T(8,128)(2,1)} %collective-permute-done.11.refs_0_.refs_6_, ...), custom_call_target="tpu_custom_call" | custom-call | tf_op jit(solution)/shard_map/pallas_call | solution.py:189
  70.5 3.2 %collective-permute-start.14 = (bf16[2,192,1536]{2,1,0:T(8,128)(2,1)S(1)}, bf16[2,192,1536]{2,1,0:T(8,128)(2,1)S(1)}, u32[]{:S(2)}, u32[]{:S(2)}) collective-permute-start(bf16[2,192,1536]{2,1,0:T(8,128)(2,1)S(1)} %convolution_convert_fusion.2), channel_id=1, source_target_pairs={{0,96},{1,25},{2,98},{3,27},{4,100},{5,29},{6,102},{7,31},{8,104},... | collective-permute-start | bytes 3538952 | tf_op jit(solution)/shard_map/ppermute | solution.py:25
  75.4 2.0 %collective-permute-start.20 = (bf16[2,192,1536]{2,1,0:T(8,128)(2,1)S(1)}, bf16[2,192,1536]{2,1,0:T(8,128)(2,1)S(1)}, u32[]{:S(2)}, u32[]{:S(2)}) collective-permute-start(bf16[2,192,1536]{2,1,0:T(8,128)(2,1)S(1)} %convolution_convert_fusion.1), channel_id=1, source_target_pairs={{0,32},{1,9},{2,34},{3,11},{4,36},{5,13},{6,38},{7,15},{8,40},{9,1... | collective-permute-start | bytes 3538952 | tf_op jit(solution)/shard_map/ppermute | solution.py:25
  77.4 10.9 %shard_map.63 = (f32[1536,512]{1,0:T(8,128)S(1)}, bf16[1536,512]{1,0:T(8,128)(2,1)S(1)}) custom-call(s32[4]{0:T(128)S(1)} %pad_add_fusion.place, bf16[512,1536]{1,0:T(8,128)(2,1)S(1)} %get-tuple-element.26.g, bf16[2,192,1536]{2,1,0:T(8,128)(2,1)S(1)} %pad_maximum_fusion.refs_0_, bf16[2,192,1536]{2,1,0:T(8,128)(2,1)S(1)} %pad_maximum_fusion.1.refs_1_, ...), custom_call_target="tpu_custom_call" | custom-call | tf_op jit(solution)/shard_map/pallas_call | solution.py:311
  89.9 2.9 %collective-permute-start.22 = (bf16[2,192,1536]{2,1,0:T(8,128)(2,1)S(1)}, bf16[2,192,1536]{2,1,0:T(8,128)(2,1)S(1)}, u32[]{:S(2)}, u32[]{:S(2)}) collective-permute-start(bf16[2,192,1536]{2,1,0:T(8,128)(2,1)S(1)} %shard_map.67), channel_id=1, source_target_pairs={{0,96},{1,25},{2,98},{3,27},{4,100},{5,29},{6,102},{7,31},{8,104},... | collective-permute-start | bytes 3538952 | tf_op jit(solution)/shard_map/ppermute | solution.py:25
  92.7 7.3 %collective-permute-done.21.down_low = bf16[2,192,1536]{2,1,0:T(8,128)(2,1)S(1)} collective-permute-done((bf16[2,192,1536]{2,1,0:T(8,128)(2,1)S(1)}, bf16[2,192,1536]{2,1,0:T(8,128)(2,1)S(1)}, u32[]{:S(2)}, u32[]{:S(2)}) %collective-permute-start.21) | collective-permute-done | bytes 1179680 | tf_op jit(solution)/shard_map/ppermute | solution.py:25
  100.5 12.2 %collective-permute-done.22.down_high = bf16[2,192,1536]{2,1,0:T(8,128)(2,1)S(1)} collective-permute-done((bf16[2,192,1536]{2,1,0:T(8,128)(2,1)S(1)}, bf16[2,192,1536]{2,1,0:T(8,128)(2,1)S(1)}, u32[]{:S(2)}, u32[]{:S(2)}) %collective-permute-start.22) | collective-permute-done | bytes 1179680 | tf_op jit(solution)/shard_map/ppermute | solution.py:25
  113.1 1.5 %shard_map.68 = (f32[192,1536]{1,0:T(8,128)S(1)}, bf16[192,1536]{1,0:T(8,128)(2,1)S(1)}, bf16[192,1536]{1,0:T(8,128)(2,1)S(1)}, bf16[192,1536]{1,0:T(8,128)(2,1)S(1)}) custom-call(bf16[4,4,192,512]{3,2,1,0:T(8,128)(2,1)S(1)} %shard_map.59.rel, bf16[512,1536]{1,0:T(8,128)(2,1)S(1)} %get-tuple-element.26.g, ...), custom_call_target="tpu_custom_call" | custom-call | tf_op jit(solution)/shard_map/pallas_call | solution.py:247
  114.7 1.6 %collective-permute-start.23 = (bf16[192,1536]{1,0:T(8,128)(2,1)S(1)}, bf16[192,1536]{1,0:T(8,128)(2,1)S(1)}, u32[]{:S(2)}, u32[]{:S(2)}) collective-permute-start(bf16[192,1536]{1,0:T(8,128)(2,1)S(1)} %get-tuple-element.40), channel_id=1, source_target_pairs={{0,16},{1,65},{2,18},{3,67},{4,20},{5,69},{6,22},{7,71},{8,24},{9,... | collective-permute-start | bytes 1769480 | tf_op jit(solution)/shard_map/ppermute | solution.py:25
  119.1 2.0 %collective-permute-start.16 = (bf16[384,512]{1,0:T(8,128)(2,1)S(1)}, bf16[384,512]{1,0:T(8,128)(2,1)S(1)}, u32[]{:S(2)}, u32[]{:S(2)}) collective-permute-start(bf16[384,512]{1,0:T(8,128)(2,1)S(1)} %get-tuple-element.34), channel_id=1, source_target_pairs={{0,2},{1,7},{2,4},{3,1},{4,6},{5,3},{6,0},{7,5},{8,10},{9,15},{10,... | collective-permute-start | bytes 1179656 | tf_op jit(solution)/shard_map/ppermute | solution.py:43
  121.1 3.6 %collective-permute-start.17 = (bf16[384,512]{1,0:T(8,128)(2,1)S(1)}, bf16[384,512]{1,0:T(8,128)(2,1)S(1)}, u32[]{:S(2)}, u32[]{:S(2)}) collective-permute-start(bf16[384,512]{1,0:T(8,128)(2,1)S(1)} %get-tuple-element.35), channel_id=1, source_target_pairs={{0,4},{1,5},{2,6},{3,7},{4,0},{5,1},{6,2},{7,3},{8,12},{9,13},{10,... | collective-permute-start | bytes 1179656 | tf_op jit(solution)/shard_map/ppermute | solution.py:38
  124.7 1.6 %collective-permute-done.23.a = bf16[192,1536]{1,0:T(8,128)(2,1)S(1)} collective-permute-done((bf16[192,1536]{1,0:T(8,128)(2,1)S(1)}, bf16[192,1536]{1,0:T(8,128)(2,1)S(1)}, u32[]{:S(2)}, u32[]{:S(2)}) %collective-permute-start.23) | collective-permute-done | bytes 589856 | tf_op jit(solution)/shard_map/ppermute | solution.py:25
  126.3 4.0 %collective-permute-start.18 = (bf16[384,512]{1,0:T(8,128)(2,1)S(1)}, bf16[384,512]{1,0:T(8,128)(2,1)S(1)}, u32[]{:S(2)}, u32[]{:S(2)}) collective-permute-start(bf16[384,512]{1,0:T(8,128)(2,1)S(1)} %get-tuple-element.36), channel_id=1, source_target_pairs={{0,6},{1,3},{2,0},{3,5},{4,2},{5,7},{6,4},{7,1},{8,14},{9,11},{10,... | collective-permute-start | bytes 1179656 | tf_op jit(solution)/shard_map/ppermute | solution.py:43
  133.8 4.8 %collective-permute-done.16.a = bf16[384,512]{1,0:T(8,128)(2,1)S(1)} collective-permute-done((bf16[384,512]{1,0:T(8,128)(2,1)S(1)}, bf16[384,512]{1,0:T(8,128)(2,1)S(1)}, u32[]{:S(2)}, u32[]{:S(2)}) %collective-permute-start.16) | collective-permute-done | bytes 393248 | tf_op jit(solution)/shard_map/ppermute | solution.py:43
  138.6 3.0 %collective-permute-done.17.b = bf16[384,512]{1,0:T(8,128)(2,1)S(1)} collective-permute-done((bf16[384,512]{1,0:T(8,128)(2,1)S(1)}, bf16[384,512]{1,0:T(8,128)(2,1)S(1)}, u32[]{:S(2)}, u32[]{:S(2)}) %collective-permute-start.17) | collective-permute-done | bytes 393248 | tf_op jit(solution)/shard_map/ppermute | solution.py:38
  (54 shorter events, 21.7 us)
Async XLA Ops:
  0.6 11.8 %collective-permute-start.4 = (bf16[192,1536]{1,0:T(8,128)(2,1)}, bf16[192,1536]{1,0:T(8,128)(2,1)S(1)}, u32[]{:S(2)}, u32[]{:S(2)}) collective-permute-start(bf16[192,1536]{1,0:T(8,128)(2,1)} %param.4), channel_id=1, source_target_pairs={{0,16},{1,65},{2,18},{3,67},{4,20},{5,69},{6,22},{7,71},{8,24},{9,... | collective-permute-start | bytes 1769480 | tf_op jit(solution)/shard_map/ppermute | solution.py:25
  2.1 14.3 %collective-permute-start.6 = (bf16[192,1536]{1,0:T(8,128)(2,1)}, bf16[192,1536]{1,0:T(8,128)(2,1)S(1)}, u32[]{:S(2)}, u32[]{:S(2)}) collective-permute-start(bf16[192,1536]{1,0:T(8,128)(2,1)} %param.4), channel_id=1, source_target_pairs={{0,8},{1,33},{2,10},{3,35},{4,12},{5,37},{6,14},{7,39},{8,16},{9,4... | collective-permute-start | bytes 1769480 | tf_op jit(solution)/shard_map/ppermute | solution.py:25
  4.2 14.4 %collective-permute-start.5 = (bf16[192,1536]{1,0:T(8,128)(2,1)}, bf16[192,1536]{1,0:T(8,128)(2,1)S(1)}, u32[]{:S(2)}, u32[]{:S(2)}) collective-permute-start(bf16[192,1536]{1,0:T(8,128)(2,1)} %param.4), channel_id=1, source_target_pairs={{0,24},{1,97},{2,26},{3,99},{4,28},{5,101},{6,30},{7,103},{8,0},{9... | collective-permute-start | bytes 1769480 | tf_op jit(solution)/shard_map/ppermute | solution.py:25
  4.2 1.0 copy-start.3
  5.2 13.4 %copy-start.4 = (bf16[192,1536]{1,0:T(8,128)(2,1)S(1)}, bf16[192,1536]{1,0:T(8,128)(2,1)}, u32[]{:S(2)}) copy-start(bf16[192,1536]{1,0:T(8,128)(2,1)} %param.4) | copy-start | bytes 1769476
  5.4 3.4 %collective-permute-start = (bf16[384,512]{1,0:T(8,128)(2,1)S(1)}, bf16[384,512]{1,0:T(8,128)(2,1)S(1)}, u32[]{:S(2)}, u32[]{:S(2)}) collective-permute-start(bf16[384,512]{1,0:T(8,128)(2,1)S(1)} %shard_map.58), channel_id=1, source_target_pairs={{0,1},{1,0},{2,3},{3,2},{4,5},{5,4},{6,7},{7,6},{8,9},{9,8},{10,11... | collective-permute-start | bytes 1179656 | tf_op jit(solution)/shard_map/ppermute | solution.py:48
  8.8 9.9 %copy-start = (bf16[2,384,512]{2,1,0:T(8,128)(2,1)}, bf16[2,384,512]{2,1,0:T(8,128)(2,1)S(1)}, u32[]{:S(2)}) copy-start(bf16[2,384,512]{2,1,0:T(8,128)(2,1)S(1)} %pad_maximum_fusion.2.here) | copy-start | bytes 2359300
  8.8 14.1 %collective-permute-start.1 = (bf16[2,384,512]{2,1,0:T(8,128)(2,1)S(1)}, bf16[2,384,512]{2,1,0:T(8,128)(2,1)S(1)}, u32[]{:S(2)}, u32[]{:S(2)}) collective-permute-start(bf16[2,384,512]{2,1,0:T(8,128)(2,1)S(1)} %pad_maximum_fusion.2.here), channel_id=1, source_target_pairs={{0,2},{1,7},{2,4},{3,1},{4,6},{5,3},{6,0},{7,5},{8,10},{9,15},{10,... | collective-permute-start | bytes 2359304 | tf_op jit(solution)/shard_map/ppermute | solution.py:43
  18.8 17.2 %collective-permute-start.7 = (bf16[2,192,1536]{2,1,0:T(8,128)(2,1)S(1)}, bf16[2,192,1536]{2,1,0:T(8,128)(2,1)}, u32[]{:S(2)}, u32[]{:S(2)}) collective-permute-start(bf16[2,192,1536]{2,1,0:T(8,128)(2,1)S(1)} %pad_maximum_fusion.refs_0_), channel_id=1, source_target_pairs={{0,96},{1,25},{2,98},{3,27},{4,100},{5,29},{6,102},{7,31},{8,104},... | collective-permute-start | bytes 3538952 | tf_op jit(solution)/shard_map/ppermute | solution.py:25
  21.9 17.6 %collective-permute-start.8 = (bf16[2,192,1536]{2,1,0:T(8,128)(2,1)S(1)}, bf16[2,192,1536]{2,1,0:T(8,128)(2,1)}, u32[]{:S(2)}, u32[]{:S(2)}) collective-permute-start(bf16[2,192,1536]{2,1,0:T(8,128)(2,1)S(1)} %pad_maximum_fusion.1.refs_1_), channel_id=1, source_target_pairs={{0,32},{1,9},{2,34},{3,11},{4,36},{5,13},{6,38},{7,15},{8,40},{9,1... | collective-permute-start | bytes 3538952 | tf_op jit(solution)/shard_map/ppermute | solution.py:25
  22.9 9.1 %collective-permute-start.2 = (bf16[1,384,512]{2,1,0:T(8,128)(2,1)S(1)}, bf16[1,384,512]{2,1,0:T(8,128)(2,1)S(1)}, u32[]{:S(2)}, u32[]{:S(2)}) collective-permute-start(bf16[1,384,512]{2,1,0:T(8,128)(2,1)S(1)} %slice.20), channel_id=1, source_target_pairs={{0,2},{1,7},{2,4},{3,1},{4,6},{5,3},{6,0},{7,5},{8,10},{9,15},{10,... | collective-permute-start | bytes 1179656 | tf_op jit(solution)/shard_map/ppermute | solution.py:43
  32.7 6.9 %collective-permute-start.3 = (bf16[3,384,512]{2,1,0:T(8,128)(2,1)}, bf16[3,384,512]{2,1,0:T(8,128)(2,1)}, u32[]{:S(2)}, u32[]{:S(2)}) collective-permute-start(bf16[3,384,512]{2,1,0:T(8,128)(2,1)} %constant_dynamic-update-slice_fusion.got), channel_id=1, source_target_pairs={{0,1},{1,0},{2,3},{3,2},{4,5},{5,4},{6,7},{7,6},{8,9},{9,8},{10,11... | collective-permute-start | bytes 3538952 | tf_op jit(solution)/shard_map/ppermute | solution.py:48
  32.7 19.3 %collective-permute-start.10 = (bf16[2,192,1536]{2,1,0:T(8,128)(2,1)S(1)}, bf16[2,192,1536]{2,1,0:T(8,128)(2,1)S(1)}, u32[]{:S(2)}, u32[]{:S(2)}) collective-permute-start(bf16[2,192,1536]{2,1,0:T(8,128)(2,1)S(1)} %pad_maximum_fusion.refs_0_), channel_id=1, source_target_pairs={{0,32},{1,9},{2,34},{3,11},{4,36},{5,13},{6,38},{7,15},{8,40},{9,1... | collective-permute-start | bytes 3538952 | tf_op jit(solution)/shard_map/ppermute | solution.py:25
  33.3 18.8 %collective-permute-start.9 = (bf16[2,192,1536]{2,1,0:T(8,128)(2,1)S(1)}, bf16[2,192,1536]{2,1,0:T(8,128)(2,1)}, u32[]{:S(2)}, u32[]{:S(2)}) collective-permute-start(bf16[2,192,1536]{2,1,0:T(8,128)(2,1)S(1)} %pad_maximum_fusion.1.refs_1_), channel_id=1, source_target_pairs={{0,96},{1,25},{2,98},{3,27},{4,100},{5,29},{6,102},{7,31},{8,104},... | collective-permute-start | bytes 3538952 | tf_op jit(solution)/shard_map/ppermute | solution.py:25
  36.0 26.5 %collective-permute-start.11 = (bf16[2,192,1536]{2,1,0:T(8,128)(2,1)}, bf16[2,192,1536]{2,1,0:T(8,128)(2,1)}, u32[]{:S(2)}, u32[]{:S(2)}) collective-permute-start(bf16[2,192,1536]{2,1,0:T(8,128)(2,1)} %collective-permute-done.7.refs_2_), channel_id=1, source_target_pairs={{0,96},{1,25},{2,98},{3,27},{4,100},{5,29},{6,102},{7,31},{8,104},... | collective-permute-start | bytes 3538952 | tf_op jit(solution)/shard_map/ppermute | solution.py:25
  39.5 25.3 %collective-permute-start.12 = (bf16[2,192,1536]{2,1,0:T(8,128)(2,1)}, bf16[2,192,1536]{2,1,0:T(8,128)(2,1)}, u32[]{:S(2)}, u32[]{:S(2)}) collective-permute-start(bf16[2,192,1536]{2,1,0:T(8,128)(2,1)} %collective-permute-done.8.refs_3_), channel_id=1, source_target_pairs={{0,32},{1,9},{2,34},{3,11},{4,36},{5,13},{6,38},{7,15},{8,40},{9,1... | collective-permute-start | bytes 3538952 | tf_op jit(solution)/shard_map/ppermute | solution.py:25
  39.6 1.1 copy-start.1
  49.5 15.4 %copy-start.2 = (bf16[512,1536]{1,0:T(8,128)(2,1)S(1)}, bf16[512,1536]{1,0:T(8,128)(2,1)}, u32[]{:S(2)}) copy-start(bf16[512,1536]{1,0:T(8,128)(2,1)} %cot.1) | copy-start | bytes 4718596
  70.4 17.9 %collective-permute-start.13 = (bf16[2,192,1536]{2,1,0:T(8,128)(2,1)S(1)}, bf16[2,192,1536]{2,1,0:T(8,128)(2,1)S(1)}, u32[]{:S(2)}, u32[]{:S(2)}) collective-permute-start(bf16[2,192,1536]{2,1,0:T(8,128)(2,1)S(1)} %convolution_convert_fusion.3), channel_id=1, source_target_pairs={{0,32},{1,9},{2,34},{3,11},{4,36},{5,13},{6,38},{7,15},{8,40},{9,1... | collective-permute-start | bytes 3538952 | tf_op jit(solution)/shard_map/ppermute | solution.py:25
  70.5 17.8 %collective-permute-start.14 = (bf16[2,192,1536]{2,1,0:T(8,128)(2,1)S(1)}, bf16[2,192,1536]{2,1,0:T(8,128)(2,1)S(1)}, u32[]{:S(2)}, u32[]{:S(2)}) collective-permute-start(bf16[2,192,1536]{2,1,0:T(8,128)(2,1)S(1)} %convolution_convert_fusion.2), channel_id=1, source_target_pairs={{0,96},{1,25},{2,98},{3,27},{4,100},{5,29},{6,102},{7,31},{8,104},... | collective-permute-start | bytes 3538952 | tf_op jit(solution)/shard_map/ppermute | solution.py:25
  74.5 25.6 %collective-permute-start.21 = (bf16[2,192,1536]{2,1,0:T(8,128)(2,1)S(1)}, bf16[2,192,1536]{2,1,0:T(8,128)(2,1)S(1)}, u32[]{:S(2)}, u32[]{:S(2)}) collective-permute-start(bf16[2,192,1536]{2,1,0:T(8,128)(2,1)S(1)} %convolution_convert_fusion), channel_id=1, source_target_pairs={{0,96},{1,25},{2,98},{3,27},{4,100},{5,29},{6,102},{7,31},{8,104},... | collective-permute-start | bytes 3538952 | tf_op jit(solution)/shard_map/ppermute | solution.py:25
  75.4 25.1 %collective-permute-start.20 = (bf16[2,192,1536]{2,1,0:T(8,128)(2,1)S(1)}, bf16[2,192,1536]{2,1,0:T(8,128)(2,1)S(1)}, u32[]{:S(2)}, u32[]{:S(2)}) collective-permute-start(bf16[2,192,1536]{2,1,0:T(8,128)(2,1)S(1)} %convolution_convert_fusion.1), channel_id=1, source_target_pairs={{0,32},{1,9},{2,34},{3,11},{4,36},{5,13},{6,38},{7,15},{8,40},{9,1... | collective-permute-start | bytes 3538952 | tf_op jit(solution)/shard_map/ppermute | solution.py:25
  89.9 22.8 %collective-permute-start.22 = (bf16[2,192,1536]{2,1,0:T(8,128)(2,1)S(1)}, bf16[2,192,1536]{2,1,0:T(8,128)(2,1)S(1)}, u32[]{:S(2)}, u32[]{:S(2)}) collective-permute-start(bf16[2,192,1536]{2,1,0:T(8,128)(2,1)S(1)} %shard_map.67), channel_id=1, source_target_pairs={{0,96},{1,25},{2,98},{3,27},{4,100},{5,29},{6,102},{7,31},{8,104},... | collective-permute-start | bytes 3538952 | tf_op jit(solution)/shard_map/ppermute | solution.py:25
  92.7 20.4 %collective-permute-start.19 = (bf16[2,192,1536]{2,1,0:T(8,128)(2,1)S(1)}, bf16[2,192,1536]{2,1,0:T(8,128)(2,1)S(1)}, u32[]{:S(2)}, u32[]{:S(2)}) collective-permute-start(bf16[2,192,1536]{2,1,0:T(8,128)(2,1)S(1)} %shard_map.66), channel_id=1, source_target_pairs={{0,32},{1,9},{2,34},{3,11},{4,36},{5,13},{6,38},{7,15},{8,40},{9,1... | collective-permute-start | bytes 3538952 | tf_op jit(solution)/shard_map/ppermute | solution.py:25
  92.7 25.5 %collective-permute-start.15 = (bf16[1536,512]{1,0:T(8,128)(2,1)S(1)}, bf16[1536,512]{1,0:T(8,128)(2,1)S(1)}, u32[]{:S(2)}, u32[]{:S(2)}) collective-permute-start(bf16[1536,512]{1,0:T(8,128)(2,1)S(1)} %get-tuple-element.32), channel_id=1, source_target_pairs={{0,1},{1,0},{2,3},{3,2},{4,5},{5,4},{6,7},{7,6},{8,9},{9,8},{10,11... | collective-permute-start | bytes 4718600 | tf_op jit(solution)/shard_map/ppermute | solution.py:48
  114.7 11.6 %collective-permute-start.23 = (bf16[192,1536]{1,0:T(8,128)(2,1)S(1)}, bf16[192,1536]{1,0:T(8,128)(2,1)S(1)}, u32[]{:S(2)}, u32[]{:S(2)}) collective-permute-start(bf16[192,1536]{1,0:T(8,128)(2,1)S(1)} %get-tuple-element.40), channel_id=1, source_target_pairs={{0,16},{1,65},{2,18},{3,67},{4,20},{5,69},{6,22},{7,71},{8,24},{9,... | collective-permute-start | bytes 1769480 | tf_op jit(solution)/shard_map/ppermute | solution.py:25
  116.3 15.4 %collective-permute-start.24 = (bf16[192,1536]{1,0:T(8,128)(2,1)S(1)}, bf16[192,1536]{1,0:T(8,128)(2,1)S(1)}, u32[]{:S(2)}, u32[]{:S(2)}) collective-permute-start(bf16[192,1536]{1,0:T(8,128)(2,1)S(1)} %get-tuple-element.41), channel_id=1, source_target_pairs={{0,8},{1,33},{2,10},{3,35},{4,12},{5,37},{6,14},{7,39},{8,16},{9,4... | collective-permute-start | bytes 1769480 | tf_op jit(solution)/shard_map/ppermute | solution.py:25
  117.4 15.0 %collective-permute-start.25 = (bf16[192,1536]{1,0:T(8,128)(2,1)S(1)}, bf16[192,1536]{1,0:T(8,128)(2,1)S(1)}, u32[]{:S(2)}, u32[]{:S(2)}) collective-permute-start(bf16[192,1536]{1,0:T(8,128)(2,1)S(1)} %get-tuple-element.42), channel_id=1, source_target_pairs={{0,24},{1,97},{2,26},{3,99},{4,28},{5,101},{6,30},{7,103},{8,0},{9... | collective-permute-start | bytes 1769480 | tf_op jit(solution)/shard_map/ppermute | solution.py:25
  119.1 19.5 %collective-permute-start.16 = (bf16[384,512]{1,0:T(8,128)(2,1)S(1)}, bf16[384,512]{1,0:T(8,128)(2,1)S(1)}, u32[]{:S(2)}, u32[]{:S(2)}) collective-permute-start(bf16[384,512]{1,0:T(8,128)(2,1)S(1)} %get-tuple-element.34), channel_id=1, source_target_pairs={{0,2},{1,7},{2,4},{3,1},{4,6},{5,3},{6,0},{7,5},{8,10},{9,15},{10,... | collective-permute-start | bytes 1179656 | tf_op jit(solution)/shard_map/ppermute | solution.py:43
  121.1 20.5 %collective-permute-start.17 = (bf16[384,512]{1,0:T(8,128)(2,1)S(1)}, bf16[384,512]{1,0:T(8,128)(2,1)S(1)}, u32[]{:S(2)}, u32[]{:S(2)}) collective-permute-start(bf16[384,512]{1,0:T(8,128)(2,1)S(1)} %get-tuple-element.35), channel_id=1, source_target_pairs={{0,4},{1,5},{2,6},{3,7},{4,0},{5,1},{6,2},{7,3},{8,12},{9,13},{10,... | collective-permute-start | bytes 1179656 | tf_op jit(solution)/shard_map/ppermute | solution.py:38
  126.3 15.3 %collective-permute-start.18 = (bf16[384,512]{1,0:T(8,128)(2,1)S(1)}, bf16[384,512]{1,0:T(8,128)(2,1)S(1)}, u32[]{:S(2)}, u32[]{:S(2)}) collective-permute-start(bf16[384,512]{1,0:T(8,128)(2,1)S(1)} %get-tuple-element.36), channel_id=1, source_target_pairs={{0,6},{1,3},{2,0},{3,5},{4,2},{5,7},{6,4},{7,1},{8,14},{9,11},{10,... | collective-permute-start | bytes 1179656 | tf_op jit(solution)/shard_map/ppermute | solution.py:43

commit v7 on v5

--- a/solution.py
+++ b/solution.py
@@ -229,25 +229,25 @@
     )(kept, other)
 
 
-def own_kernel(rel, g, up_low, up_high, down_low, down_high, kept, *sent):
-    for j in (2, 1, 3, 0):
-        total = dot(rel[0, j], g[...], 1, 0)
-        for low, high in ((up_low, up_high), (down_low, down_high)):
-            total += (low if j < 2 else high)[j % 2].astype(F32)
-        if j == 0:
-            kept[...] = total
-        else:
-            sent[j - 1][...] = total.astype(BF)
-
-
-def own(rel, g, *arrived):
-    depth, width = rel.shape[2], g.shape[1]
-    block = jax.ShapeDtypeStruct((depth, width), BF)
-    return pl.pallas_call(
-        own_kernel,
-        out_shape=(jax.ShapeDtypeStruct((depth, width), F32), block, block, block),
+def own_sums(j, rel, g, up_low, up_high, down_low, down_high):
+    total = dot(rel[0, j], g[...], 1, 0)
+    for low, high in ((up_low, up_high), (down_low, down_high)):
+        total += (low if j < 2 else high)[j % 2].astype(F32)
+    return total
+
+
+def own_kernel(steps, *refs):
+    for j, out in zip(steps, refs[6:]):
+        out[...] = own_sums(j, *refs[:6]).astype(out.dtype)
+
+
+def own(steps, rel, g, *arrived):
+    shape = (rel.shape[2], g.shape[1])
+    return pl.pallas_call(
+        functools.partial(own_kernel, steps),
+        out_shape=tuple(jax.ShapeDtypeStruct(shape, BF if j else F32) for j in steps),
         in_specs=whole(6),
-        out_specs=tuple(whole(4)),
+        out_specs=tuple(whole(len(steps))),
         **limits(0),
     )(rel, g, *arrived)
 
@@ -353,7 +353,9 @@
 
     base, z1, z2, z3 = mix(kept, swap_core(given))
     z1, z3, z2 = shift_z(z1, 1), shift_z(z3, -1), shift_z(z2, 2)
-    total, sent_1, sent_2, sent_3 = own(rel, g, up_low, up_high, down_low, down_high)
+    arrived = (up_low, up_high, down_low, down_high)
+    (sent_2,) = own((2,), rel, g, *arrived)
+    sent_1, sent_3, total = own((1, 3, 0), rel, g, *arrived)
     weight_grad = add_all(total, small(sent_2, 2), small(sent_1, 1), small(sent_3, -1))
     input_grad = join(base, z1, z2, z3)
     return (activated, input_grad, weight_grad)

time: 141 us -> 140 us (level)
  transfers between devices with their start and end apart: 26 -> 26, of which waited for: 19 -> 16; matrix products, arithmetic and copies ran while one was open for 4% -> 4% of each run, Pallas kernels for 20% -> 20%
where the time goes in v7:
time: 140 us
  waiting for transfers between devices  57.7 us (41%)
  starting transfers between devices  40 us (29%)
  Pallas kernels  32.7 us (23%)
  local copies, waits for them, and re-layouts  3.88 us (3%)
  matrix products  3.08 us (2%)
  other arithmetic  1.69 us (1%)
    ppermute x18, waiting for transfers between devices, shift(): return lax.ppermute(block, ('row', 'col'), pairs)  43.4 us
    ppermute x18, starting transfers between devices, shift(): return lax.ppermute(block, ('row', 'col'), pairs)  25.3 us
    pallas_call x1, Pallas kernels, input_partial(): pl.pallas_call(functools.partial(input_kernel, tuple(pieces)), out_shape=...  10.9 us
    ppermute x3, starting transfers between devices, shift_z(): return lax.ppermute(block, 'col', pairs)  9.49 us
    pallas_call x2, Pallas kernels, add_sums(): pl.pallas_call(functools.partial(sum_kernel, tuple(pieces), len(firsts)),...  8.21 us
    ppermute x2, waiting for transfers between devices, spread_z(): return lax.ppermute(block, 'col', pairs)  7.83 us
    ppermute x3, waiting for transfers between devices, shift_z(): return lax.ppermute(block, 'col', pairs)  5.14 us
    pallas_call x1, Pallas kernels, finish(): pl.pallas_call(functools.partial(late_kernel, tuple(pieces)), out_shape=(...  3.99 us
  transfers between devices with their start and end apart: 26, of which 16 were waited for; matrix products, arithmetic and copies ran while one was open for 4% of the time, Pallas kernels for 20%

profile of v7, /device:TPU:6, one launch (start us, length us, event | category | flops | bytes accessed | tf_op | source)
XLA Modules:
  0.0 139.8 jit_solution(17818343688826731855)
XLA Ops:
  0.6 1.5 %collective-permute-start.4 = (bf16[192,1536]{1,0:T(8,128)(2,1)}, bf16[192,1536]{1,0:T(8,128)(2,1)S(1)}, u32[]{:S(2)}, u32[]{:S(2)}) collective-permute-start(bf16[192,1536]{1,0:T(8,128)(2,1)} %param.4), channel_id=1, source_target_pairs={{0,16},{1,65},{2,18},{3,67},{4,20},{5,69},{6,22},{7,71},{8,24},{9,... | collective-permute-start | bytes 1769480 | tf_op jit(solution)/shard_map/ppermute | solution.py:25
  2.1 2.1 %collective-permute-start.6 = (bf16[192,1536]{1,0:T(8,128)(2,1)}, bf16[192,1536]{1,0:T(8,128)(2,1)S(1)}, u32[]{:S(2)}, u32[]{:S(2)}) collective-permute-start(bf16[192,1536]{1,0:T(8,128)(2,1)} %param.4), channel_id=1, source_target_pairs={{0,8},{1,33},{2,10},{3,35},{4,12},{5,37},{6,14},{7,39},{8,16},{9,4... | collective-permute-start | bytes 1769480 | tf_op jit(solution)/shard_map/ppermute | solution.py:25
  5.4 2.0 %collective-permute-start = (bf16[384,512]{1,0:T(8,128)(2,1)S(1)}, bf16[384,512]{1,0:T(8,128)(2,1)S(1)}, u32[]{:S(2)}, u32[]{:S(2)}) collective-permute-start(bf16[384,512]{1,0:T(8,128)(2,1)S(1)} %shard_map.58), channel_id=1, source_target_pairs={{0,1},{1,0},{2,3},{3,2},{4,5},{5,4},{6,7},{7,6},{8,9},{9,8},{10,11... | collective-permute-start | bytes 1179656 | tf_op jit(solution)/shard_map/ppermute | solution.py:48
  7.4 1.3 collective-permute-done
  8.8 2.0 %collective-permute-start.1 = (bf16[2,384,512]{2,1,0:T(8,128)(2,1)S(1)}, bf16[2,384,512]{2,1,0:T(8,128)(2,1)S(1)}, u32[]{:S(2)}, u32[]{:S(2)}) collective-permute-start(bf16[2,384,512]{2,1,0:T(8,128)(2,1)S(1)} %pad_maximum_fusion.2.here), channel_id=1, source_target_pairs={{0,2},{1,7},{2,4},{3,1},{4,6},{5,3},{6,0},{7,5},{8,10},{9,15},{10,... | collective-permute-start | bytes 2359304 | tf_op jit(solution)/shard_map/ppermute | solution.py:43
  10.8 1.6 %collective-permute-done.4 = bf16[192,1536]{1,0:T(8,128)(2,1)S(1)} collective-permute-done((bf16[192,1536]{1,0:T(8,128)(2,1)}, bf16[192,1536]{1,0:T(8,128)(2,1)S(1)}, u32[]{:S(2)}, u32[]{:S(2)}) %collective-permute-start.4) | collective-permute-done | bytes 589856 | tf_op jit(solution)/shard_map/ppermute | solution.py:25
  12.4 4.0 %collective-permute-done.6 = bf16[192,1536]{1,0:T(8,128)(2,1)S(1)} collective-permute-done((bf16[192,1536]{1,0:T(8,128)(2,1)}, bf16[192,1536]{1,0:T(8,128)(2,1)S(1)}, u32[]{:S(2)}, u32[]{:S(2)}) %collective-permute-start.6) | collective-permute-done | bytes 589856 | tf_op jit(solution)/shard_map/ppermute | solution.py:25
  16.4 2.2 %collective-permute-done.5 = bf16[192,1536]{1,0:T(8,128)(2,1)S(1)} collective-permute-done((bf16[192,1536]{1,0:T(8,128)(2,1)}, bf16[192,1536]{1,0:T(8,128)(2,1)S(1)}, u32[]{:S(2)}, u32[]{:S(2)}) %collective-permute-start.5) | collective-permute-done | bytes 589856 | tf_op jit(solution)/shard_map/ppermute | solution.py:25
  18.8 3.1 %collective-permute-start.7 = (bf16[2,192,1536]{2,1,0:T(8,128)(2,1)S(1)}, bf16[2,192,1536]{2,1,0:T(8,128)(2,1)}, u32[]{:S(2)}, u32[]{:S(2)}) collective-permute-start(bf16[2,192,1536]{2,1,0:T(8,128)(2,1)S(1)} %pad_maximum_fusion.refs_0_), channel_id=1, source_target_pairs={{0,96},{1,25},{2,98},{3,27},{4,100},{5,29},{6,102},{7,31},{8,104},... | collective-permute-start | bytes 3538952 | tf_op jit(solution)/shard_map/ppermute | solution.py:25
  25.0 7.0 %collective-permute-done.2 = bf16[1,384,512]{2,1,0:T(8,128)(2,1)S(1)} collective-permute-done((bf16[1,384,512]{2,1,0:T(8,128)(2,1)S(1)}, bf16[1,384,512]{2,1,0:T(8,128)(2,1)S(1)}, u32[]{:S(2)}, u32[]{:S(2)}) %collective-permute-start.2) | collective-permute-done | bytes 393248 | tf_op jit(solution)/shard_map/ppermute | solution.py:43
  33.3 2.7 %collective-permute-start.9 = (bf16[2,192,1536]{2,1,0:T(8,128)(2,1)S(1)}, bf16[2,192,1536]{2,1,0:T(8,128)(2,1)}, u32[]{:S(2)}, u32[]{:S(2)}) collective-permute-start(bf16[2,192,1536]{2,1,0:T(8,128)(2,1)S(1)} %pad_maximum_fusion.1.refs_1_), channel_id=1, source_target_pairs={{0,96},{1,25},{2,98},{3,27},{4,100},{5,29},{6,102},{7,31},{8,104},... | collective-permute-start | bytes 3538952 | tf_op jit(solution)/shard_map/ppermute | solution.py:25
  36.0 3.4 %collective-permute-start.11 = (bf16[2,192,1536]{2,1,0:T(8,128)(2,1)}, bf16[2,192,1536]{2,1,0:T(8,128)(2,1)}, u32[]{:S(2)}, u32[]{:S(2)}) collective-permute-start(bf16[2,192,1536]{2,1,0:T(8,128)(2,1)} %collective-permute-done.7.refs_2_), channel_id=1, source_target_pairs={{0,96},{1,25},{2,98},{3,27},{4,100},{5,29},{6,102},{7,31},{8,104},... | collective-permute-start | bytes 3538952 | tf_op jit(solution)/shard_map/ppermute | solution.py:25
  40.8 3.6 %shard_map.59.rel.refs_0_ = bf16[4,4,192,512]{3,2,1,0:T(8,128)(2,1)S(1)} custom-call(s32[4]{0:T(128)S(1)} %pad_add_fusion.place, bf16[2,384,512]{2,1,0:T(8,128)(2,1)S(1)} %copy-done.1, bf16[3,384,512]{2,1,0:T(8,128)(2,1)} %constant_dynamic-update-slice_fusion.got, bf16[3,384,512]{2,1,0:T(8,128)(2,1)} %collective-permute-done.3.other), custom_call_target="tpu_custom_call" | custom-call | tf_op jit(solution)/shard_map/pallas_call | solution.py:125
  44.4 5.1 %shard_map.60.refs_0_ = f32[512,1536]{1,0:T(8,128)S(1)} custom-call(bf16[4,4,192,512]{3,2,1,0:T(8,128)(2,1)S(1)} %shard_map.59.rel.refs_0_, bf16[2,192,1536]{2,1,0:T(8,128)(2,1)S(1)} %pad_maximum_fusion.refs_0_, bf16[2,192,1536]{2,1,0:T(8,128)(2,1)S(1)} %pad_maximum_fusion.1.refs_1_, bf16[2,192,1536]{2,1,0:T(8,128)(2,1)} %collective-permute-done.7.refs_2_, ...), custom_call_target="tpu_custom_call" | custom-call | tf_op jit(solution)/shard_map/pallas_call | solution.py:161
  49.5 2.6 %collective-permute-done.10.refs_2_.refs_5_ = bf16[2,192,1536]{2,1,0:T(8,128)(2,1)S(1)} collective-permute-done((bf16[2,192,1536]{2,1,0:T(8,128)(2,1)S(1)}, bf16[2,192,1536]{2,1,0:T(8,128)(2,1)S(1)}, u32[]{:S(2)}, u32[]{:S(2)}) %collective-permute-start.10) | collective-permute-done | bytes 1179680 | tf_op jit(solution)/shard_map/ppermute | solution.py:25
  52.1 3.1 %shard_map.61.sums = f32[512,1536]{1,0:T(8,128)S(1)} custom-call(bf16[4,4,192,512]{3,2,1,0:T(8,128)(2,1)S(1)} %shard_map.59.rel.refs_0_, f32[512,1536]{1,0:T(8,128)S(1)} %shard_map.60.refs_0_, bf16[2,192,1536]{2,1,0:T(8,128)(2,1)} %collective-permute-done.9.refs_1_.refs_4_, bf16[2,192,1536]{2,1,0:T(8,128)(2,1)S(1)} %collective-permute-done.10.refs_2_.refs_5_), custom_call_target="tpu_custom_call" | custom-call | tf_op jit(solution)/shard_map/pallas_call | solution.py:161
  55.2 7.2 %collective-permute-done.11.refs_0_.refs_6_ = bf16[2,192,1536]{2,1,0:T(8,128)(2,1)} collective-permute-done((bf16[2,192,1536]{2,1,0:T(8,128)(2,1)}, bf16[2,192,1536]{2,1,0:T(8,128)(2,1)}, u32[]{:S(2)}, u32[]{:S(2)}) %collective-permute-start.11) | collective-permute-done | bytes 1179680 | tf_op jit(solution)/shard_map/ppermute | solution.py:25
  62.5 2.4 %collective-permute-done.12.refs_1_.refs_7_ = bf16[2,192,1536]{2,1,0:T(8,128)(2,1)} collective-permute-done((bf16[2,192,1536]{2,1,0:T(8,128)(2,1)}, bf16[2,192,1536]{2,1,0:T(8,128)(2,1)}, u32[]{:S(2)}, u32[]{:S(2)}) %collective-permute-start.12) | collective-permute-done | bytes 1179680 | tf_op jit(solution)/shard_map/ppermute | solution.py:25
  64.8 4.0 %shard_map.62 = (f32[512,1536]{1,0:T(8,128)S(1)}, bf16[512,1536]{1,0:T(8,128)(2,1)S(1)}) custom-call(bf16[4,4,192,512]{3,2,1,0:T(8,128)(2,1)S(1)} %shard_map.59.rel.refs_0_, f32[512,1536]{1,0:T(8,128)S(1)} %shard_map.61.sums, bf16[512,1536]{1,0:T(8,128)(2,1)S(1)} %copy-done.2, bf16[2,192,1536]{2,1,0:T(8,128)(2,1)} %collective-permute-done.11.refs_0_.refs_6_, ...), custom_call_target="tpu_custom_call" | custom-call | tf_op jit(solution)/shard_map/pallas_call | solution.py:189
  70.5 3.2 %collective-permute-start.14 = (bf16[2,192,1536]{2,1,0:T(8,128)(2,1)S(1)}, bf16[2,192,1536]{2,1,0:T(8,128)(2,1)S(1)}, u32[]{:S(2)}, u32[]{:S(2)}) collective-permute-start(bf16[2,192,1536]{2,1,0:T(8,128)(2,1)S(1)} %convolution_convert_fusion.2), channel_id=1, source_target_pairs={{0,96},{1,25},{2,98},{3,27},{4,100},{5,29},{6,102},{7,31},{8,104},... | collective-permute-start | bytes 3538952 | tf_op jit(solution)/shard_map/ppermute | solution.py:25
  75.4 2.0 %collective-permute-start.20 = (bf16[2,192,1536]{2,1,0:T(8,128)(2,1)S(1)}, bf16[2,192,1536]{2,1,0:T(8,128)(2,1)S(1)}, u32[]{:S(2)}, u32[]{:S(2)}) collective-permute-start(bf16[2,192,1536]{2,1,0:T(8,128)(2,1)S(1)} %convolution_convert_fusion.1), channel_id=1, source_target_pairs={{0,32},{1,9},{2,34},{3,11},{4,36},{5,13},{6,38},{7,15},{8,40},{9,1... | collective-permute-start | bytes 3538952 | tf_op jit(solution)/shard_map/ppermute | solution.py:25
  77.4 10.9 %shard_map.63 = (f32[1536,512]{1,0:T(8,128)S(1)}, bf16[1536,512]{1,0:T(8,128)(2,1)S(1)}) custom-call(s32[4]{0:T(128)S(1)} %pad_add_fusion.place, bf16[512,1536]{1,0:T(8,128)(2,1)S(1)} %get-tuple-element.25.g.refs_1_, bf16[2,192,1536]{2,1,0:T(8,128)(2,1)S(1)} %pad_maximum_fusion.refs_0_, bf16[2,192,1536]{2,1,0:T(8,128)(2,1)S(1)} %pad_maximum_fusion.1.refs_1_, ...), custom_call_target="tpu_custom_call" | custom-call | tf_op jit(solution)/shard_map/pallas_call | solution.py:310
  89.9 2.9 %collective-permute-start.22 = (bf16[2,192,1536]{2,1,0:T(8,128)(2,1)S(1)}, bf16[2,192,1536]{2,1,0:T(8,128)(2,1)S(1)}, u32[]{:S(2)}, u32[]{:S(2)}) collective-permute-start(bf16[2,192,1536]{2,1,0:T(8,128)(2,1)S(1)} %shard_map.67), channel_id=1, source_target_pairs={{0,96},{1,25},{2,98},{3,27},{4,100},{5,29},{6,102},{7,31},{8,104},... | collective-permute-start | bytes 3538952 | tf_op jit(solution)/shard_map/ppermute | solution.py:25
  92.7 7.3 %collective-permute-done.21.refs_4_ = bf16[2,192,1536]{2,1,0:T(8,128)(2,1)S(1)} collective-permute-done((bf16[2,192,1536]{2,1,0:T(8,128)(2,1)S(1)}, bf16[2,192,1536]{2,1,0:T(8,128)(2,1)S(1)}, u32[]{:S(2)}, u32[]{:S(2)}) %collective-permute-start.21) | collective-permute-done | bytes 1179680 | tf_op jit(solution)/shard_map/ppermute | solution.py:25
  100.5 12.2 %collective-permute-done.22.refs_5_ = bf16[2,192,1536]{2,1,0:T(8,128)(2,1)S(1)} collective-permute-done((bf16[2,192,1536]{2,1,0:T(8,128)(2,1)S(1)}, bf16[2,192,1536]{2,1,0:T(8,128)(2,1)S(1)}, u32[]{:S(2)}, u32[]{:S(2)}) %collective-permute-start.22) | collective-permute-done | bytes 1179680 | tf_op jit(solution)/shard_map/ppermute | solution.py:25
  115.0 1.4 %collective-permute-start.25 = (bf16[192,1536]{1,0:T(8,128)(2,1)S(1)}, bf16[192,1536]{1,0:T(8,128)(2,1)S(1)}, u32[]{:S(2)}, u32[]{:S(2)}) collective-permute-start(bf16[192,1536]{1,0:T(8,128)(2,1)S(1)} %get-tuple-element.40), channel_id=1, source_target_pairs={{0,24},{1,97},{2,26},{3,99},{4,28},{5,101},{6,30},{7,103},{8,0},{9... | collective-permute-start | bytes 1769480 | tf_op jit(solution)/shard_map/ppermute | solution.py:25
  116.9 1.6 %collective-permute-start.23 = (bf16[192,1536]{1,0:T(8,128)(2,1)S(1)}, bf16[192,1536]{1,0:T(8,128)(2,1)S(1)}, u32[]{:S(2)}, u32[]{:S(2)}) collective-permute-start(bf16[192,1536]{1,0:T(8,128)(2,1)S(1)} %shard_map.69), channel_id=1, source_target_pairs={{0,16},{1,65},{2,18},{3,67},{4,20},{5,69},{6,22},{7,71},{8,24},{9,... | collective-permute-start | bytes 1769480 | tf_op jit(solution)/shard_map/ppermute | solution.py:25
  118.8 2.0 %collective-permute-start.16 = (bf16[384,512]{1,0:T(8,128)(2,1)S(1)}, bf16[384,512]{1,0:T(8,128)(2,1)S(1)}, u32[]{:S(2)}, u32[]{:S(2)}) collective-permute-start(bf16[384,512]{1,0:T(8,128)(2,1)S(1)} %get-tuple-element.33), channel_id=1, source_target_pairs={{0,2},{1,3},{2,4},{3,5},{4,6},{5,7},{6,0},{7,1},{8,10},{9,11},{10,... | collective-permute-start | bytes 1179656 | tf_op jit(solution)/shard_map/ppermute | solution.py:38
  120.8 3.6 %collective-permute-start.17 = (bf16[384,512]{1,0:T(8,128)(2,1)S(1)}, bf16[384,512]{1,0:T(8,128)(2,1)S(1)}, u32[]{:S(2)}, u32[]{:S(2)}) collective-permute-start(bf16[384,512]{1,0:T(8,128)(2,1)S(1)} %get-tuple-element.34), channel_id=1, source_target_pairs={{0,4},{1,5},{2,6},{3,7},{4,0},{5,1},{6,2},{7,3},{8,12},{9,13},{10,... | collective-permute-start | bytes 1179656 | tf_op jit(solution)/shard_map/ppermute | solution.py:38
  124.4 3.9 %collective-permute-start.18 = (bf16[384,512]{1,0:T(8,128)(2,1)S(1)}, bf16[384,512]{1,0:T(8,128)(2,1)S(1)}, u32[]{:S(2)}, u32[]{:S(2)}) collective-permute-start(bf16[384,512]{1,0:T(8,128)(2,1)S(1)} %get-tuple-element.35), channel_id=1, source_target_pairs={{0,6},{1,7},{2,0},{3,1},{4,2},{5,3},{6,4},{7,5},{8,14},{9,15},{10,... | collective-permute-start | bytes 1179656 | tf_op jit(solution)/shard_map/ppermute | solution.py:38
  129.6 2.8 %collective-permute-done.25.c = bf16[192,1536]{1,0:T(8,128)(2,1)S(1)} collective-permute-done((bf16[192,1536]{1,0:T(8,128)(2,1)S(1)}, bf16[192,1536]{1,0:T(8,128)(2,1)S(1)}, u32[]{:S(2)}, u32[]{:S(2)}) %collective-permute-start.25) | collective-permute-done | bytes 589856 | tf_op jit(solution)/shard_map/ppermute | solution.py:25
  133.7 5.1 %collective-permute-done.17.b = bf16[384,512]{1,0:T(8,128)(2,1)S(1)} collective-permute-done((bf16[384,512]{1,0:T(8,128)(2,1)S(1)}, bf16[384,512]{1,0:T(8,128)(2,1)S(1)}, u32[]{:S(2)}, u32[]{:S(2)}) %collective-permute-start.17) | collective-permute-done | bytes 393248 | tf_op jit(solution)/shard_map/ppermute | solution.py:38
  (55 shorter events, 19.3 us)
Async XLA Ops:
  0.6 11.8 %collective-permute-start.4 = (bf16[192,1536]{1,0:T(8,128)(2,1)}, bf16[192,1536]{1,0:T(8,128)(2,1)S(1)}, u32[]{:S(2)}, u32[]{:S(2)}) collective-permute-start(bf16[192,1536]{1,0:T(8,128)(2,1)} %param.4), channel_id=1, source_target_pairs={{0,16},{1,65},{2,18},{3,67},{4,20},{5,69},{6,22},{7,71},{8,24},{9,... | collective-permute-start | bytes 1769480 | tf_op jit(solution)/shard_map/ppermute | solution.py:25
  2.1 14.3 %collective-permute-start.6 = (bf16[192,1536]{1,0:T(8,128)(2,1)}, bf16[192,1536]{1,0:T(8,128)(2,1)S(1)}, u32[]{:S(2)}, u32[]{:S(2)}) collective-permute-start(bf16[192,1536]{1,0:T(8,128)(2,1)} %param.4), channel_id=1, source_target_pairs={{0,8},{1,33},{2,10},{3,35},{4,12},{5,37},{6,14},{7,39},{8,16},{9,4... | collective-permute-start | bytes 1769480 | tf_op jit(solution)/shard_map/ppermute | solution.py:25
  4.2 14.4 %collective-permute-start.5 = (bf16[192,1536]{1,0:T(8,128)(2,1)}, bf16[192,1536]{1,0:T(8,128)(2,1)S(1)}, u32[]{:S(2)}, u32[]{:S(2)}) collective-permute-start(bf16[192,1536]{1,0:T(8,128)(2,1)} %param.4), channel_id=1, source_target_pairs={{0,24},{1,97},{2,26},{3,99},{4,28},{5,101},{6,30},{7,103},{8,0},{9... | collective-permute-start | bytes 1769480 | tf_op jit(solution)/shard_map/ppermute | solution.py:25
  4.2 1.0 copy-start.3
  5.2 13.4 %copy-start.4 = (bf16[192,1536]{1,0:T(8,128)(2,1)S(1)}, bf16[192,1536]{1,0:T(8,128)(2,1)}, u32[]{:S(2)}) copy-start(bf16[192,1536]{1,0:T(8,128)(2,1)} %param.4) | copy-start | bytes 1769476
  5.4 3.4 %collective-permute-start = (bf16[384,512]{1,0:T(8,128)(2,1)S(1)}, bf16[384,512]{1,0:T(8,128)(2,1)S(1)}, u32[]{:S(2)}, u32[]{:S(2)}) collective-permute-start(bf16[384,512]{1,0:T(8,128)(2,1)S(1)} %shard_map.58), channel_id=1, source_target_pairs={{0,1},{1,0},{2,3},{3,2},{4,5},{5,4},{6,7},{7,6},{8,9},{9,8},{10,11... | collective-permute-start | bytes 1179656 | tf_op jit(solution)/shard_map/ppermute | solution.py:48
  8.8 9.9 %copy-start = (bf16[2,384,512]{2,1,0:T(8,128)(2,1)}, bf16[2,384,512]{2,1,0:T(8,128)(2,1)S(1)}, u32[]{:S(2)}) copy-start(bf16[2,384,512]{2,1,0:T(8,128)(2,1)S(1)} %pad_maximum_fusion.2.here) | copy-start | bytes 2359300
  8.8 14.1 %collective-permute-start.1 = (bf16[2,384,512]{2,1,0:T(8,128)(2,1)S(1)}, bf16[2,384,512]{2,1,0:T(8,128)(2,1)S(1)}, u32[]{:S(2)}, u32[]{:S(2)}) collective-permute-start(bf16[2,384,512]{2,1,0:T(8,128)(2,1)S(1)} %pad_maximum_fusion.2.here), channel_id=1, source_target_pairs={{0,2},{1,7},{2,4},{3,1},{4,6},{5,3},{6,0},{7,5},{8,10},{9,15},{10,... | collective-permute-start | bytes 2359304 | tf_op jit(solution)/shard_map/ppermute | solution.py:43
  18.8 17.2 %collective-permute-start.7 = (bf16[2,192,1536]{2,1,0:T(8,128)(2,1)S(1)}, bf16[2,192,1536]{2,1,0:T(8,128)(2,1)}, u32[]{:S(2)}, u32[]{:S(2)}) collective-permute-start(bf16[2,192,1536]{2,1,0:T(8,128)(2,1)S(1)} %pad_maximum_fusion.refs_0_), channel_id=1, source_target_pairs={{0,96},{1,25},{2,98},{3,27},{4,100},{5,29},{6,102},{7,31},{8,104},... | collective-permute-start | bytes 3538952 | tf_op jit(solution)/shard_map/ppermute | solution.py:25
  21.9 17.6 %collective-permute-start.8 = (bf16[2,192,1536]{2,1,0:T(8,128)(2,1)S(1)}, bf16[2,192,1536]{2,1,0:T(8,128)(2,1)}, u32[]{:S(2)}, u32[]{:S(2)}) collective-permute-start(bf16[2,192,1536]{2,1,0:T(8,128)(2,1)S(1)} %pad_maximum_fusion.1.refs_1_), channel_id=1, source_target_pairs={{0,32},{1,9},{2,34},{3,11},{4,36},{5,13},{6,38},{7,15},{8,40},{9,1... | collective-permute-start | bytes 3538952 | tf_op jit(solution)/shard_map/ppermute | solution.py:25
  22.9 9.1 %collective-permute-start.2 = (bf16[1,384,512]{2,1,0:T(8,128)(2,1)S(1)}, bf16[1,384,512]{2,1,0:T(8,128)(2,1)S(1)}, u32[]{:S(2)}, u32[]{:S(2)}) collective-permute-start(bf16[1,384,512]{2,1,0:T(8,128)(2,1)S(1)} %slice.20), channel_id=1, source_target_pairs={{0,2},{1,7},{2,4},{3,1},{4,6},{5,3},{6,0},{7,5},{8,10},{9,15},{10,... | collective-permute-start | bytes 1179656 | tf_op jit(solution)/shard_map/ppermute | solution.py:43
  32.7 6.9 %collective-permute-start.3 = (bf16[3,384,512]{2,1,0:T(8,128)(2,1)}, bf16[3,384,512]{2,1,0:T(8,128)(2,1)}, u32[]{:S(2)}, u32[]{:S(2)}) collective-permute-start(bf16[3,384,512]{2,1,0:T(8,128)(2,1)} %constant_dynamic-update-slice_fusion.got), channel_id=1, source_target_pairs={{0,1},{1,0},{2,3},{3,2},{4,5},{5,4},{6,7},{7,6},{8,9},{9,8},{10,11... | collective-permute-start | bytes 3538952 | tf_op jit(solution)/shard_map/ppermute | solution.py:48
  32.7 19.3 %collective-permute-start.10 = (bf16[2,192,1536]{2,1,0:T(8,128)(2,1)S(1)}, bf16[2,192,1536]{2,1,0:T(8,128)(2,1)S(1)}, u32[]{:S(2)}, u32[]{:S(2)}) collective-permute-start(bf16[2,192,1536]{2,1,0:T(8,128)(2,1)S(1)} %pad_maximum_fusion.refs_0_), channel_id=1, source_target_pairs={{0,32},{1,9},{2,34},{3,11},{4,36},{5,13},{6,38},{7,15},{8,40},{9,1... | collective-permute-start | bytes 3538952 | tf_op jit(solution)/shard_map/ppermute | solution.py:25
  33.3 18.8 %collective-permute-start.9 = (bf16[2,192,1536]{2,1,0:T(8,128)(2,1)S(1)}, bf16[2,192,1536]{2,1,0:T(8,128)(2,1)}, u32[]{:S(2)}, u32[]{:S(2)}) collective-permute-start(bf16[2,192,1536]{2,1,0:T(8,128)(2,1)S(1)} %pad_maximum_fusion.1.refs_1_), channel_id=1, source_target_pairs={{0,96},{1,25},{2,98},{3,27},{4,100},{5,29},{6,102},{7,31},{8,104},... | collective-permute-start | bytes 3538952 | tf_op jit(solution)/shard_map/ppermute | solution.py:25
  36.0 26.5 %collective-permute-start.11 = (bf16[2,192,1536]{2,1,0:T(8,128)(2,1)}, bf16[2,192,1536]{2,1,0:T(8,128)(2,1)}, u32[]{:S(2)}, u32[]{:S(2)}) collective-permute-start(bf16[2,192,1536]{2,1,0:T(8,128)(2,1)} %collective-permute-done.7.refs_2_), channel_id=1, source_target_pairs={{0,96},{1,25},{2,98},{3,27},{4,100},{5,29},{6,102},{7,31},{8,104},... | collective-permute-start | bytes 3538952 | tf_op jit(solution)/shard_map/ppermute | solution.py:25
  39.5 25.3 %collective-permute-start.12 = (bf16[2,192,1536]{2,1,0:T(8,128)(2,1)}, bf16[2,192,1536]{2,1,0:T(8,128)(2,1)}, u32[]{:S(2)}, u32[]{:S(2)}) collective-permute-start(bf16[2,192,1536]{2,1,0:T(8,128)(2,1)} %collective-permute-done.8.refs_3_), channel_id=1, source_target_pairs={{0,32},{1,9},{2,34},{3,11},{4,36},{5,13},{6,38},{7,15},{8,40},{9,1... | collective-permute-start | bytes 3538952 | tf_op jit(solution)/shard_map/ppermute | solution.py:25
  39.6 1.1 copy-start.1
  49.5 15.4 %copy-start.2 = (bf16[512,1536]{1,0:T(8,128)(2,1)S(1)}, bf16[512,1536]{1,0:T(8,128)(2,1)}, u32[]{:S(2)}) copy-start(bf16[512,1536]{1,0:T(8,128)(2,1)} %cot.1) | copy-start | bytes 4718596
  70.4 17.9 %collective-permute-start.13 = (bf16[2,192,1536]{2,1,0:T(8,128)(2,1)S(1)}, bf16[2,192,1536]{2,1,0:T(8,128)(2,1)S(1)}, u32[]{:S(2)}, u32[]{:S(2)}) collective-permute-start(bf16[2,192,1536]{2,1,0:T(8,128)(2,1)S(1)} %convolution_convert_fusion.3), channel_id=1, source_target_pairs={{0,32},{1,9},{2,34},{3,11},{4,36},{5,13},{6,38},{7,15},{8,40},{9,1... | collective-permute-start | bytes 3538952 | tf_op jit(solution)/shard_map/ppermute | solution.py:25
  70.5 17.8 %collective-permute-start.14 = (bf16[2,192,1536]{2,1,0:T(8,128)(2,1)S(1)}, bf16[2,192,1536]{2,1,0:T(8,128)(2,1)S(1)}, u32[]{:S(2)}, u32[]{:S(2)}) collective-permute-start(bf16[2,192,1536]{2,1,0:T(8,128)(2,1)S(1)} %convolution_convert_fusion.2), channel_id=1, source_target_pairs={{0,96},{1,25},{2,98},{3,27},{4,100},{5,29},{6,102},{7,31},{8,104},... | collective-permute-start | bytes 3538952 | tf_op jit(solution)/shard_map/ppermute | solution.py:25
  74.5 25.6 %collective-permute-start.21 = (bf16[2,192,1536]{2,1,0:T(8,128)(2,1)S(1)}, bf16[2,192,1536]{2,1,0:T(8,128)(2,1)S(1)}, u32[]{:S(2)}, u32[]{:S(2)}) collective-permute-start(bf16[2,192,1536]{2,1,0:T(8,128)(2,1)S(1)} %convolution_convert_fusion), channel_id=1, source_target_pairs={{0,96},{1,25},{2,98},{3,27},{4,100},{5,29},{6,102},{7,31},{8,104},... | collective-permute-start | bytes 3538952 | tf_op jit(solution)/shard_map/ppermute | solution.py:25
  75.4 25.1 %collective-permute-start.20 = (bf16[2,192,1536]{2,1,0:T(8,128)(2,1)S(1)}, bf16[2,192,1536]{2,1,0:T(8,128)(2,1)S(1)}, u32[]{:S(2)}, u32[]{:S(2)}) collective-permute-start(bf16[2,192,1536]{2,1,0:T(8,128)(2,1)S(1)} %convolution_convert_fusion.1), channel_id=1, source_target_pairs={{0,32},{1,9},{2,34},{3,11},{4,36},{5,13},{6,38},{7,15},{8,40},{9,1... | collective-permute-start | bytes 3538952 | tf_op jit(solution)/shard_map/ppermute | solution.py:25
  89.9 22.8 %collective-permute-start.22 = (bf16[2,192,1536]{2,1,0:T(8,128)(2,1)S(1)}, bf16[2,192,1536]{2,1,0:T(8,128)(2,1)S(1)}, u32[]{:S(2)}, u32[]{:S(2)}) collective-permute-start(bf16[2,192,1536]{2,1,0:T(8,128)(2,1)S(1)} %shard_map.67), channel_id=1, source_target_pairs={{0,96},{1,25},{2,98},{3,27},{4,100},{5,29},{6,102},{7,31},{8,104},... | collective-permute-start | bytes 3538952 | tf_op jit(solution)/shard_map/ppermute | solution.py:25
  92.7 20.4 %collective-permute-start.19 = (bf16[2,192,1536]{2,1,0:T(8,128)(2,1)S(1)}, bf16[2,192,1536]{2,1,0:T(8,128)(2,1)S(1)}, u32[]{:S(2)}, u32[]{:S(2)}) collective-permute-start(bf16[2,192,1536]{2,1,0:T(8,128)(2,1)S(1)} %shard_map.66), channel_id=1, source_target_pairs={{0,32},{1,9},{2,34},{3,11},{4,36},{5,13},{6,38},{7,15},{8,40},{9,1... | collective-permute-start | bytes 3538952 | tf_op jit(solution)/shard_map/ppermute | solution.py:25
  92.7 25.7 %collective-permute-start.15 = (bf16[1536,512]{1,0:T(8,128)(2,1)S(1)}, bf16[1536,512]{1,0:T(8,128)(2,1)S(1)}, u32[]{:S(2)}, u32[]{:S(2)}) collective-permute-start(bf16[1536,512]{1,0:T(8,128)(2,1)S(1)} %get-tuple-element.31), channel_id=1, source_target_pairs={{0,1},{1,0},{2,3},{3,2},{4,5},{5,4},{6,7},{7,6},{8,9},{9,8},{10,11... | collective-permute-start | bytes 4718600 | tf_op jit(solution)/shard_map/ppermute | solution.py:48
  114.3 10.1 %collective-permute-start.24 = (bf16[192,1536]{1,0:T(8,128)(2,1)S(1)}, bf16[192,1536]{1,0:T(8,128)(2,1)S(1)}, u32[]{:S(2)}, u32[]{:S(2)}) collective-permute-start(bf16[192,1536]{1,0:T(8,128)(2,1)S(1)} %get-tuple-element.39), channel_id=1, source_target_pairs={{0,8},{1,33},{2,10},{3,35},{4,12},{5,37},{6,14},{7,39},{8,16},{9,4... | collective-permute-start | bytes 1769480 | tf_op jit(solution)/shard_map/ppermute | solution.py:25
  115.0 17.4 %collective-permute-start.25 = (bf16[192,1536]{1,0:T(8,128)(2,1)S(1)}, bf16[192,1536]{1,0:T(8,128)(2,1)S(1)}, u32[]{:S(2)}, u32[]{:S(2)}) collective-permute-start(bf16[192,1536]{1,0:T(8,128)(2,1)S(1)} %get-tuple-element.40), channel_id=1, source_target_pairs={{0,24},{1,97},{2,26},{3,99},{4,28},{5,101},{6,30},{7,103},{8,0},{9... | collective-permute-start | bytes 1769480 | tf_op jit(solution)/shard_map/ppermute | solution.py:25
  116.9 15.5 %collective-permute-start.23 = (bf16[192,1536]{1,0:T(8,128)(2,1)S(1)}, bf16[192,1536]{1,0:T(8,128)(2,1)S(1)}, u32[]{:S(2)}, u32[]{:S(2)}) collective-permute-start(bf16[192,1536]{1,0:T(8,128)(2,1)S(1)} %shard_map.69), channel_id=1, source_target_pairs={{0,16},{1,65},{2,18},{3,67},{4,20},{5,69},{6,22},{7,71},{8,24},{9,... | collective-permute-start | bytes 1769480 | tf_op jit(solution)/shard_map/ppermute | solution.py:25
  118.8 14.9 %collective-permute-start.16 = (bf16[384,512]{1,0:T(8,128)(2,1)S(1)}, bf16[384,512]{1,0:T(8,128)(2,1)S(1)}, u32[]{:S(2)}, u32[]{:S(2)}) collective-permute-start(bf16[384,512]{1,0:T(8,128)(2,1)S(1)} %get-tuple-element.33), channel_id=1, source_target_pairs={{0,2},{1,3},{2,4},{3,5},{4,6},{5,7},{6,0},{7,1},{8,10},{9,11},{10,... | collective-permute-start | bytes 1179656 | tf_op jit(solution)/shard_map/ppermute | solution.py:38
  120.8 18.0 %collective-permute-start.17 = (bf16[384,512]{1,0:T(8,128)(2,1)S(1)}, bf16[384,512]{1,0:T(8,128)(2,1)S(1)}, u32[]{:S(2)}, u32[]{:S(2)}) collective-permute-start(bf16[384,512]{1,0:T(8,128)(2,1)S(1)} %get-tuple-element.34), channel_id=1, source_target_pairs={{0,4},{1,5},{2,6},{3,7},{4,0},{5,1},{6,2},{7,3},{8,12},{9,13},{10,... | collective-permute-start | bytes 1179656 | tf_op jit(solution)/shard_map/ppermute | solution.py:38
  124.4 14.4 %collective-permute-start.18 = (bf16[384,512]{1,0:T(8,128)(2,1)S(1)}, bf16[384,512]{1,0:T(8,128)(2,1)S(1)}, u32[]{:S(2)}, u32[]{:S(2)}) collective-permute-start(bf16[384,512]{1,0:T(8,128)(2,1)S(1)} %get-tuple-element.35), channel_id=1, source_target_pairs={{0,6},{1,7},{2,0},{3,1},{4,2},{5,3},{6,4},{7,5},{8,14},{9,15},{10,... | collective-permute-start | bytes 1179656 | tf_op jit(solution)/shard_map/ppermute | solution.py:38

commit v8 on v7

--- a/solution.py
+++ b/solution.py
@@ -355,7 +355,8 @@
     z1, z3, z2 = shift_z(z1, 1), shift_z(z3, -1), shift_z(z2, 2)
     arrived = (up_low, up_high, down_low, down_high)
     (sent_2,) = own((2,), rel, g, *arrived)
-    sent_1, sent_3, total = own((1, 3, 0), rel, g, *arrived)
+    sent_1, sent_3 = own((1, 3), rel, g, *arrived)
+    (total,) = own((0,), rel, g, *arrived)
     weight_grad = add_all(total, small(sent_2, 2), small(sent_1, 1), small(sent_3, -1))
     input_grad = join(base, z1, z2, z3)
     return (activated, input_grad, weight_grad)

time: 140 us -> 143 us (1.021)
  starting transfers between devices: 40 us -> 46.1 us
  waiting for transfers between devices: 57.7 us -> 53.4 us
    ppermute x3, starting transfers between devices: 9.49 us -> 15.6 us  [shift_z(): return lax.ppermute(block, 'col', pairs)]
    ppermute x18, waiting for transfers between devices: 43.4 us -> 40.6 us  [shift(): return lax.ppermute(block, ('row', 'col'), pairs)]
    ppermute x3, waiting for transfers between devices: 5.14 us -> 3.65 us  [shift_z(): return lax.ppermute(block, 'col', pairs)]
  transfers between devices with their start and end apart: 26 -> 26, of which waited for: 16 -> 15; matrix products, arithmetic and copies ran while one was open for 4% -> 3% of each run, Pallas kernels for 20% -> 20%
where the time goes in v8:
time: 143 us; the launch traced here: 142 us
  waiting for transfers between devices  53.4 us (37%)
  starting transfers between devices  46.1 us (32%)
  Pallas kernels  32.8 us (23%)
  local copies, waits for them, and re-layouts  3.88 us (3%)
  matrix products  3.08 us (2%)
  other arithmetic  1.69 us (1%)
    ppermute x18, waiting for transfers between devices, shift(): return lax.ppermute(block, ('row', 'col'), pairs)  40.6 us
    ppermute x18, starting transfers between devices, shift(): return lax.ppermute(block, ('row', 'col'), pairs)  25.3 us
    ppermute x3, starting transfers between devices, shift_z(): return lax.ppermute(block, 'col', pairs)  15.6 us
    pallas_call x1, Pallas kernels, input_partial(): pl.pallas_call(functools.partial(input_kernel, tuple(pieces)), out_shape=...  10.9 us
    pallas_call x2, Pallas kernels, add_sums(): pl.pallas_call(functools.partial(sum_kernel, tuple(pieces), len(firsts)),...  8.21 us
    ppermute x2, waiting for transfers between devices, spread_z(): return lax.ppermute(block, 'col', pairs)  7.83 us
    pallas_call x1, Pallas kernels, finish(): pl.pallas_call(functools.partial(late_kernel, tuple(pieces)), out_shape=(...  4.04 us
    ppermute x3, waiting for transfers between devices, shift_z(): return lax.ppermute(block, 'col', pairs)  3.65 us
  transfers between devices with their start and end apart: 26, of which 15 were waited for; matrix products, arithmetic and copies ran while one was open for 3% of the time, Pallas kernels for 20%

profile of v8, /device:TPU:6, one launch (start us, length us, event | category | flops | bytes accessed | tf_op | source)
XLA Modules:
  0.0 141.8 jit_solution(7432486138410776178)
XLA Ops:
  0.6 1.5 %collective-permute-start.4 = (bf16[192,1536]{1,0:T(8,128)(2,1)}, bf16[192,1536]{1,0:T(8,128)(2,1)S(1)}, u32[]{:S(2)}, u32[]{:S(2)}) collective-permute-start(bf16[192,1536]{1,0:T(8,128)(2,1)} %param.4), channel_id=1, source_target_pairs={{0,16},{1,65},{2,18},{3,67},{4,20},{5,69},{6,22},{7,71},{8,24},{9,... | collective-permute-start | bytes 1769480 | tf_op jit(solution)/shard_map/ppermute | solution.py:25
  2.1 2.1 %collective-permute-start.6 = (bf16[192,1536]{1,0:T(8,128)(2,1)}, bf16[192,1536]{1,0:T(8,128)(2,1)S(1)}, u32[]{:S(2)}, u32[]{:S(2)}) collective-permute-start(bf16[192,1536]{1,0:T(8,128)(2,1)} %param.4), channel_id=1, source_target_pairs={{0,8},{1,33},{2,10},{3,35},{4,12},{5,37},{6,14},{7,39},{8,16},{9,4... | collective-permute-start | bytes 1769480 | tf_op jit(solution)/shard_map/ppermute | solution.py:25
  5.4 2.0 %collective-permute-start = (bf16[384,512]{1,0:T(8,128)(2,1)S(1)}, bf16[384,512]{1,0:T(8,128)(2,1)S(1)}, u32[]{:S(2)}, u32[]{:S(2)}) collective-permute-start(bf16[384,512]{1,0:T(8,128)(2,1)S(1)} %shard_map.58), channel_id=1, source_target_pairs={{0,1},{1,0},{2,3},{3,2},{4,5},{5,4},{6,7},{7,6},{8,9},{9,8},{10,11... | collective-permute-start | bytes 1179656 | tf_op jit(solution)/shard_map/ppermute | solution.py:48
  7.4 1.3 collective-permute-done
  8.8 2.0 %collective-permute-start.1 = (bf16[2,384,512]{2,1,0:T(8,128)(2,1)S(1)}, bf16[2,384,512]{2,1,0:T(8,128)(2,1)S(1)}, u32[]{:S(2)}, u32[]{:S(2)}) collective-permute-start(bf16[2,384,512]{2,1,0:T(8,128)(2,1)S(1)} %pad_maximum_fusion.2.here), channel_id=1, source_target_pairs={{0,2},{1,7},{2,4},{3,1},{4,6},{5,3},{6,0},{7,5},{8,10},{9,15},{10,... | collective-permute-start | bytes 2359304 | tf_op jit(solution)/shard_map/ppermute | solution.py:43
  10.8 1.6 %collective-permute-done.4 = bf16[192,1536]{1,0:T(8,128)(2,1)S(1)} collective-permute-done((bf16[192,1536]{1,0:T(8,128)(2,1)}, bf16[192,1536]{1,0:T(8,128)(2,1)S(1)}, u32[]{:S(2)}, u32[]{:S(2)}) %collective-permute-start.4) | collective-permute-done | bytes 589856 | tf_op jit(solution)/shard_map/ppermute | solution.py:25
  12.4 4.0 %collective-permute-done.6 = bf16[192,1536]{1,0:T(8,128)(2,1)S(1)} collective-permute-done((bf16[192,1536]{1,0:T(8,128)(2,1)}, bf16[192,1536]{1,0:T(8,128)(2,1)S(1)}, u32[]{:S(2)}, u32[]{:S(2)}) %collective-permute-start.6) | collective-permute-done | bytes 589856 | tf_op jit(solution)/shard_map/ppermute | solution.py:25
  16.4 2.2 %collective-permute-done.5 = bf16[192,1536]{1,0:T(8,128)(2,1)S(1)} collective-permute-done((bf16[192,1536]{1,0:T(8,128)(2,1)}, bf16[192,1536]{1,0:T(8,128)(2,1)S(1)}, u32[]{:S(2)}, u32[]{:S(2)}) %collective-permute-start.5) | collective-permute-done | bytes 589856 | tf_op jit(solution)/shard_map/ppermute | solution.py:25
  18.8 3.1 %collective-permute-start.7 = (bf16[2,192,1536]{2,1,0:T(8,128)(2,1)S(1)}, bf16[2,192,1536]{2,1,0:T(8,128)(2,1)}, u32[]{:S(2)}, u32[]{:S(2)}) collective-permute-start(bf16[2,192,1536]{2,1,0:T(8,128)(2,1)S(1)} %pad_maximum_fusion.refs_0_), channel_id=1, source_target_pairs={{0,96},{1,25},{2,98},{3,27},{4,100},{5,29},{6,102},{7,31},{8,104},... | collective-permute-start | bytes 3538952 | tf_op jit(solution)/shard_map/ppermute | solution.py:25
  25.0 7.0 %collective-permute-done.2 = bf16[1,384,512]{2,1,0:T(8,128)(2,1)S(1)} collective-permute-done((bf16[1,384,512]{2,1,0:T(8,128)(2,1)S(1)}, bf16[1,384,512]{2,1,0:T(8,128)(2,1)S(1)}, u32[]{:S(2)}, u32[]{:S(2)}) %collective-permute-start.2) | collective-permute-done | bytes 393248 | tf_op jit(solution)/shard_map/ppermute | solution.py:43
  33.3 2.7 %collective-permute-start.9 = (bf16[2,192,1536]{2,1,0:T(8,128)(2,1)S(1)}, bf16[2,192,1536]{2,1,0:T(8,128)(2,1)}, u32[]{:S(2)}, u32[]{:S(2)}) collective-permute-start(bf16[2,192,1536]{2,1,0:T(8,128)(2,1)S(1)} %pad_maximum_fusion.1.refs_1_), channel_id=1, source_target_pairs={{0,96},{1,25},{2,98},{3,27},{4,100},{5,29},{6,102},{7,31},{8,104},... | collective-permute-start | bytes 3538952 | tf_op jit(solution)/shard_map/ppermute | solution.py:25
  36.0 3.4 %collective-permute-start.11 = (bf16[2,192,1536]{2,1,0:T(8,128)(2,1)}, bf16[2,192,1536]{2,1,0:T(8,128)(2,1)}, u32[]{:S(2)}, u32[]{:S(2)}) collective-permute-start(bf16[2,192,1536]{2,1,0:T(8,128)(2,1)} %collective-permute-done.7.refs_2_), channel_id=1, source_target_pairs={{0,96},{1,25},{2,98},{3,27},{4,100},{5,29},{6,102},{7,31},{8,104},... | collective-permute-start | bytes 3538952 | tf_op jit(solution)/shard_map/ppermute | solution.py:25
  40.8 3.6 %shard_map.59.rel.refs_0_ = bf16[4,4,192,512]{3,2,1,0:T(8,128)(2,1)S(1)} custom-call(s32[4]{0:T(128)S(1)} %pad_add_fusion.place, bf16[2,384,512]{2,1,0:T(8,128)(2,1)S(1)} %copy-done.1, bf16[3,384,512]{2,1,0:T(8,128)(2,1)} %constant_dynamic-update-slice_fusion.got, bf16[3,384,512]{2,1,0:T(8,128)(2,1)} %collective-permute-done.3.other), custom_call_target="tpu_custom_call" | custom-call | tf_op jit(solution)/shard_map/pallas_call | solution.py:125
  44.4 5.1 %shard_map.60.refs_0_ = f32[512,1536]{1,0:T(8,128)S(1)} custom-call(bf16[4,4,192,512]{3,2,1,0:T(8,128)(2,1)S(1)} %shard_map.59.rel.refs_0_, bf16[2,192,1536]{2,1,0:T(8,128)(2,1)S(1)} %pad_maximum_fusion.refs_0_, bf16[2,192,1536]{2,1,0:T(8,128)(2,1)S(1)} %pad_maximum_fusion.1.refs_1_, bf16[2,192,1536]{2,1,0:T(8,128)(2,1)} %collective-permute-done.7.refs_2_, ...), custom_call_target="tpu_custom_call" | custom-call | tf_op jit(solution)/shard_map/pallas_call | solution.py:161
  49.5 2.6 %collective-permute-done.10.refs_2_.refs_5_ = bf16[2,192,1536]{2,1,0:T(8,128)(2,1)S(1)} collective-permute-done((bf16[2,192,1536]{2,1,0:T(8,128)(2,1)S(1)}, bf16[2,192,1536]{2,1,0:T(8,128)(2,1)S(1)}, u32[]{:S(2)}, u32[]{:S(2)}) %collective-permute-start.10) | collective-permute-done | bytes 1179680 | tf_op jit(solution)/shard_map/ppermute | solution.py:25
  52.1 3.1 %shard_map.61.sums = f32[512,1536]{1,0:T(8,128)S(1)} custom-call(bf16[4,4,192,512]{3,2,1,0:T(8,128)(2,1)S(1)} %shard_map.59.rel.refs_0_, f32[512,1536]{1,0:T(8,128)S(1)} %shard_map.60.refs_0_, bf16[2,192,1536]{2,1,0:T(8,128)(2,1)} %collective-permute-done.9.refs_1_.refs_4_, bf16[2,192,1536]{2,1,0:T(8,128)(2,1)S(1)} %collective-permute-done.10.refs_2_.refs_5_), custom_call_target="tpu_custom_call" | custom-call | tf_op jit(solution)/shard_map/pallas_call | solution.py:161
  55.2 7.2 %collective-permute-done.11.refs_0_.refs_6_ = bf16[2,192,1536]{2,1,0:T(8,128)(2,1)} collective-permute-done((bf16[2,192,1536]{2,1,0:T(8,128)(2,1)}, bf16[2,192,1536]{2,1,0:T(8,128)(2,1)}, u32[]{:S(2)}, u32[]{:S(2)}) %collective-permute-start.11) | collective-permute-done | bytes 1179680 | tf_op jit(solution)/shard_map/ppermute | solution.py:25
  62.5 2.4 %collective-permute-done.12.refs_1_.refs_7_ = bf16[2,192,1536]{2,1,0:T(8,128)(2,1)} collective-permute-done((bf16[2,192,1536]{2,1,0:T(8,128)(2,1)}, bf16[2,192,1536]{2,1,0:T(8,128)(2,1)}, u32[]{:S(2)}, u32[]{:S(2)}) %collective-permute-start.12) | collective-permute-done | bytes 1179680 | tf_op jit(solution)/shard_map/ppermute | solution.py:25
  64.8 4.0 %shard_map.62 = (f32[512,1536]{1,0:T(8,128)S(1)}, bf16[512,1536]{1,0:T(8,128)(2,1)S(1)}) custom-call(bf16[4,4,192,512]{3,2,1,0:T(8,128)(2,1)S(1)} %shard_map.59.rel.refs_0_, f32[512,1536]{1,0:T(8,128)S(1)} %shard_map.61.sums, bf16[512,1536]{1,0:T(8,128)(2,1)S(1)} %copy-done.2, bf16[2,192,1536]{2,1,0:T(8,128)(2,1)} %collective-permute-done.11.refs_0_.refs_6_, ...), custom_call_target="tpu_custom_call" | custom-call | tf_op jit(solution)/shard_map/pallas_call | solution.py:189
  70.5 3.2 %collective-permute-start.14 = (bf16[2,192,1536]{2,1,0:T(8,128)(2,1)S(1)}, bf16[2,192,1536]{2,1,0:T(8,128)(2,1)S(1)}, u32[]{:S(2)}, u32[]{:S(2)}) collective-permute-start(bf16[2,192,1536]{2,1,0:T(8,128)(2,1)S(1)} %convolution_convert_fusion.2), channel_id=1, source_target_pairs={{0,96},{1,25},{2,98},{3,27},{4,100},{5,29},{6,102},{7,31},{8,104},... | collective-permute-start | bytes 3538952 | tf_op jit(solution)/shard_map/ppermute | solution.py:25
  75.5 2.0 %collective-permute-start.20 = (bf16[2,192,1536]{2,1,0:T(8,128)(2,1)S(1)}, bf16[2,192,1536]{2,1,0:T(8,128)(2,1)S(1)}, u32[]{:S(2)}, u32[]{:S(2)}) collective-permute-start(bf16[2,192,1536]{2,1,0:T(8,128)(2,1)S(1)} %convolution_convert_fusion.1), channel_id=1, source_target_pairs={{0,32},{1,9},{2,34},{3,11},{4,36},{5,13},{6,38},{7,15},{8,40},{9,1... | collective-permute-start | bytes 3538952 | tf_op jit(solution)/shard_map/ppermute | solution.py:25
  77.4 10.9 %shard_map.63 = (f32[1536,512]{1,0:T(8,128)S(1)}, bf16[1536,512]{1,0:T(8,128)(2,1)S(1)}) custom-call(s32[4]{0:T(128)S(1)} %pad_add_fusion.place, bf16[512,1536]{1,0:T(8,128)(2,1)S(1)} %get-tuple-element.24.g.refs_1_, bf16[2,192,1536]{2,1,0:T(8,128)(2,1)S(1)} %pad_maximum_fusion.refs_0_, bf16[2,192,1536]{2,1,0:T(8,128)(2,1)S(1)} %pad_maximum_fusion.1.refs_1_, ...), custom_call_target="tpu_custom_call" | custom-call | tf_op jit(solution)/shard_map/pallas_call | solution.py:310
  90.0 2.8 %collective-permute-start.22 = (bf16[2,192,1536]{2,1,0:T(8,128)(2,1)S(1)}, bf16[2,192,1536]{2,1,0:T(8,128)(2,1)S(1)}, u32[]{:S(2)}, u32[]{:S(2)}) collective-permute-start(bf16[2,192,1536]{2,1,0:T(8,128)(2,1)S(1)} %shard_map.67), channel_id=1, source_target_pairs={{0,96},{1,25},{2,98},{3,27},{4,100},{5,29},{6,102},{7,31},{8,104},... | collective-permute-start | bytes 3538952 | tf_op jit(solution)/shard_map/ppermute | solution.py:25
  92.8 7.3 %collective-permute-done.21.refs_4_ = bf16[2,192,1536]{2,1,0:T(8,128)(2,1)S(1)} collective-permute-done((bf16[2,192,1536]{2,1,0:T(8,128)(2,1)S(1)}, bf16[2,192,1536]{2,1,0:T(8,128)(2,1)S(1)}, u32[]{:S(2)}, u32[]{:S(2)}) %collective-permute-start.21) | collective-permute-done | bytes 1179680 | tf_op jit(solution)/shard_map/ppermute | solution.py:25
  100.5 12.2 %collective-permute-done.22.refs_5_ = bf16[2,192,1536]{2,1,0:T(8,128)(2,1)S(1)} collective-permute-done((bf16[2,192,1536]{2,1,0:T(8,128)(2,1)S(1)}, bf16[2,192,1536]{2,1,0:T(8,128)(2,1)S(1)}, u32[]{:S(2)}, u32[]{:S(2)}) %collective-permute-start.22) | collective-permute-done | bytes 1179680 | tf_op jit(solution)/shard_map/ppermute | solution.py:25
  113.7 1.6 %collective-permute-start.23 = (bf16[192,1536]{1,0:T(8,128)(2,1)S(1)}, bf16[192,1536]{1,0:T(8,128)(2,1)S(1)}, u32[]{:S(2)}, u32[]{:S(2)}) collective-permute-start(bf16[192,1536]{1,0:T(8,128)(2,1)S(1)} %shard_map.69), channel_id=1, source_target_pairs={{0,16},{1,65},{2,18},{3,67},{4,20},{5,69},{6,22},{7,71},{8,24},{9,... | collective-permute-start | bytes 1769480 | tf_op jit(solution)/shard_map/ppermute | solution.py:25
  116.1 1.3 collective-permute-start.24
  118.5 8.8 %collective-permute-start.16 = (bf16[384,512]{1,0:T(8,128)(2,1)S(1)}, bf16[384,512]{1,0:T(8,128)(2,1)S(1)}, u32[]{:S(2)}, u32[]{:S(2)}) collective-permute-start(bf16[384,512]{1,0:T(8,128)(2,1)S(1)} %get-tuple-element.32), channel_id=1, source_target_pairs={{0,2},{1,3},{2,4},{3,5},{4,6},{5,7},{6,0},{7,1},{8,10},{9,11},{10,... | collective-permute-start | bytes 1179656 | tf_op jit(solution)/shard_map/ppermute | solution.py:38
  127.3 3.6 %collective-permute-start.17 = (bf16[384,512]{1,0:T(8,128)(2,1)S(1)}, bf16[384,512]{1,0:T(8,128)(2,1)S(1)}, u32[]{:S(2)}, u32[]{:S(2)}) collective-permute-start(bf16[384,512]{1,0:T(8,128)(2,1)S(1)} %get-tuple-element.33), channel_id=1, source_target_pairs={{0,4},{1,5},{2,6},{3,7},{4,0},{5,1},{6,2},{7,3},{8,12},{9,13},{10,... | collective-permute-start | bytes 1179656 | tf_op jit(solution)/shard_map/ppermute | solution.py:38
  130.9 3.2 %collective-permute-start.18 = (bf16[384,512]{1,0:T(8,128)(2,1)S(1)}, bf16[384,512]{1,0:T(8,128)(2,1)S(1)}, u32[]{:S(2)}, u32[]{:S(2)}) collective-permute-start(bf16[384,512]{1,0:T(8,128)(2,1)S(1)} %get-tuple-element.34), channel_id=1, source_target_pairs={{0,6},{1,7},{2,0},{3,1},{4,2},{5,3},{6,4},{7,5},{8,14},{9,15},{10,... | collective-permute-start | bytes 1179656 | tf_op jit(solution)/shard_map/ppermute | solution.py:38
  134.1 1.3 convert_element_type.17
  137.2 3.6 %collective-permute-done.17.b = bf16[384,512]{1,0:T(8,128)(2,1)S(1)} collective-permute-done((bf16[384,512]{1,0:T(8,128)(2,1)S(1)}, bf16[384,512]{1,0:T(8,128)(2,1)S(1)}, u32[]{:S(2)}, u32[]{:S(2)}) %collective-permute-start.17) | collective-permute-done | bytes 393248 | tf_op jit(solution)/shard_map/ppermute | solution.py:38
  (56 shorter events, 18.2 us)
Async XLA Ops:
  0.6 11.8 %collective-permute-start.4 = (bf16[192,1536]{1,0:T(8,128)(2,1)}, bf16[192,1536]{1,0:T(8,128)(2,1)S(1)}, u32[]{:S(2)}, u32[]{:S(2)}) collective-permute-start(bf16[192,1536]{1,0:T(8,128)(2,1)} %param.4), channel_id=1, source_target_pairs={{0,16},{1,65},{2,18},{3,67},{4,20},{5,69},{6,22},{7,71},{8,24},{9,... | collective-permute-start | bytes 1769480 | tf_op jit(solution)/shard_map/ppermute | solution.py:25
  2.1 14.3 %collective-permute-start.6 = (bf16[192,1536]{1,0:T(8,128)(2,1)}, bf16[192,1536]{1,0:T(8,128)(2,1)S(1)}, u32[]{:S(2)}, u32[]{:S(2)}) collective-permute-start(bf16[192,1536]{1,0:T(8,128)(2,1)} %param.4), channel_id=1, source_target_pairs={{0,8},{1,33},{2,10},{3,35},{4,12},{5,37},{6,14},{7,39},{8,16},{9,4... | collective-permute-start | bytes 1769480 | tf_op jit(solution)/shard_map/ppermute | solution.py:25
  4.2 14.4 %collective-permute-start.5 = (bf16[192,1536]{1,0:T(8,128)(2,1)}, bf16[192,1536]{1,0:T(8,128)(2,1)S(1)}, u32[]{:S(2)}, u32[]{:S(2)}) collective-permute-start(bf16[192,1536]{1,0:T(8,128)(2,1)} %param.4), channel_id=1, source_target_pairs={{0,24},{1,97},{2,26},{3,99},{4,28},{5,101},{6,30},{7,103},{8,0},{9... | collective-permute-start | bytes 1769480 | tf_op jit(solution)/shard_map/ppermute | solution.py:25
  4.2 1.0 copy-start.3
  5.2 13.4 %copy-start.4 = (bf16[192,1536]{1,0:T(8,128)(2,1)S(1)}, bf16[192,1536]{1,0:T(8,128)(2,1)}, u32[]{:S(2)}) copy-start(bf16[192,1536]{1,0:T(8,128)(2,1)} %param.4) | copy-start | bytes 1769476
  5.4 3.4 %collective-permute-start = (bf16[384,512]{1,0:T(8,128)(2,1)S(1)}, bf16[384,512]{1,0:T(8,128)(2,1)S(1)}, u32[]{:S(2)}, u32[]{:S(2)}) collective-permute-start(bf16[384,512]{1,0:T(8,128)(2,1)S(1)} %shard_map.58), channel_id=1, source_target_pairs={{0,1},{1,0},{2,3},{3,2},{4,5},{5,4},{6,7},{7,6},{8,9},{9,8},{10,11... | collective-permute-start | bytes 1179656 | tf_op jit(solution)/shard_map/ppermute | solution.py:48
  8.8 9.9 %copy-start = (bf16[2,384,512]{2,1,0:T(8,128)(2,1)}, bf16[2,384,512]{2,1,0:T(8,128)(2,1)S(1)}, u32[]{:S(2)}) copy-start(bf16[2,384,512]{2,1,0:T(8,128)(2,1)S(1)} %pad_maximum_fusion.2.here) | copy-start | bytes 2359300
  8.8 14.1 %collective-permute-start.1 = (bf16[2,384,512]{2,1,0:T(8,128)(2,1)S(1)}, bf16[2,384,512]{2,1,0:T(8,128)(2,1)S(1)}, u32[]{:S(2)}, u32[]{:S(2)}) collective-permute-start(bf16[2,384,512]{2,1,0:T(8,128)(2,1)S(1)} %pad_maximum_fusion.2.here), channel_id=1, source_target_pairs={{0,2},{1,7},{2,4},{3,1},{4,6},{5,3},{6,0},{7,5},{8,10},{9,15},{10,... | collective-permute-start | bytes 2359304 | tf_op jit(solution)/shard_map/ppermute | solution.py:43
  18.8 17.2 %collective-permute-start.7 = (bf16[2,192,1536]{2,1,0:T(8,128)(2,1)S(1)}, bf16[2,192,1536]{2,1,0:T(8,128)(2,1)}, u32[]{:S(2)}, u32[]{:S(2)}) collective-permute-start(bf16[2,192,1536]{2,1,0:T(8,128)(2,1)S(1)} %pad_maximum_fusion.refs_0_), channel_id=1, source_target_pairs={{0,96},{1,25},{2,98},{3,27},{4,100},{5,29},{6,102},{7,31},{8,104},... | collective-permute-start | bytes 3538952 | tf_op jit(solution)/shard_map/ppermute | solution.py:25
  21.9 17.6 %collective-permute-start.8 = (bf16[2,192,1536]{2,1,0:T(8,128)(2,1)S(1)}, bf16[2,192,1536]{2,1,0:T(8,128)(2,1)}, u32[]{:S(2)}, u32[]{:S(2)}) collective-permute-start(bf16[2,192,1536]{2,1,0:T(8,128)(2,1)S(1)} %pad_maximum_fusion.1.refs_1_), channel_id=1, source_target_pairs={{0,32},{1,9},{2,34},{3,11},{4,36},{5,13},{6,38},{7,15},{8,40},{9,1... | collective-permute-start | bytes 3538952 | tf_op jit(solution)/shard_map/ppermute | solution.py:25
  22.9 9.1 %collective-permute-start.2 = (bf16[1,384,512]{2,1,0:T(8,128)(2,1)S(1)}, bf16[1,384,512]{2,1,0:T(8,128)(2,1)S(1)}, u32[]{:S(2)}, u32[]{:S(2)}) collective-permute-start(bf16[1,384,512]{2,1,0:T(8,128)(2,1)S(1)} %slice.20), channel_id=1, source_target_pairs={{0,2},{1,7},{2,4},{3,1},{4,6},{5,3},{6,0},{7,5},{8,10},{9,15},{10,... | collective-permute-start | bytes 1179656 | tf_op jit(solution)/shard_map/ppermute | solution.py:43
  32.7 6.9 %collective-permute-start.3 = (bf16[3,384,512]{2,1,0:T(8,128)(2,1)}, bf16[3,384,512]{2,1,0:T(8,128)(2,1)}, u32[]{:S(2)}, u32[]{:S(2)}) collective-permute-start(bf16[3,384,512]{2,1,0:T(8,128)(2,1)} %constant_dynamic-update-slice_fusion.got), channel_id=1, source_target_pairs={{0,1},{1,0},{2,3},{3,2},{4,5},{5,4},{6,7},{7,6},{8,9},{9,8},{10,11... | collective-permute-start | bytes 3538952 | tf_op jit(solution)/shard_map/ppermute | solution.py:48
  32.7 19.3 %collective-permute-start.10 = (bf16[2,192,1536]{2,1,0:T(8,128)(2,1)S(1)}, bf16[2,192,1536]{2,1,0:T(8,128)(2,1)S(1)}, u32[]{:S(2)}, u32[]{:S(2)}) collective-permute-start(bf16[2,192,1536]{2,1,0:T(8,128)(2,1)S(1)} %pad_maximum_fusion.refs_0_), channel_id=1, source_target_pairs={{0,32},{1,9},{2,34},{3,11},{4,36},{5,13},{6,38},{7,15},{8,40},{9,1... | collective-permute-start | bytes 3538952 | tf_op jit(solution)/shard_map/ppermute | solution.py:25
  33.3 18.8 %collective-permute-start.9 = (bf16[2,192,1536]{2,1,0:T(8,128)(2,1)S(1)}, bf16[2,192,1536]{2,1,0:T(8,128)(2,1)}, u32[]{:S(2)}, u32[]{:S(2)}) collective-permute-start(bf16[2,192,1536]{2,1,0:T(8,128)(2,1)S(1)} %pad_maximum_fusion.1.refs_1_), channel_id=1, source_target_pairs={{0,96},{1,25},{2,98},{3,27},{4,100},{5,29},{6,102},{7,31},{8,104},... | collective-permute-start | bytes 3538952 | tf_op jit(solution)/shard_map/ppermute | solution.py:25
  36.0 26.5 %collective-permute-start.11 = (bf16[2,192,1536]{2,1,0:T(8,128)(2,1)}, bf16[2,192,1536]{2,1,0:T(8,128)(2,1)}, u32[]{:S(2)}, u32[]{:S(2)}) collective-permute-start(bf16[2,192,1536]{2,1,0:T(8,128)(2,1)} %collective-permute-done.7.refs_2_), channel_id=1, source_target_pairs={{0,96},{1,25},{2,98},{3,27},{4,100},{5,29},{6,102},{7,31},{8,104},... | collective-permute-start | bytes 3538952 | tf_op jit(solution)/shard_map/ppermute | solution.py:25
  39.5 25.3 %collective-permute-start.12 = (bf16[2,192,1536]{2,1,0:T(8,128)(2,1)}, bf16[2,192,1536]{2,1,0:T(8,128)(2,1)}, u32[]{:S(2)}, u32[]{:S(2)}) collective-permute-start(bf16[2,192,1536]{2,1,0:T(8,128)(2,1)} %collective-permute-done.8.refs_3_), channel_id=1, source_target_pairs={{0,32},{1,9},{2,34},{3,11},{4,36},{5,13},{6,38},{7,15},{8,40},{9,1... | collective-permute-start | bytes 3538952 | tf_op jit(solution)/shard_map/ppermute | solution.py:25
  39.6 1.1 copy-start.1
  49.5 15.4 %copy-start.2 = (bf16[512,1536]{1,0:T(8,128)(2,1)S(1)}, bf16[512,1536]{1,0:T(8,128)(2,1)}, u32[]{:S(2)}) copy-start(bf16[512,1536]{1,0:T(8,128)(2,1)} %cot.1) | copy-start | bytes 4718596
  70.4 17.9 %collective-permute-start.13 = (bf16[2,192,1536]{2,1,0:T(8,128)(2,1)S(1)}, bf16[2,192,1536]{2,1,0:T(8,128)(2,1)S(1)}, u32[]{:S(2)}, u32[]{:S(2)}) collective-permute-start(bf16[2,192,1536]{2,1,0:T(8,128)(2,1)S(1)} %convolution_convert_fusion.3), channel_id=1, source_target_pairs={{0,32},{1,9},{2,34},{3,11},{4,36},{5,13},{6,38},{7,15},{8,40},{9,1... | collective-permute-start | bytes 3538952 | tf_op jit(solution)/shard_map/ppermute | solution.py:25
  70.5 17.9 %collective-permute-start.14 = (bf16[2,192,1536]{2,1,0:T(8,128)(2,1)S(1)}, bf16[2,192,1536]{2,1,0:T(8,128)(2,1)S(1)}, u32[]{:S(2)}, u32[]{:S(2)}) collective-permute-start(bf16[2,192,1536]{2,1,0:T(8,128)(2,1)S(1)} %convolution_convert_fusion.2), channel_id=1, source_target_pairs={{0,96},{1,25},{2,98},{3,27},{4,100},{5,29},{6,102},{7,31},{8,104},... | collective-permute-start | bytes 3538952 | tf_op jit(solution)/shard_map/ppermute | solution.py:25
  74.5 25.6 %collective-permute-start.21 = (bf16[2,192,1536]{2,1,0:T(8,128)(2,1)S(1)}, bf16[2,192,1536]{2,1,0:T(8,128)(2,1)S(1)}, u32[]{:S(2)}, u32[]{:S(2)}) collective-permute-start(bf16[2,192,1536]{2,1,0:T(8,128)(2,1)S(1)} %convolution_convert_fusion), channel_id=1, source_target_pairs={{0,96},{1,25},{2,98},{3,27},{4,100},{5,29},{6,102},{7,31},{8,104},... | collective-permute-start | bytes 3538952 | tf_op jit(solution)/shard_map/ppermute | solution.py:25
  75.5 25.1 %collective-permute-start.20 = (bf16[2,192,1536]{2,1,0:T(8,128)(2,1)S(1)}, bf16[2,192,1536]{2,1,0:T(8,128)(2,1)S(1)}, u32[]{:S(2)}, u32[]{:S(2)}) collective-permute-start(bf16[2,192,1536]{2,1,0:T(8,128)(2,1)S(1)} %convolution_convert_fusion.1), channel_id=1, source_target_pairs={{0,32},{1,9},{2,34},{3,11},{4,36},{5,13},{6,38},{7,15},{8,40},{9,1... | collective-permute-start | bytes 3538952 | tf_op jit(solution)/shard_map/ppermute | solution.py:25
  90.0 22.8 %collective-permute-start.22 = (bf16[2,192,1536]{2,1,0:T(8,128)(2,1)S(1)}, bf16[2,192,1536]{2,1,0:T(8,128)(2,1)S(1)}, u32[]{:S(2)}, u32[]{:S(2)}) collective-permute-start(bf16[2,192,1536]{2,1,0:T(8,128)(2,1)S(1)} %shard_map.67), channel_id=1, source_target_pairs={{0,96},{1,25},{2,98},{3,27},{4,100},{5,29},{6,102},{7,31},{8,104},... | collective-permute-start | bytes 3538952 | tf_op jit(solution)/shard_map/ppermute | solution.py:25
  92.8 20.4 %collective-permute-start.19 = (bf16[2,192,1536]{2,1,0:T(8,128)(2,1)S(1)}, bf16[2,192,1536]{2,1,0:T(8,128)(2,1)S(1)}, u32[]{:S(2)}, u32[]{:S(2)}) collective-permute-start(bf16[2,192,1536]{2,1,0:T(8,128)(2,1)S(1)} %shard_map.66), channel_id=1, source_target_pairs={{0,32},{1,9},{2,34},{3,11},{4,36},{5,13},{6,38},{7,15},{8,40},{9,1... | collective-permute-start | bytes 3538952 | tf_op jit(solution)/shard_map/ppermute | solution.py:25
  92.8 25.4 %collective-permute-start.15 = (bf16[1536,512]{1,0:T(8,128)(2,1)S(1)}, bf16[1536,512]{1,0:T(8,128)(2,1)S(1)}, u32[]{:S(2)}, u32[]{:S(2)}) collective-permute-start(bf16[1536,512]{1,0:T(8,128)(2,1)S(1)} %get-tuple-element.30), channel_id=1, source_target_pairs={{0,1},{1,0},{2,3},{3,2},{4,5},{5,4},{6,7},{7,6},{8,9},{9,8},{10,11... | collective-permute-start | bytes 4718600 | tf_op jit(solution)/shard_map/ppermute | solution.py:48
  113.7 17.2 %collective-permute-start.23 = (bf16[192,1536]{1,0:T(8,128)(2,1)S(1)}, bf16[192,1536]{1,0:T(8,128)(2,1)S(1)}, u32[]{:S(2)}, u32[]{:S(2)}) collective-permute-start(bf16[192,1536]{1,0:T(8,128)(2,1)S(1)} %shard_map.69), channel_id=1, source_target_pairs={{0,16},{1,65},{2,18},{3,67},{4,20},{5,69},{6,22},{7,71},{8,24},{9,... | collective-permute-start | bytes 1769480 | tf_op jit(solution)/shard_map/ppermute | solution.py:25
  116.1 19.8 %collective-permute-start.24 = (bf16[192,1536]{1,0:T(8,128)(2,1)S(1)}, bf16[192,1536]{1,0:T(8,128)(2,1)S(1)}, u32[]{:S(2)}, u32[]{:S(2)}) collective-permute-start(bf16[192,1536]{1,0:T(8,128)(2,1)S(1)} %get-tuple-element.37), channel_id=1, source_target_pairs={{0,8},{1,33},{2,10},{3,35},{4,12},{5,37},{6,14},{7,39},{8,16},{9,4... | collective-permute-start | bytes 1769480 | tf_op jit(solution)/shard_map/ppermute | solution.py:25
  117.4 18.6 %collective-permute-start.25 = (bf16[192,1536]{1,0:T(8,128)(2,1)S(1)}, bf16[192,1536]{1,0:T(8,128)(2,1)S(1)}, u32[]{:S(2)}, u32[]{:S(2)}) collective-permute-start(bf16[192,1536]{1,0:T(8,128)(2,1)S(1)} %get-tuple-element.38), channel_id=1, source_target_pairs={{0,24},{1,97},{2,26},{3,99},{4,28},{5,101},{6,30},{7,103},{8,0},{9... | collective-permute-start | bytes 1769480 | tf_op jit(solution)/shard_map/ppermute | solution.py:25
  118.5 18.7 %collective-permute-start.16 = (bf16[384,512]{1,0:T(8,128)(2,1)S(1)}, bf16[384,512]{1,0:T(8,128)(2,1)S(1)}, u32[]{:S(2)}, u32[]{:S(2)}) collective-permute-start(bf16[384,512]{1,0:T(8,128)(2,1)S(1)} %get-tuple-element.32), channel_id=1, source_target_pairs={{0,2},{1,3},{2,4},{3,5},{4,6},{5,7},{6,0},{7,1},{8,10},{9,11},{10,... | collective-permute-start | bytes 1179656 | tf_op jit(solution)/shard_map/ppermute | solution.py:38
  127.3 13.5 %collective-permute-start.17 = (bf16[384,512]{1,0:T(8,128)(2,1)S(1)}, bf16[384,512]{1,0:T(8,128)(2,1)S(1)}, u32[]{:S(2)}, u32[]{:S(2)}) collective-permute-start(bf16[384,512]{1,0:T(8,128)(2,1)S(1)} %get-tuple-element.33), channel_id=1, source_target_pairs={{0,4},{1,5},{2,6},{3,7},{4,0},{5,1},{6,2},{7,3},{8,12},{9,13},{10,... | collective-permute-start | bytes 1179656 | tf_op jit(solution)/shard_map/ppermute | solution.py:38
  130.9 10.0 %collective-permute-start.18 = (bf16[384,512]{1,0:T(8,128)(2,1)S(1)}, bf16[384,512]{1,0:T(8,128)(2,1)S(1)}, u32[]{:S(2)}, u32[]{:S(2)}) collective-permute-start(bf16[384,512]{1,0:T(8,128)(2,1)S(1)} %get-tuple-element.34), channel_id=1, source_target_pairs={{0,6},{1,7},{2,0},{3,1},{4,2},{5,3},{6,4},{7,5},{8,14},{9,15},{10,... | collective-permute-start | bytes 1179656 | tf_op jit(solution)/shard_map/ppermute | solution.py:38
